TPU v7x, 32 devices: a whole 2x2x4 slice. The times are simulated.
32 devices in a mesh: expert: 8 (over z, y), section: 4 (over x, core).
Axes of the slice: x: 2, y: 2, z: 4, core: 2. Of those that a mesh axis runs over, the one named last changes fastest.
Arguments:
- section_acts: bfloat16 [4, 1536, 2048], P('section', 'expert'), may hold values from -6 to 6
- section_input_gradients: bfloat16 [4, 1536, 2048], P('section', 'expert'), may hold values from -6 to 6
- saved_input: bfloat16 [4, 1536, 2048], P('section', 'expert'), may hold values from -6 to 6
- fwd_routes: int32 [4, 768, 8], P('section'), may hold values from 0 to 255, all different within a row; in each aligned block of 192 rows (0 to 191, 192 to 383, ..., all dimensions but the last counted through in order) at most 12 rows name the same one
- fwd_probs: float32 [4, 768, 8], P('section'), may hold values from 0.1 to 1
- back_routes: int32 [4, 768, 8], P('section'), may hold values from 0 to 255, all different within a row; in each aligned block of 192 rows (0 to 191, 192 to 383, ..., all dimensions but the last counted through in order) at most 12 rows name the same one
- back_probs: float32 [4, 768, 8], P('section'), may hold values from 0.1 to 1
- w_gate: bfloat16 [4, 8192, 4096], P('section', 'expert'), may hold values from -0.09375 to 0.09375
- w_up: bfloat16 [4, 8192, 4096], P('section', 'expert'), may hold values from -0.09375 to 0.09375
- w_down: bfloat16 [4, 8192, 4096], P('section', 'expert'), may hold values from -0.125 to 0.125
Outputs:
- section_out: bfloat16 [4, 1536, 2048], P('section', 'expert')
- input_grads: bfloat16 [4, 1536, 2048], P('section', 'expert')
Inputs may be any that keep to these rules, and one draw needn't show every extreme that they name: `fwd_routes`: in each aligned block of 192 rows (one group of one section) no id is named by more than 12 rows, and some block has an id named by exactly 12; every id is named somewhere. `back_routes`: in each aligned block of 192 rows (one group of one section) no id is named by more than 12 rows, and some block has an id named by exactly 12; every id is named somewhere.
All inputs are finite; a program needn't handle non-finite values.
Results may differ from a plain program's by a relative error of at most 0.0075.
Values may be sent and summed in bfloat16 or wider, within the bound.
No kernel may reach another device: no remote copies, remote signals or barrier semaphores. Data moves between devices by JAX's collectives and lax.ppermute only.
A program may use at most 64 MiB of HBM per device.

v0:
```python
import jax
import jax.numpy as jnp
from jax import lax
from jax.sharding import PartitionSpec as P

N_ROUTED = 256
TOP = 8
E_WIN = 4


def from_behind(x, axis, by):
    peers = lax.axis_size(axis)
    return lax.ppermute(x, axis, [(i, (i + by) % peers) for i in range(peers)])


def route_tables(routes, probs, first, count):
    capacity = count * TOP * 2 // N_ROUTED
    block = lax.dynamic_slice_in_dim(routes, first, count, 0)
    gains = lax.dynamic_slice_in_dim(probs, first, count, 0)
    labels = jnp.arange(E_WIN, dtype=jnp.int32)
    hits = block[:, :, None] == labels[None, None, :]
    chosen = jnp.sum(hits.astype(jnp.int32), axis=1, dtype=jnp.int32)
    weight = jnp.sum(jnp.where(hits, gains[:, :, None], jnp.float32(0.0)), axis=1)
    before = jnp.cumsum(chosen, axis=0, dtype=jnp.int32) - chosen
    places = jnp.arange(capacity, dtype=jnp.int32)
    mask = (before[:, None, :] == places[None, :, None]) & (chosen[:, None, :] > 0)
    picker = mask.astype(jnp.float32).reshape(count, capacity * E_WIN)
    weighted = jnp.where(mask, weight[:, None, :], jnp.float32(0.0)).reshape(
        count, capacity * E_WIN
    )
    return (picker, weighted)


def pick_rows(picker, values):
    return jnp.einsum(
        "tm,td->md", picker.astype(jnp.bfloat16), values, preferred_element_type=jnp.float32
    )


def fan_out(rows, split):
    width = rows.shape[1]
    capacity = rows.shape[0] // E_WIN
    spread = jnp.broadcast_to(
        rows.reshape(capacity, E_WIN, 1, width), (capacity, E_WIN, split, width)
    )
    return spread.reshape(capacity, E_WIN * split, width)


def expert_rows(piece):
    count = piece.shape[0]
    return piece.reshape(count * E_WIN, piece.shape[1] * piece.shape[2] // E_WIN)


def slot_layout(rows, count, width):
    return rows.reshape(count, rows.shape[1] // width * E_WIN, width)


def fold_slices(received, split):
    count = received.shape[0]
    width = received.shape[2]
    summed = jnp.sum(received.reshape(count, E_WIN, split, width).astype(jnp.float32), axis=2)
    return summed.reshape(count * E_WIN, width)


def forward_rows(rows, gate_w, up_w, down_w):
    gate_pre = jnp.einsum("md,hd->mh", rows, gate_w, preferred_element_type=jnp.float32)
    up_pre = jnp.einsum("md,hd->mh", rows, up_w, preferred_element_type=jnp.float32)
    hidden = (jax.nn.silu(gate_pre) * up_pre).astype(jnp.bfloat16)
    return jnp.dot(hidden, down_w, preferred_element_type=jnp.float32).astype(jnp.bfloat16)


def backward_rows(rows, scaled, gate_w, up_w, down_w):
    gate_pre = jnp.einsum("md,hd->mh", rows, gate_w, preferred_element_type=jnp.float32)
    up_pre = jnp.einsum("md,hd->mh", rows, up_w, preferred_element_type=jnp.float32)
    sig = jax.nn.sigmoid(gate_pre)
    act = gate_pre * sig
    d_hidden = jnp.einsum("md,hd->mh", scaled, down_w, preferred_element_type=jnp.float32)
    d_up = (d_hidden * act).astype(jnp.bfloat16)
    d_gate = (d_hidden * up_pre * sig * (1.0 + gate_pre * (1.0 - sig))).astype(jnp.bfloat16)
    back = jnp.dot(d_gate, gate_w, preferred_element_type=jnp.float32) + jnp.dot(
        d_up, up_w, preferred_element_type=jnp.float32
    )
    return back.astype(jnp.bfloat16)


def shards(
    section_acts,
    section_input_gradients,
    saved_input,
    fwd_routes,
    fwd_probs,
    back_routes,
    back_probs,
    w_gate,
    w_up,
    w_down,
):
    split = lax.axis_size("expert") // E_WIN
    group = lax.axis_index("expert") // split
    x_in = from_behind(section_acts, "section", 1)[0]
    dy_in = from_behind(section_input_gradients, "section", -1)[0]
    backward_input = saved_input[0]
    count = x_in.shape[0]
    width = x_in.shape[1]
    gate_w = w_gate[0]
    up_w = w_up[0]
    down_w = w_down[0]
    f_pick, f_weight = route_tables(fwd_routes[0], fwd_probs[0], group * count, count)
    b_pick, b_weight = route_tables(back_routes[0], back_probs[0], group * count, count)
    scale = jnp.sum(b_weight, axis=0)
    fwd_send = fan_out(pick_rows(f_pick, x_in).astype(jnp.bfloat16), split)
    backward_outbound = fan_out(pick_rows(b_pick, backward_input).astype(jnp.bfloat16), split)
    grad_send = fan_out((pick_rows(b_pick, dy_in) * scale[:, None]).astype(jnp.bfloat16), split)
    piece = lax.all_to_all(fwd_send, "expert", split_axis=1, concat_axis=1, tiled=True)
    slots = piece.shape[0]
    made = forward_rows(expert_rows(piece), gate_w, up_w, down_w)
    made_back = lax.all_to_all(
        slot_layout(made, slots, width), "expert", split_axis=1, concat_axis=1, tiled=True
    )
    pieces = (
        lax.all_to_all(backward_outbound, "expert", split_axis=1, concat_axis=1, tiled=True),
        lax.all_to_all(grad_send, "expert", split_axis=1, concat_axis=1, tiled=True),
    )
    slots = pieces[0].shape[0]
    back = backward_rows(expert_rows(pieces[0]), expert_rows(pieces[1]), gate_w, up_w, down_w)
    grad_back = lax.all_to_all(
        slot_layout(back, slots, width), "expert", split_axis=1, concat_axis=1, tiled=True
    )
    high = lax.Precision.HIGHEST
    moe = jnp.dot(f_weight, fold_slices(made_back, split), precision=high)
    dx_moe = jnp.dot(b_pick, fold_slices(grad_back, split), precision=high)
    section_out = (x_in.astype(jnp.float32) + moe).astype(jnp.bfloat16)
    input_grads = (dy_in.astype(jnp.float32) + dx_moe).astype(jnp.bfloat16)
    return (section_out[None], input_grads[None])


def solution(mesh):
    return jax.shard_map(
        shards,
        mesh=mesh,
        in_specs=(
            P("section", "expert", None),
            P("section", "expert", None),
            P("section", "expert", None),
            P("section", None, None),
            P("section", None, None),
            P("section", None, None),
            P("section", None, None),
            P("section", "expert", None),
            P("section", "expert", None),
            P("section", "expert", None),
        ),
        out_specs=(P("section", "expert", None), P("section", "expert", None)),
        check_vma=False,
    )
```

profile of v0, /device:TPU:0, one launch (start us, length us, event | category | flops | bytes accessed | tf_op | source)
XLA Modules:
  0.0 122.3 jit_solution(15047384021287468297)
XLA Ops:
  0.6 2.4 %collective-permute-start.1 = (bf16[1,192,2048]{2,1,0:T(8,128)(2,1)}, bf16[1,192,2048]{2,1,0:T(8,128)(2,1)S(1)}, u32[]{:S(2)}, u32[]{:S(2)}) collective-permute-start(bf16[1,192,2048]{2,1,0:T(8,128)(2,1)} %param.11), channel_id=1, source_target_pairs={{0,3},{1,0},{2,1},{3,2},{4,7},{5,4},{6,5},{7,6},{8,11},{9,8},{10,9... | collective-permute-start | bytes 2359304 | tf_op jit(solution)/shard_map/ppermute | solution.py:13
  3.1 0.8 dynamic-slice_bitcast_fusion.1
  3.9 1.2 %reduce-window.16 = s32[4,2,128]{2,1,0:T(2,128)S(1)} reduce-window(s32[4,2,128]{2,1,0:T(2,128)S(1)} %reshape.203, s32[]{:T(128)} %constant.31.clone.1), window={size=1x1x128 pad=0_0x0_0x127_0}, to_apply=%region_6.7 | reduce-window | flops 130048 | bytes 8196 | tf_op jit(solution)/shard_map/reduce-window.2
  5.6 0.3 convolution_convert_fusion
  6.1 0.9 broadcast_in_dim.96
  7.0 5.8 %all-to-all-start.3 = ((bf16[12,8,2048]{2,0,1:T(8,128)(2,1)}), bf16[12,8,2048]{2,0,1:T(8,128)(2,1)S(1)}, u32[]{:S(2)}, u32[]{:S(2)}) async-start(bf16[12,8,2048]{2,0,1:T(8,128)(2,1)} %bitcast.21), calls=%async_computation.3 | async-start | bytes 1048576 | tf_op jit(solution)/shard_map/all_to_all | solution.py:121
  12.8 0.8 dynamic-slice_bitcast_fusion
  13.7 1.2 %reduce-window.14 = s32[4,2,128]{2,1,0:T(2,128)S(1)} reduce-window(s32[4,2,128]{2,1,0:T(2,128)S(1)} %reshape.198, s32[]{:T(128)} %constant.31.clone.1), window={size=1x1x128 pad=0_0x0_0x127_0}, to_apply=%region_1.2 | reduce-window | flops 130048 | bytes 8196 | tf_op jit(solution)/shard_map/reduce-window
  15.6 11.5 %all-to-all-done.3 = bf16[12,8,2048]{2,0,1:T(8,128)(2,1)S(1)} async-done(((bf16[12,8,2048]{2,0,1:T(8,128)(2,1)}), bf16[12,8,2048]{2,0,1:T(8,128)(2,1)S(1)}, u32[]{:S(2)}, u32[]{:S(2)}) %all-to-all-start.3) | async-done | bytes 393248 | tf_op jit(solution)/shard_map/all_to_all | solution.py:121
  27.1 0.2 copy.80
  27.5 0.3 fusion.25
  27.9 0.8 broadcast_in_dim.94
  28.8 3.6 %all-to-all-start.2 = ((bf16[12,8,2048]{2,0,1:T(8,128)(2,1)}), bf16[12,8,2048]{2,0,1:T(8,128)(2,1)S(1)}, u32[]{:S(2)}, u32[]{:S(2)}) async-start(bf16[12,8,2048]{2,0,1:T(8,128)(2,1)} %bitcast.19), calls=%async_computation.2 | async-start | bytes 1048576 | tf_op jit(solution)/shard_map/all_to_all | solution.py:122
  32.4 6.0 %fusion.12 = f32[48,1024]{1,0:T(8,128)S(1)} fusion(bf16[48,4096]{1,0:T(8,128)(2,1)S(1)} %reshape.208, bf16[1,1024,4096]{2,1,0:T(8,128)(2,1)} %param.17), kind=kOutput, calls=%fused_computation.12 | convolution fusion | flops 402653184 | bytes 8978432 | tf_op jit(solution)/shard_map/md,hd->mh/dot_general | solution.py:73
  38.4 0.3 convolution_convert_fusion.1
  38.9 8.0 %all-to-all-done.2 = bf16[12,8,2048]{2,0,1:T(8,128)(2,1)S(1)} async-done(((bf16[12,8,2048]{2,0,1:T(8,128)(2,1)}), bf16[12,8,2048]{2,0,1:T(8,128)(2,1)S(1)}, u32[]{:S(2)}, u32[]{:S(2)}) %all-to-all-start.2) | async-done | bytes 393248 | tf_op jit(solution)/shard_map/all_to_all | solution.py:122
  46.9 0.9 broadcast_in_dim.88
  47.8 3.6 %all-to-all-start = ((bf16[12,8,2048]{2,0,1:T(8,128)(2,1)}), bf16[12,8,2048]{2,0,1:T(8,128)(2,1)S(1)}, u32[]{:S(2)}, u32[]{:S(2)}) async-start(bf16[12,8,2048]{2,0,1:T(8,128)(2,1)} %bitcast.6), calls=%async_computation | async-start | bytes 1048576 | tf_op jit(solution)/shard_map/all_to_all | solution.py:114
  51.4 0.2 copy.78
  51.8 6.0 %fusion = f32[48,1024]{1,0:T(8,128)S(1)} fusion(bf16[48,4096]{1,0:T(8,128)(2,1)S(1)} %reshape.206, bf16[1,1024,4096]{2,1,0:T(8,128)(2,1)} %param.19), kind=kOutput, calls=%fused_computation | convolution fusion | flops 402653184 | bytes 8978432 | tf_op jit(solution)/shard_map/md,hd->mh/dot_general | solution.py:77
  57.8 4.9 %fusion.4 = f32[48,4096]{1,0:T(8,128)S(1)} fusion(bf16[1,1024,4096]{2,1,0:T(8,128)(2,1)} %param.18, f32[48,1024]{1,0:T(8,128)S(1)} %fusion, f32[48,1024]{1,0:T(8,128)S(1)} %fusion.12), kind=kOutput, calls=%fused_computation.4 | convolution fusion | flops 402948096 | bytes 9568256 | tf_op jit(solution)/shard_map/dot_general | solution.py:80
  62.7 9.9 %fusion.19 = bf16[48,4096]{1,0:T(8,128)(2,1)S(1)} fusion(f32[48,4096]{1,0:T(8,128)S(1)} %fusion.4, bf16[1,1024,4096]{2,1,0:T(8,128)(2,1)} %param.17, f32[48,1024]{1,0:T(8,128)S(1)} %fusion, bf16[48,4096]{1,0:T(8,128)(2,1)S(1)} %reshape.208, bf16[1,1024,4096]{2,1,0:T(8,128)(2,1)} %param.18, f32[48,1024]{1,0:T(8,128)S(1)} %fusion.12), kind=kOutput, calls=%fused_computation.17 | convolution fusion | flops 806191104 | bytes 18743296 | tf_op jit(solution)/shard_map/dot_general | solution.py:80
  72.8 1.0 copy.81
  73.8 6.0 %all-to-all-start.4 = ((bf16[12,8,2048]{2,0,1:T(8,128)(2,1)}), bf16[12,8,2048]{2,0,1:T(8,128)(2,1)S(1)}, u32[]{:S(2)}, u32[]{:S(2)}) async-start(bf16[12,8,2048]{2,0,1:T(8,128)(2,1)} %copy.81), calls=%async_computation.4 | async-start | bytes 1048576 | tf_op jit(solution)/shard_map/all_to_all | solution.py:126
  79.8 0.2 copy.70
  80.1 6.0 %fusion.14 = f32[48,1024]{1,0:T(8,128)S(1)} fusion(bf16[48,4096]{1,0:T(8,128)(2,1)S(1)} %reshape.201, bf16[1,1024,4096]{2,1,0:T(8,128)(2,1)} %param.17), kind=kOutput, calls=%fused_computation.14 | convolution fusion | flops 402653184 | bytes 8978432 | tf_op jit(solution)/shard_map/md,hd->mh/dot_general | solution.py:66
  86.2 10.0 %fusion.22 = bf16[48,4096]{1,0:T(8,128)(2,1)S(1)} fusion(bf16[1,1024,4096]{2,1,0:T(8,128)(2,1)} %param.19, bf16[48,4096]{1,0:T(8,128)(2,1)S(1)} %reshape.201, bf16[1,1024,4096]{2,1,0:T(8,128)(2,1)} %param.18, f32[48,1024]{1,0:T(8,128)S(1)} %fusion.14), kind=kOutput, calls=%fused_computation.18 | convolution fusion | flops 805797888 | bytes 17760256 | tf_op jit(solution)/shard_map/dot_general | solution.py:69
  96.3 1.0 copy.71
  97.3 6.0 %all-to-all-start.1 = ((bf16[12,8,2048]{2,0,1:T(8,128)(2,1)}), bf16[12,8,2048]{2,0,1:T(8,128)(2,1)S(1)}, u32[]{:S(2)}, u32[]{:S(2)}) async-start(bf16[12,8,2048]{2,0,1:T(8,128)(2,1)} %copy.71), calls=%async_computation.1 | async-start | bytes 1048576 | tf_op jit(solution)/shard_map/all_to_all | solution.py:117
  103.5 13.4 %all-to-all-done.1 = bf16[12,8,2048]{2,0,1:T(8,128)(2,1)S(1)} async-done(((bf16[12,8,2048]{2,0,1:T(8,128)(2,1)}), bf16[12,8,2048]{2,0,1:T(8,128)(2,1)S(1)}, u32[]{:S(2)}, u32[]{:S(2)}) %all-to-all-start.1) | async-done | bytes 393248 | tf_op jit(solution)/shard_map/all_to_all | solution.py:117
  117.0 1.8 %fusion.45 = bf16[1,192,2048]{2,1,0:T(8,128)(2,1)} fusion(bf16[1,192,2048]{2,1,0:T(8,128)(2,1)S(1)} %copy-done.2, f32[12,4,2048]{2,0,1:T(8,128)S(1)} %convert_reduce_fusion, pred[192,12,4]{0,2,1:T(4,128)(4,1)S(1)} %get-tuple-element.2), kind=kOutput, calls=%fused_computation.36 | convolution fusion | flops 227672064 | bytes 1975296 | tf_op jit(solution)/shard_map/dot_general | solution.py:131
  118.8 3.5 %fusion.44 = bf16[1,192,2048]{2,1,0:T(8,128)(2,1)} fusion(bf16[1,192,2048]{2,1,0:T(8,128)(2,1)} %copy-done.3, f32[12,4,2048]{2,0,1:T(8,128)S(1)} %convert_reduce_fusion.1, f32[192,12,4]{0,2,1:T(4,128)S(1)} %fusion.72), kind=kOutput, calls=%fused_computation.35 | convolution fusion | flops 227672064 | bytes 2002944 | tf_op jit(solution)/shard_map/dot_general | solution.py:130
  (59 shorter events, 2.8 us)
Async XLA Ops:
  0.6 5.0 %copy-start = (bf16[1,192,2048]{2,1,0:T(8,128)(2,1)S(1)}, bf16[1,192,2048]{2,1,0:T(8,128)(2,1)}, u32[]{:S(2)}) copy-start(bf16[1,192,2048]{2,1,0:T(8,128)(2,1)} %param.12) | copy-start | bytes 2359300
  0.6 26.8 %collective-permute-start.1 = (bf16[1,192,2048]{2,1,0:T(8,128)(2,1)}, bf16[1,192,2048]{2,1,0:T(8,128)(2,1)S(1)}, u32[]{:S(2)}, u32[]{:S(2)}) collective-permute-start(bf16[1,192,2048]{2,1,0:T(8,128)(2,1)} %param.11), channel_id=1, source_target_pairs={{0,3},{1,0},{2,1},{3,2},{4,7},{5,4},{6,5},{7,6},{8,11},{9,8},{10,9... | collective-permute-start | bytes 2359304 | tf_op jit(solution)/shard_map/ppermute | solution.py:13
  7.0 20.1 %all-to-all-start.3 = ((bf16[12,8,2048]{2,0,1:T(8,128)(2,1)}), bf16[12,8,2048]{2,0,1:T(8,128)(2,1)S(1)}, u32[]{:S(2)}, u32[]{:S(2)}) async-start(bf16[12,8,2048]{2,0,1:T(8,128)(2,1)} %bitcast.21), calls=%async_computation.3 | async-start | bytes 1048576 | tf_op jit(solution)/shard_map/all_to_all | solution.py:121
  12.8 25.6 %collective-permute-start = (bf16[1,192,2048]{2,1,0:T(8,128)(2,1)}, bf16[1,192,2048]{2,1,0:T(8,128)(2,1)S(1)}, u32[]{:S(2)}, u32[]{:S(2)}) collective-permute-start(bf16[1,192,2048]{2,1,0:T(8,128)(2,1)} %param.10), channel_id=1, source_target_pairs={{0,1},{1,2},{2,3},{3,0},{4,5},{5,6},{6,7},{7,4},{8,9},{9,10},{10,1... | collective-permute-start | bytes 2359304 | tf_op jit(solution)/shard_map/ppermute | solution.py:13
  27.4 1.3 %copy-start.1 = (bf16[1,192,2048]{2,1,0:T(8,128)(2,1)}, bf16[1,192,2048]{2,1,0:T(8,128)(2,1)S(1)}, u32[]{:S(2)}) copy-start(bf16[1,192,2048]{2,1,0:T(8,128)(2,1)S(1)} %collective-permute-done.1) | copy-start | bytes 2359300
  28.8 18.1 %all-to-all-start.2 = ((bf16[12,8,2048]{2,0,1:T(8,128)(2,1)}), bf16[12,8,2048]{2,0,1:T(8,128)(2,1)S(1)}, u32[]{:S(2)}, u32[]{:S(2)}) async-start(bf16[12,8,2048]{2,0,1:T(8,128)(2,1)} %bitcast.19), calls=%async_computation.2 | async-start | bytes 1048576 | tf_op jit(solution)/shard_map/all_to_all | solution.py:122
  38.4 9.3 %copy-start.3 = (bf16[1,192,2048]{2,1,0:T(8,128)(2,1)}, bf16[1,192,2048]{2,1,0:T(8,128)(2,1)S(1)}, u32[]{:S(2)}) copy-start(bf16[1,192,2048]{2,1,0:T(8,128)(2,1)S(1)} %collective-permute-done) | copy-start | bytes 2359300
  47.8 26.0 %all-to-all-start = ((bf16[12,8,2048]{2,0,1:T(8,128)(2,1)}), bf16[12,8,2048]{2,0,1:T(8,128)(2,1)S(1)}, u32[]{:S(2)}, u32[]{:S(2)}) async-start(bf16[12,8,2048]{2,0,1:T(8,128)(2,1)} %bitcast.6), calls=%async_computation | async-start | bytes 1048576 | tf_op jit(solution)/shard_map/all_to_all | solution.py:114
  73.8 23.5 %all-to-all-start.4 = ((bf16[12,8,2048]{2,0,1:T(8,128)(2,1)}), bf16[12,8,2048]{2,0,1:T(8,128)(2,1)S(1)}, u32[]{:S(2)}, u32[]{:S(2)}) async-start(bf16[12,8,2048]{2,0,1:T(8,128)(2,1)} %copy.81), calls=%async_computation.4 | async-start | bytes 1048576 | tf_op jit(solution)/shard_map/all_to_all | solution.py:126
  86.2 30.8 %copy-start.2 = (bf16[1,192,2048]{2,1,0:T(8,128)(2,1)S(1)}, bf16[1,192,2048]{2,1,0:T(8,128)(2,1)}, u32[]{:S(2)}) copy-start(bf16[1,192,2048]{2,1,0:T(8,128)(2,1)} %copy-done.1) | copy-start | bytes 2359300
  97.3 19.5 %all-to-all-start.1 = ((bf16[12,8,2048]{2,0,1:T(8,128)(2,1)}), bf16[12,8,2048]{2,0,1:T(8,128)(2,1)S(1)}, u32[]{:S(2)}, u32[]{:S(2)}) async-start(bf16[12,8,2048]{2,0,1:T(8,128)(2,1)} %copy.71), calls=%async_computation.1 | async-start | bytes 1048576 | tf_op jit(solution)/shard_map/all_to_all | solution.py:117
where the time goes:
time: 123 us; the launch traced here: 122 us
  matrix products  48.9 us (40%)
  waiting for transfers between devices  32.9 us (27%)
  starting transfers between devices  27.5 us (22%)
  local copies, waits for them, and re-layouts  8.93 us (7%)
  other arithmetic  3.16 us (3%)
    all_to_all x1, waiting for transfers between devices, shards(): lax.all_to_all(slot_layout(made, slots, width), 'expert', split_axis=1, c...  13.4 us
    all_to_all x1, waiting for transfers between devices, shards(): lax.all_to_all(backward_outbound, 'expert', split_axis=1, concat_axis=1,...  11.5 us
    dot_general x1, matrix products, forward_rows(): jnp.dot(hidden, down_w, preferred_element_type=jnp.float32)  9.96 us
    dot_general x1, matrix products, backward_rows(): jnp.dot(d_gate, gate_w, preferred_element_type=jnp.float32)  9.92 us
    all_to_all x1, waiting for transfers between devices, shards(): lax.all_to_all(grad_send, 'expert', split_axis=1, concat_axis=1, tiled=True)  7.98 us
    dot_general x1, matrix products, backward_rows(): jnp.einsum('md,hd->mh', scaled, down_w, preferred_element_type=jnp.float32)  6.01 us
    dot_general x1, matrix products, forward_rows(): jnp.einsum('md,hd->mh', rows, gate_w, preferred_element_type=jnp.float32)  6.01 us
    dot_general x1, matrix products, backward_rows(): jnp.einsum('md,hd->mh', rows, gate_w, preferred_element_type=jnp.float32)  6 us
  transfers between devices with their start and end apart: 7, of which 3 were waited for; matrix products, arithmetic and copies ran while one was open for 45% of the time, Pallas kernels for 0%

commit v1 on v0

v1 whole, which is shorter than its diff:
```python
import functools
import jax
import jax.numpy as jnp
from jax import lax
from jax.experimental import pallas as pl
from jax.experimental.pallas import tpu as pltpu
from jax.sharding import PartitionSpec as P

N_ROUTED = 256
TOP = 8
E_WIN = 4
F32 = jnp.float32
BF16 = jnp.bfloat16
VMEM_LIMIT = 8 << 20


def mm(a, b, ca=1, cb=0, precision=None):
    dims = (((ca,), (cb,)), ((), ()))
    return lax.dot_general(a, b, dims, precision=precision, preferred_element_type=F32)


class Sizes:
    def __init__(self, count, width, hidden, split):
        self.count, self.width, self.hidden, self.split = count, width, hidden, split
        self.cap = count * TOP * 2 // N_ROUTED
        self.slots = E_WIN * self.cap
        self.parts = min(4, width // 128)
        self.cols = width // self.parts
        self.piece = self.parts * self.cap
        self.spread = E_WIN * self.piece


def place_of(sz, i):
    piece = sum([(i >= sz.piece * n).astype(jnp.int32) for n in range(1, E_WIN)])
    i = i - sz.piece * piece
    part = sum([(i >= sz.cap * n).astype(jnp.int32) for n in range(1, sz.parts)])
    return piece, part, i - sz.cap * part


def one_hot(mask):
    return jnp.where(mask, 1.0, 0.0).astype(BF16)


def route_masks(routes, probs, expert, place, earlier):
    chosen = jnp.zeros(expert.shape, F32)
    weight = jnp.zeros(expert.shape, F32)
    for c in range(TOP):
        hit = routes[c : c + 1, :] == expert
        chosen += jnp.where(hit, 1.0, 0.0)
        if probs is not None:
            weight += jnp.where(hit, probs[c : c + 1, :], 0.0)
    before = mm(chosen.astype(BF16), earlier)
    mask = (chosen > 0.5) & (jnp.abs(before - place.astype(F32)) < 0.5)
    return mask, weight


def my_group(ref, group, count):
    block = ref[:, :count]
    for n in range(1, E_WIN):
        block = jnp.where(group == n, ref[:, n * count : (n + 1) * count], block)
    return block


def earlier_tokens(sz):
    shape = (sz.count, sz.count)
    return one_hot(lax.broadcasted_iota(jnp.int32, shape, 0) < lax.broadcasted_iota(jnp.int32, shape, 1))


def piece_masks(sz, routes_ref, probs_ref):
    group = lax.axis_index("expert") // sz.split
    shape = (sz.spread, sz.count)
    piece, part, place = place_of(sz, lax.broadcasted_iota(jnp.int32, shape, 0))
    routes = my_group(routes_ref, group, sz.count)
    probs = None if probs_ref is None else my_group(probs_ref, group, sz.count)
    mask, weight = route_masks(routes, probs, piece ^ group, place, earlier_tokens(sz))
    return mask, weight, part


def pick(sz, mask, part, values):
    picked = jnp.zeros((sz.spread, sz.cols), F32)
    for q in range(sz.parts):
        picked += mm(one_hot(mask & (part == q)), values[:, q * sz.cols : (q + 1) * sz.cols])
    return picked


def put_pieces(sz, values, pieces):
    for o, piece in enumerate(pieces):
        piece[...] = values[o * sz.piece : (o + 1) * sz.piece].astype(BF16)


def fetch(pairs, sems):
    copies = [pltpu.make_async_copy(src, dst, sems.at[n]) for n, (src, dst) in enumerate(pairs)]
    for c in copies:
        c.start()
    return copies


def local_kernel(sz, fr, fp, br, bp, saved, w_f, w_b, *rest):
    pieces, (fr_v, fp_v, br_v, bp_v, saved_v, sems) = rest[:E_WIN], rest[E_WIN:]
    pairs = [(br, br_v), (bp, bp_v), (fr, fr_v), (fp, fp_v), (saved, saved_v)]
    copies = fetch(pairs, sems)
    for c in copies[:4]:
        c.wait()
    mask, _, part = piece_masks(sz, br_v, bp_v)
    w_b[...] = one_hot(mask)
    copies[4].wait()
    put_pieces(sz, pick(sz, mask, part, saved_v), pieces)
    mask, weight, _ = piece_masks(sz, fr_v, fp_v)
    w_f[...] = jnp.where(mask, weight, 0.0)


def pick_kernel(sz, br, bp, fr, grads, acts, after, *refs):
    g_out, x_out, (grads_v, acts_v, sems) = refs[:E_WIN], refs[E_WIN : 2 * E_WIN], refs[2 * E_WIN :]
    copies = fetch([(grads, grads_v), (acts, acts_v)], sems)
    g_mask, weight, part = piece_masks(sz, br, bp)
    scale = jnp.sum(jnp.where(g_mask, weight, 0.0), axis=1, keepdims=True)
    x_mask, _, _ = piece_masks(sz, fr, None)
    copies[0].wait()
    put_pieces(sz, pick(sz, g_mask, part, grads_v) * scale, g_out)
    copies[1].wait()
    put_pieces(sz, pick(sz, x_mask, part, acts_v), x_out)


def unpick(sz, cat, rows):
    shape = (sz.slots, sz.spread)
    slot = lax.broadcasted_iota(jnp.int32, shape, 0)
    piece, part, place = place_of(sz, lax.broadcasted_iota(jnp.int32, shape, 1))
    here = slot == piece * sz.cap + place
    for q in range(sz.parts):
        rows[:, q * sz.cols : (q + 1) * sz.cols] = mm(one_hot(here & (part == q)), cat).astype(BF16)


def unpick_kernel(sz, *refs):
    unpick(sz, jnp.concatenate([p[...] for p in refs[:E_WIN]], axis=0), refs[-1])


def fold_kernel(sz, *refs):
    slices, pieces = refs[: sz.split], refs[sz.split :]
    rows = slices[0][...].astype(F32)
    for s in slices[1:]:
        rows += s[...].astype(F32)
    rows = rows.astype(BF16)
    shape = (sz.spread, sz.slots)
    piece, part, place = place_of(sz, lax.broadcasted_iota(jnp.int32, shape, 0))
    here = lax.broadcasted_iota(jnp.int32, shape, 1) == piece * sz.cap + place
    out = jnp.zeros((sz.spread, sz.cols), F32)
    for q in range(sz.parts):
        out += mm(one_hot(here & (part == q)), rows[:, q * sz.cols : (q + 1) * sz.cols])
    put_pieces(sz, out, pieces)


def combine_kernel(sz, weighted, *refs):
    values, w, pieces, out = refs[0], refs[1], refs[2 : 2 + E_WIN], refs[2 + E_WIN]
    cat = jnp.concatenate([p[...] for p in pieces], axis=0)
    _, part, _ = place_of(sz, lax.broadcasted_iota(jnp.int32, (sz.spread, sz.count), 0))
    for q in range(sz.parts):
        columns = slice(q * sz.cols, (q + 1) * sz.cols)
        if weighted:
            mine = jnp.where(part == q, w[...], 0.0)
            high = mine.astype(BF16)
            low = (mine - high.astype(F32)).astype(BF16)
            total = mm(high, cat, 0, 0) + mm(low, cat, 0, 0)
        else:
            total = mm(jnp.where(part == q, w[...].astype(F32), 0.0).astype(BF16), cat, 0, 0)
        out[:, columns] = (values[:, columns].astype(F32) + total).astype(BF16)


def lay_rows(sz, slices, rows):
    me = lax.rem(lax.axis_index("expert"), sz.split)
    for j, s in enumerate(slices):
        at = lax.rem(me + sz.split - j, sz.split) * sz.width
        rows[:, pl.ds(pl.multiple_of(at, 128), sz.width)] = s[...]


def load_kernel(weight, after, held, sems):
    block = weight.shape[0] // sems.shape[0]
    cut = [pl.ds(n * block, block) for n in range(sems.shape[0])]
    for c in fetch([(weight.at[c], held.at[c]) for c in cut], sems):
        c.wait()


def load_and_pre_kernel(sz, chunks, *refs):
    n = sz.split
    slices, (wg, wu, wg_near, wu_near, gate, up, rows, turned, sems) = refs[:n], refs[n:]
    block = sz.hidden // chunks
    cut = [pl.ds(c * block, block) for c in range(chunks)]
    steps = [(src.at[c], dst, c, out) for c in cut for src, dst, out in ((wg, wg_near, gate), (wu, wu_near, up))]
    copies = [pltpu.make_async_copy(src, dst.at[c], sems.at[n]) for n, (src, dst, c, _) in enumerate(steps)]
    ahead = 3
    always = lax.axis_index("expert") >= 0
    for c in copies[:ahead]:
        c.start()
    lay_rows(sz, slices, rows)
    turned[...] = rows[...].T
    for n, (_, dst, c, out) in enumerate(steps):
        copies[n].wait()
        if n + ahead < len(steps):
            copies[n + ahead].start()

        @pl.when(always)
        def _(dst=dst, c=c, out=out):
            out[c, :] = mm(dst[c, :], turned[...])


def columns_of(sz, j):
    me = lax.rem(lax.axis_index("expert"), sz.split)
    at = lax.rem(me + j, sz.split) * sz.width
    block = min(512, sz.width)
    return [
        (pl.ds(n * block, block), pl.ds(pl.multiple_of(at + n * block, 128), block))
        for n in range(sz.width // block)
    ]


def backward_slices(sz, js, d_gate, d_up, wg, wu, outs):
    for j, out in zip(js, outs):
        for here, there in columns_of(sz, j):
            out[:, here] = (mm(d_gate, wg[:, there]) + mm(d_up, wu[:, there])).astype(BF16)


def forward_slices(sz, js, hidden, wd, outs):
    for j, out in zip(js, outs):
        for here, there in columns_of(sz, j):
            out[:, here] = mm(hidden, wd[:, there]).astype(BF16)


def backward_kernel(sz, *refs):
    n = sz.split
    slices, (gate, up, wd, wg, wu, d_gate, d_up), outs, rows = refs[:n], refs[n : n + 7], refs[n + 7 : -1], refs[-1]
    lay_rows(sz, slices, rows)
    dh = mm(wd[...], rows[...].T)
    g = gate[...]
    sig = jax.nn.sigmoid(g)
    d_up[...] = (dh * (g * sig)).T.astype(BF16)
    d_gate[...] = (dh * up[...] * sig * (1.0 + g * (1.0 - sig))).T.astype(BF16)
    backward_slices(sz, range(1, n), d_gate[...], d_up[...], wg, wu, outs)


def backward_own_kernel(sz, d_gate, d_up, wg, wu, out):
    backward_slices(sz, (0,), d_gate[...], d_up[...], wg, wu, (out,))


def forward_kernel(sz, *refs):
    n = sz.split
    slices, (wg, wu, wd, hidden), outs, rows = refs[:n], refs[n : n + 4], refs[n + 4 : -1], refs[-1]
    lay_rows(sz, slices, rows)
    turned = rows[...].T
    gate = mm(wg[...], turned)
    up = mm(wu[...], turned)
    hidden[...] = (gate * jax.nn.sigmoid(gate) * up).T.astype(BF16)
    forward_slices(sz, range(1, n), hidden[...], wd, outs)


def forward_own_kernel(sz, hidden, wd, out):
    forward_slices(sz, (0,), hidden[...], wd, (out,))


def near(kernel, outs, args, name, us=0.3, far=(), scratch=()):
    spec = lambda i: pl.BlockSpec(memory_space=pltpu.HBM if i in far else pltpu.VMEM)
    args = [pltpu.with_memory_space_constraint(a, pltpu.HBM) if i in far else a for i, a in enumerate(args)]
    return pl.pallas_call(
        kernel,
        out_shape=[jax.ShapeDtypeStruct(s, d) for s, d in outs],
        name=name,
        in_specs=[spec(i) for i in range(len(args))],
        out_specs=[pl.BlockSpec(memory_space=pltpu.VMEM) for _ in outs],
        scratch_shapes=list(scratch),
        compiler_params=pltpu.CompilerParams(vmem_limit_bytes=VMEM_LIMIT),
        cost_estimate=pl.CostEstimate(flops=int(us * 1.1e9), bytes_accessed=1 << 16, transcendentals=0),
    )(*args)


def shards(
    section_acts,
    section_input_gradients,
    saved_input,
    fwd_routes,
    fwd_probs,
    back_routes,
    back_probs,
    w_gate,
    w_up,
    w_down,
):
    experts = lax.axis_size("expert")
    sections = lax.axis_size("section")
    split = experts // E_WIN
    acts, grads, saved = section_acts[0], section_input_gradients[0], saved_input[0]
    wg, wu, wd = w_gate[0], w_up[0], w_down[0]
    count, width = acts.shape
    sz = Sizes(count, width, wg.shape[0], split)
    full = width * split
    piece = ((sz.piece, sz.cols), BF16)
    rows = ((sz.slots, width), BF16)

    def by_section(x, by):
        return lax.ppermute(x, "section", [(i, (i + by) % sections) for i in range(sections)])

    def to_expert(x, offset, by):
        pairs = [
            (e * sections + n, ((e // split ^ offset) * split + e % split) * sections + (n + by) % sections)
            for e in range(experts)
            for n in range(sections)
        ]
        return lax.ppermute(x, ("expert", "section"), pairs)

    def exchange(pieces, by=0):
        return [p if o == 0 and by == 0 else to_expert(p, o, by) for o, p in enumerate(pieces)]

    def along_group(x, by):
        pairs = [(e, e // split * split + (e + by) % split) for e in range(experts)]
        return lax.ppermute(x, "expert", pairs)

    def gather(x):
        return [x] + [along_group(x, j) for j in range(1, split)]

    def scatter(slices):
        return [along_group(s, j) for j, s in enumerate(slices, 1)]

    part = functools.partial
    pieces = [piece] * E_WIN
    block = ((count, width), BF16)
    held = ((sz.spread, sz.cols), BF16)
    route_scratch = [pltpu.VMEM(fwd_routes.shape[:0:-1], d) for d in (jnp.int32, F32)]
    block_scratch = pltpu.VMEM((count, width), BF16)
    rows_scratch = pltpu.VMEM((sz.slots, full), BF16)

    fr, fp, br, bp = fwd_routes[0].T, fwd_probs[0].T, back_routes[0].T, back_probs[0].T
    br_next, bp_next = by_section(back_routes, 1)[0].T, by_section(back_probs, 1)[0].T
    fr_next = by_section(fwd_routes, -1)[0].T
    w_f, w_b, *b_out = near(
        part(local_kernel, sz),
        [((sz.spread, count), F32), ((sz.spread, count), BF16)] + pieces,
        (fr, fp, br, bp, saved),
        "local",
        2.0,
        far=range(5),
        scratch=route_scratch * 2 + [block_scratch, pltpu.SemaphoreType.DMA((5,))],
    )
    picked = near(
        part(pick_kernel, sz),
        pieces * 2,
        (br_next, bp_next, fr_next, grads, acts, w_b),
        "pick",
        2.0,
        far=(3, 4),
        scratch=[block_scratch, block_scratch, pltpu.SemaphoreType.DMA((2,))],
    )
    g_in = exchange(picked[:E_WIN], -1)
    x_in = exchange(picked[E_WIN:], 1)
    b_in = exchange(b_out)
    wd_near = near(
        load_kernel, [(wd.shape, BF16)], (wd, picked[0]), "load", 3.5, far=(0,), scratch=[pltpu.SemaphoreType.DMA((2,))]
    )[0]
    unpicked = lambda pieces, name: near(part(unpick_kernel, sz), [rows], pieces, name)[0]
    b_rows = gather(unpicked(b_in, "unpick_saved"))
    g_rows = gather(unpicked(g_in, "unpick_gradients"))
    x_rows = gather(unpicked(x_in, "unpick_acts"))

    chunks = 4
    hidden_f32 = ((sz.hidden, sz.slots), F32)
    hidden_bf16 = ((sz.slots, sz.hidden), BF16)
    wg_near, wu_near, gate, up = near(
        part(load_and_pre_kernel, sz, chunks),
        [(wg.shape, BF16)] * 2 + [hidden_f32] * 2,
        (*b_rows, wg, wu),
        "pre",
        6.0,
        far=(split, split + 1),
        scratch=[rows_scratch, pltpu.VMEM((full, sz.slots), BF16), pltpu.SemaphoreType.DMA((2 * chunks,))],
    )
    d_gate, d_up, *back = near(
        part(backward_kernel, sz),
        [hidden_bf16] * 2 + [rows] * (split - 1),
        (*g_rows, gate, up, wd_near, wg_near, wu_near),
        "backward",
        4.0,
        scratch=[rows_scratch],
    )
    back_in = scatter(back)
    back_own = near(part(backward_own_kernel, sz), [rows], (d_gate, d_up, wg_near, wu_near), "backward_own", 2.0)
    hidden, *made = near(
        part(forward_kernel, sz),
        [hidden_bf16] + [rows] * (split - 1),
        (*x_rows, wg_near, wu_near, wd_near),
        "forward",
        5.0,
        scratch=[rows_scratch],
    )
    made_in = scatter(made)
    made_own = near(part(forward_own_kernel, sz), [rows], (hidden, wd_near), "forward_own", 1.0)
    back_pieces = exchange(near(part(fold_kernel, sz), pieces, (*back_own, *back_in), "fold_backward"))
    made_pieces = exchange(near(part(fold_kernel, sz), pieces, (*made_own, *made_in), "fold_forward"))

    acts, grads, *_ = lax.optimization_barrier((acts, grads, *g_in, *x_in))
    x_full, dy_full = by_section(acts, 1), by_section(grads, -1)
    input_grads = near(part(combine_kernel, sz, False), [block], (dy_full, w_b, *back_pieces), "combine_gradients", 1.5)[0]
    section_out = near(part(combine_kernel, sz, True), [block], (x_full, w_f, *made_pieces), "combine_acts", 1.5)[0]
    return (section_out[None], input_grads[None])


def solution(mesh):
    return jax.shard_map(
        shards,
        mesh=mesh,
        in_specs=(
            P("section", "expert", None),
            P("section", "expert", None),
            P("section", "expert", None),
            P("section", None, None),
            P("section", None, None),
            P("section", None, None),
            P("section", None, None),
            P("section", "expert", None),
            P("section", "expert", None),
            P("section", "expert", None),
        ),
        out_specs=(P("section", "expert", None), P("section", "expert", None)),
        check_vma=False,
    )
```

time: 123 us -> 72.5 us (0.59)
  matrix products: 48.9 us -> 0 us
  Pallas kernels: 0 us -> 33.1 us
  waiting for transfers between devices: 32.9 us -> 1.37 us
  starting transfers between devices: 27.5 us -> 37 us
  local copies, waits for them, and re-layouts: 8.93 us -> 0.01 us
  other arithmetic: 3.16 us -> 0 us
    dot_general x11 -> x0, matrix products: 48.9 us -> none  [the longest x1 9.96 us: forward_rows(): jnp.dot(hidden, down_w, preferred_element_type=jnp.float32)]
    ppermute x2 -> x27, starting transfers between devices: 2.43 us -> 37 us  [the longest x17 26.9 us: to_expert(): return lax.ppermute(x, ('expert', 'section'), pairs)]
    pallas_call x0 -> x15, Pallas kernels: none -> 33.1 us  [near(): pl.pallas_call(kernel, out_shape=[jax.ShapeDtypeStruct(s, d) for s, d in...]
    all_to_all x5 -> x0, waiting for transfers between devices: 32.9 us -> none  [the longest x1 13.4 us: shards(): lax.all_to_all(slot_layout(made, slots, width), 'expert', split_axis=1, c...]
    all_to_all x5 -> x0, starting transfers between devices: 25.1 us -> none  [the longest x1 6 us: shards(): lax.all_to_all(slot_layout(made, slots, width), 'expert', split_axis=1, c...]
    broadcast_in_dim x10 -> x0, local copies, waits for them, and re-layouts: 3.96 us -> none  [the longest x9 3.16 us: fan_out(): jnp.broadcast_to(rows.reshape(capacity, E_WIN, 1, width), (capacity, E_WI...]
    reshape x8 -> x0, local copies, waits for them, and re-layouts: 2.75 us -> none  [the longest x4 2.33 us: slot_layout(): return rows.reshape(count, rows.shape[1] // width * E_WIN, width)]
    another operation x4 -> x0, other arithmetic: 2.52 us -> none
  transfers between devices with their start and end apart: 7 -> 27, of which waited for: 3 -> 3; matrix products, arithmetic and copies ran while one was open for 45% -> 0% of each run, Pallas kernels for 0% -> 44%
where the time goes in v1:
time: 72.5 us; the launch traced here: 72.4 us
  starting transfers between devices  37 us (51%)
  Pallas kernels  33.1 us (46%)
  waiting for transfers between devices  1.37 us (2%)
  between operations  0.86 us (1%)
    pallas_call x15, Pallas kernels, near(): pl.pallas_call(kernel, out_shape=[jax.ShapeDtypeStruct(s, d) for s, d in...  33.1 us
    ppermute x17, starting transfers between devices, to_expert(): return lax.ppermute(x, ('expert', 'section'), pairs)  26.9 us
    ppermute x5, starting transfers between devices, along_group(): return lax.ppermute(x, 'expert', pairs)  5.85 us
    ppermute x5, starting transfers between devices, by_section(): lax.ppermute(x, 'section', [(i, (i + by) % sections) for i in range(secti...  4.21 us
  transfers between devices with their start and end apart: 27, of which 3 were waited for; matrix products, arithmetic and copies ran while one was open for 0% of the time, Pallas kernels for 44%

profile of v1, /device:TPU:0, one launch (start us, length us, event | category | flops | bytes accessed | tf_op | source)
XLA Modules:
  0.0 72.4 jit_solution(11007562270001717367)
XLA Ops:
  0.6 0.5 collective-permute-start
  1.1 2.6 %collective-permute-start.1 = (f32[1,768,8]{1,2,0:T(8,128)}, f32[1,768,8]{1,2,0:T(8,128)S(1)}, u32[]{:S(2)}, u32[]{:S(2)}) collective-permute-start(f32[1,768,8]{1,2,0:T(8,128)} %param.16), channel_id=1, source_target_pairs={{0,1},{1,2},{2,3},{3,0},{4,5},{5,6},{6,7},{7,4},{8,9},{9,10},{10,1... | collective-permute-start | bytes 73736 | tf_op jit(solution)/shard_map/ppermute | solution.py:297
  3.7 2.1 %local.1 = (f32[192,192]{1,0:T(8,128)S(1)}, bf16[192,192]{1,0:T(8,128)(2,1)S(1)}, bf16[48,512]{1,0:T(8,128)(2,1)S(1)}, bf16[48,512]{1,0:T(8,128)(2,1)S(1)}, bf16...) custom-call(s32[8,768]{1,0:T(8,128)} %bitcast.43, f32[8,768]{1,0:T(8,128)} %bitcast.40, s32[8,768]{1,0:T(8,128)} %bitcast.41, ...), custom_call_target="tpu_custom_call" | custom-call | flops 2200000000 | bytes 65536 | tf_op jit(solution)/shard_map/local/pallas_call | solution.py:261
  5.9 1.8 %collective-permute-start.13 = (bf16[48,512]{1,0:T(8,128)(2,1)S(1)}, bf16[48,512]{1,0:T(8,128)(2,1)S(1)}, u32[]{:S(2)}, u32[]{:S(2)}) collective-permute-start(bf16[48,512]{1,0:T(8,128)(2,1)S(1)} %get-tuple-element.47), channel_id=1, source_target_pairs={{0,8},{1,9},{2,10},{3,11},{4,12},{5,13},{6,14},{7,15},{8,0},{9,1},... | collective-permute-start | bytes 147464 | tf_op jit(solution)/shard_map/ppermute | solution.py:305
  7.7 2.6 %collective-permute-start.14 = (bf16[48,512]{1,0:T(8,128)(2,1)S(1)}, bf16[48,512]{1,0:T(8,128)(2,1)S(1)}, u32[]{:S(2)}, u32[]{:S(2)}) collective-permute-start(bf16[48,512]{1,0:T(8,128)(2,1)S(1)} %get-tuple-element.48), channel_id=1, source_target_pairs={{0,16},{1,17},{2,18},{3,19},{4,20},{5,21},{6,22},{7,23},{8,24},{9,... | collective-permute-start | bytes 147464 | tf_op jit(solution)/shard_map/ppermute | solution.py:305
  10.3 2.5 %pick.1 = (bf16[48,512]{1,0:T(8,128)(2,1)S(1)}, bf16[48,512]{1,0:T(8,128)(2,1)S(1)}, bf16[48,512]{1,0:T(8,128)(2,1)S(1)}, bf16[48,512]{1,0:T(8,128)(2,1)S(1)}, b...) custom-call(s32[8,768]{1,0:T(8,128)S(1)} %bitcast.29, ...), custom_call_target="tpu_custom_call" | custom-call | flops 2200000000 | bytes 65536 | tf_op jit(solution)/shard_map/pick/pallas_call | solution.py:261
  12.9 1.9 %collective-permute-start.4 = (bf16[48,512]{1,0:T(8,128)(2,1)S(1)}, bf16[48,512]{1,0:T(8,128)(2,1)S(1)}, u32[]{:S(2)}, u32[]{:S(2)}) collective-permute-start(bf16[48,512]{1,0:T(8,128)(2,1)S(1)} %get-tuple-element.37), channel_id=1, source_target_pairs={{0,11},{1,8},{2,9},{3,10},{4,15},{5,12},{6,13},{7,14},{8,3},{9,0},... | collective-permute-start | bytes 147464 | tf_op jit(solution)/shard_map/ppermute | solution.py:305
  14.8 3.2 %collective-permute-start.5 = (bf16[48,512]{1,0:T(8,128)(2,1)S(1)}, bf16[48,512]{1,0:T(8,128)(2,1)S(1)}, u32[]{:S(2)}, u32[]{:S(2)}) collective-permute-start(bf16[48,512]{1,0:T(8,128)(2,1)S(1)} %get-tuple-element.38), channel_id=1, source_target_pairs={{0,19},{1,16},{2,17},{3,18},{4,23},{5,20},{6,21},{7,22},{8,27},{9,... | collective-permute-start | bytes 147464 | tf_op jit(solution)/shard_map/ppermute | solution.py:305
  18.0 3.5 %collective-permute-start.10 = (bf16[48,512]{1,0:T(8,128)(2,1)S(1)}, bf16[48,512]{1,0:T(8,128)(2,1)S(1)}, u32[]{:S(2)}, u32[]{:S(2)}) collective-permute-start(bf16[48,512]{1,0:T(8,128)(2,1)S(1)} %get-tuple-element.43), channel_id=1, source_target_pairs={{0,25},{1,26},{2,27},{3,24},{4,29},{5,30},{6,31},{7,28},{8,17},{9,... | collective-permute-start | bytes 147464 | tf_op jit(solution)/shard_map/ppermute | solution.py:305
  21.8 1.4 %collective-permute-start.7 = (bf16[48,512]{1,0:T(8,128)(2,1)S(1)}, bf16[48,512]{1,0:T(8,128)(2,1)S(1)}, u32[]{:S(2)}, u32[]{:S(2)}) collective-permute-start(bf16[48,512]{1,0:T(8,128)(2,1)S(1)} %get-tuple-element.40), channel_id=1, source_target_pairs={{0,1},{1,2},{2,3},{3,0},{4,5},{5,6},{6,7},{7,4},{8,9},{9,10},{10,1... | collective-permute-start | bytes 147464 | tf_op jit(solution)/shard_map/ppermute | solution.py:305
  23.5 1.7 %collective-permute-start.16 = (bf16[48,2048]{1,0:T(8,128)(2,1)S(1)}, bf16[48,2048]{1,0:T(8,128)(2,1)S(1)}, u32[]{:S(2)}, u32[]{:S(2)}) collective-permute-start(bf16[48,2048]{1,0:T(8,128)(2,1)S(1)} %unpick_saved.1.refs_0_), channel_id=1, source_target_pairs={{0,4},{4,0},{8,12},{12,8},{16,20},{20,16},{24,28},{28,24},{1,5},{5... | collective-permute-start | bytes 589832 | tf_op jit(solution)/shard_map/ppermute | solution.py:312
  25.2 3.6 %load.1.refs_4_.wd = bf16[1024,4096]{1,0:T(8,128)(2,1)S(1)} custom-call(bf16[1024,4096]{1,0:T(8,128)(2,1)} %bitcast.32, bf16[48,512]{1,0:T(8,128)(2,1)S(1)} %get-tuple-element.36.after), custom_call_target="tpu_custom_call" | custom-call | flops 3849999872 | bytes 65536 | tf_op jit(solution)/shard_map/load/pallas_call | solution.py:261
  29.1 0.4 collective-permute-start.22
  29.5 1.1 %collective-permute-start.21 = (bf16[192,2048]{1,0:T(8,128)(2,1)S(1)}, bf16[192,2048]{1,0:T(8,128)(2,1)S(1)}, u32[]{:S(2)}, u32[]{:S(2)}) collective-permute-start(bf16[192,2048]{1,0:T(8,128)(2,1)S(1)} %bitcast.37), channel_id=1, source_target_pairs={{0,3},{1,0},{2,1},{3,2},{4,7},{5,4},{6,5},{7,6},{8,11},{9,8},{10,9... | collective-permute-start | bytes 2359304 | tf_op jit(solution)/shard_map/ppermute | solution.py:297
  30.8 1.6 %collective-permute-start.12 = (bf16[48,2048]{1,0:T(8,128)(2,1)S(1)}, bf16[48,2048]{1,0:T(8,128)(2,1)S(1)}, u32[]{:S(2)}, u32[]{:S(2)}) collective-permute-start(bf16[48,2048]{1,0:T(8,128)(2,1)S(1)} %unpick_acts.1.refs_0_), channel_id=1, source_target_pairs={{0,4},{4,0},{8,12},{12,8},{16,20},{20,16},{24,28},{28,24},{1,5},{5... | collective-permute-start | bytes 589832 | tf_op jit(solution)/shard_map/ppermute | solution.py:312
  32.4 7.5 %pre.1 = (bf16[1024,4096]{1,0:T(8,128)(2,1)S(1)}, bf16[1024,4096]{1,0:T(8,128)(2,1)S(1)}, f32[1024,48]{1,0:T(8,128)S(1)}, f32[1024,48]{1,0:T(8,128)S(1)}) custom-call(bf16[48,2048]{1,0:T(8,128)(2,1)S(1)} %unpick_saved.1.refs_0_, bf16[48,2048]{1,0:T(8,128)(2,1)S(1)} %collective-permute-done.16.refs_1_, bf16[1024,4096]{1,0:T(8,128)(2,1)} %bitcast.33, ...), custom_call_target="tpu_custom_call" | custom-call | flops 6600000000 | bytes 65536 | tf_op jit(solution)/shard_map/pre/pallas_call | solution.py:261
  40.0 5.6 %backward.1 = (bf16[48,1024]{1,0:T(8,128)(2,1)S(1)}, bf16[48,1024]{1,0:T(8,128)(2,1)S(1)}, bf16[48,2048]{1,0:T(8,128)(2,1)S(1)}) custom-call(bf16[48,2048]{1,0:T(8,128)(2,1)S(1)} %unpick_gradients.1.refs_0_, bf16[48,2048]{1,0:T(8,128)(2,1)S(1)} %collective-permute-done.22.refs_1_, f32[1024,48]{1,0:T(8,128)S(1)} %get-tuple-element.59.refs_2_, ...), custom_call_target="tpu_custom_call" | custom-call | flops 4400000000 | bytes 65536 | tf_op jit(solution)/shard_map/backward/pallas_call | solution.py:261
  45.6 0.6 collective-permute-start.23
  46.2 5.2 %forward.1 = (bf16[48,1024]{1,0:T(8,128)(2,1)S(1)}, bf16[48,2048]{1,0:T(8,128)(2,1)S(1)}) custom-call(bf16[48,2048]{1,0:T(8,128)(2,1)S(1)} %unpick_acts.1.refs_0_, bf16[48,2048]{1,0:T(8,128)(2,1)S(1)} %collective-permute-done.12.refs_1_, bf16[1024,4096]{1,0:T(8,128)(2,1)S(1)} %get-tuple-element.50.refs_2_.refs_5_.wg, ...), custom_call_target="tpu_custom_call" | custom-call | flops 5500000256 | bytes 65536 | tf_op jit(solution)/shard_map/forward/pallas_call | solution.py:261
  51.4 1.6 %collective-permute-start.17 = (bf16[48,2048]{1,0:T(8,128)(2,1)S(1)}, bf16[48,2048]{1,0:T(8,128)(2,1)S(1)}, u32[]{:S(2)}, u32[]{:S(2)}) collective-permute-start(bf16[48,2048]{1,0:T(8,128)(2,1)S(1)} %get-tuple-element.53), channel_id=1, source_target_pairs={{0,4},{4,0},{8,12},{12,8},{16,20},{20,16},{24,28},{28,24},{1,5},{5... | collective-permute-start | bytes 589832 | tf_op jit(solution)/shard_map/ppermute | solution.py:312
  53.0 1.5 %backward_own.1.refs_0_ = bf16[48,2048]{1,0:T(8,128)(2,1)S(1)} custom-call(bf16[48,1024]{1,0:T(8,128)(2,1)S(1)} %get-tuple-element.61.d_gate, bf16[48,1024]{1,0:T(8,128)(2,1)S(1)} %get-tuple-element.62.d_up, bf16[1024,4096]{1,0:T(8,128)(2,1)S(1)} %get-tuple-element.50.refs_2_.refs_5_.wg, bf16[1024,4096]{1,0:T(8,128)(2,1)S(1)} %get-tuple-element.51.refs_3_.refs_6_.wu), custom_call_target="tpu_custom_call" | custom-call | flops 2200000000 | bytes 65536 | tf_op jit(solution)/shard_map/backward_own/pallas_call | solution.py:261
  54.6 0.3 fold_backward.1
  54.9 1.4 %collective-permute-start.24 = (bf16[48,512]{1,0:T(8,128)(2,1)S(1)}, bf16[48,512]{1,0:T(8,128)(2,1)S(1)}, u32[]{:S(2)}, u32[]{:S(2)}) collective-permute-start(bf16[48,512]{1,0:T(8,128)(2,1)S(1)} %get-tuple-element.65), channel_id=1, source_target_pairs={{0,8},{1,9},{2,10},{3,11},{4,12},{5,13},{6,14},{7,15},{8,0},{9,1},... | collective-permute-start | bytes 147464 | tf_op jit(solution)/shard_map/ppermute | solution.py:305
  56.4 2.5 %collective-permute-start.25 = (bf16[48,512]{1,0:T(8,128)(2,1)S(1)}, bf16[48,512]{1,0:T(8,128)(2,1)S(1)}, u32[]{:S(2)}, u32[]{:S(2)}) collective-permute-start(bf16[48,512]{1,0:T(8,128)(2,1)S(1)} %get-tuple-element.66), channel_id=1, source_target_pairs={{0,16},{1,17},{2,18},{3,19},{4,20},{5,21},{6,22},{7,23},{8,24},{9,... | collective-permute-start | bytes 147464 | tf_op jit(solution)/shard_map/ppermute | solution.py:305
  59.0 3.3 %collective-permute-start.26 = (bf16[48,512]{1,0:T(8,128)(2,1)S(1)}, bf16[48,512]{1,0:T(8,128)(2,1)S(1)}, u32[]{:S(2)}, u32[]{:S(2)}) collective-permute-start(bf16[48,512]{1,0:T(8,128)(2,1)S(1)} %get-tuple-element.67), channel_id=1, source_target_pairs={{0,24},{1,25},{2,26},{3,27},{4,28},{5,29},{6,30},{7,31},{8,16},{9,... | collective-permute-start | bytes 147464 | tf_op jit(solution)/shard_map/ppermute | solution.py:305
  62.3 0.8 %forward_own.1.refs_0_ = bf16[48,2048]{1,0:T(8,128)(2,1)S(1)} custom-call(bf16[48,1024]{1,0:T(8,128)(2,1)S(1)} %get-tuple-element.52.hidden, bf16[1024,4096]{1,0:T(8,128)(2,1)S(1)} %load.1.refs_4_.wd), custom_call_target="tpu_custom_call" | custom-call | flops 1100000000 | bytes 65536 | tf_op jit(solution)/shard_map/forward_own/pallas_call | solution.py:261
  63.2 0.4 fold_forward.1
  63.6 1.0 %collective-permute-start.19 = (bf16[48,512]{1,0:T(8,128)(2,1)S(1)}, bf16[48,512]{1,0:T(8,128)(2,1)S(1)}, u32[]{:S(2)}, u32[]{:S(2)}) collective-permute-start(bf16[48,512]{1,0:T(8,128)(2,1)S(1)} %get-tuple-element.56), channel_id=1, source_target_pairs={{0,16},{1,17},{2,18},{3,19},{4,20},{5,21},{6,22},{7,23},{8,24},{9,... | collective-permute-start | bytes 147464 | tf_op jit(solution)/shard_map/ppermute | solution.py:305
  64.9 3.7 %collective-permute-start.20 = (bf16[48,512]{1,0:T(8,128)(2,1)S(1)}, bf16[48,512]{1,0:T(8,128)(2,1)S(1)}, u32[]{:S(2)}, u32[]{:S(2)}) collective-permute-start(bf16[48,512]{1,0:T(8,128)(2,1)S(1)} %get-tuple-element.57), channel_id=1, source_target_pairs={{0,24},{1,25},{2,26},{3,27},{4,28},{5,29},{6,30},{7,31},{8,16},{9,... | collective-permute-start | bytes 147464 | tf_op jit(solution)/shard_map/ppermute | solution.py:305
  68.6 1.3 %combine_gradients.1 = bf16[192,2048]{1,0:T(8,128)(2,1)} custom-call(bf16[192,2048]{1,0:T(8,128)(2,1)S(1)} %collective-permute-done.21.refs_0_, bf16[192,192]{1,0:T(8,128)(2,1)S(1)} %get-tuple-element.35.after.refs_1_, bf16[48,512]{1,0:T(8,128)(2,1)S(1)} %get-tuple-element.64.refs_2_, bf16[48,512]{1,0:T(8,128)(2,1)S(1)} %collective-permute-done.24.refs_3_, ...), custom_call_target="tpu_custom_call" | custom-call | flops 1650000000 | bytes 65536 | tf_op jit(solution)/shard_map/combine_gradients/pallas_call | solution.py:261
  69.9 0.9 %collective-permute-done.20.refs_5_ = bf16[48,512]{1,0:T(8,128)(2,1)S(1)} collective-permute-done((bf16[48,512]{1,0:T(8,128)(2,1)S(1)}, bf16[48,512]{1,0:T(8,128)(2,1)S(1)}, u32[]{:S(2)}, u32[]{:S(2)}) %collective-permute-start.20) | collective-permute-done | bytes 49184 | tf_op jit(solution)/shard_map/ppermute | solution.py:305
  70.9 1.5 %combine_acts.1 = bf16[192,2048]{1,0:T(8,128)(2,1)} custom-call(bf16[192,2048]{1,0:T(8,128)(2,1)S(1)} %collective-permute-done.11.refs_0_, f32[192,192]{1,0:T(8,128)S(1)} %get-tuple-element.45.refs_1_, bf16[48,512]{1,0:T(8,128)(2,1)S(1)} %get-tuple-element.54.refs_2_, bf16[48,512]{1,0:T(8,128)(2,1)S(1)} %collective-permute-done.18.refs_3_, ...), custom_call_target="tpu_custom_call" | custom-call | flops 1650000000 | bytes 65536 | tf_op jit(solution)/shard_map/combine_acts/pallas_call | solution.py:261
  (41 shorter events, 1.6 us)
Async XLA Ops:
  0.6 9.7 %collective-permute-start = (s32[1,768,8]{1,2,0:T(8,128)}, s32[1,768,8]{1,2,0:T(8,128)S(1)}, u32[]{:S(2)}, u32[]{:S(2)}) collective-permute-start(s32[1,768,8]{1,2,0:T(8,128)} %param.15), channel_id=1, source_target_pairs={{0,1},{1,2},{2,3},{3,0},{4,5},{5,6},{6,7},{7,4},{8,9},{9,10},{10,1... | collective-permute-start | bytes 73736 | tf_op jit(solution)/shard_map/ppermute | solution.py:297
  1.1 9.2 %collective-permute-start.1 = (f32[1,768,8]{1,2,0:T(8,128)}, f32[1,768,8]{1,2,0:T(8,128)S(1)}, u32[]{:S(2)}, u32[]{:S(2)}) collective-permute-start(f32[1,768,8]{1,2,0:T(8,128)} %param.16), channel_id=1, source_target_pairs={{0,1},{1,2},{2,3},{3,0},{4,5},{5,6},{6,7},{7,4},{8,9},{9,10},{10,1... | collective-permute-start | bytes 73736 | tf_op jit(solution)/shard_map/ppermute | solution.py:297
  3.7 6.6 %collective-permute-start.2 = (s32[1,768,8]{1,2,0:T(8,128)}, s32[1,768,8]{1,2,0:T(8,128)S(1)}, u32[]{:S(2)}, u32[]{:S(2)}) collective-permute-start(s32[1,768,8]{1,2,0:T(8,128)} %param.13), channel_id=1, source_target_pairs={{0,3},{1,0},{2,1},{3,2},{4,7},{5,4},{6,5},{7,6},{8,11},{9,8},{10,9... | collective-permute-start | bytes 73736 | tf_op jit(solution)/shard_map/ppermute | solution.py:297
  5.9 9.0 %collective-permute-start.13 = (bf16[48,512]{1,0:T(8,128)(2,1)S(1)}, bf16[48,512]{1,0:T(8,128)(2,1)S(1)}, u32[]{:S(2)}, u32[]{:S(2)}) collective-permute-start(bf16[48,512]{1,0:T(8,128)(2,1)S(1)} %get-tuple-element.47), channel_id=1, source_target_pairs={{0,8},{1,9},{2,10},{3,11},{4,12},{5,13},{6,14},{7,15},{8,0},{9,1},... | collective-permute-start | bytes 147464 | tf_op jit(solution)/shard_map/ppermute | solution.py:305
  7.7 10.3 %collective-permute-start.14 = (bf16[48,512]{1,0:T(8,128)(2,1)S(1)}, bf16[48,512]{1,0:T(8,128)(2,1)S(1)}, u32[]{:S(2)}, u32[]{:S(2)}) collective-permute-start(bf16[48,512]{1,0:T(8,128)(2,1)S(1)} %get-tuple-element.48), channel_id=1, source_target_pairs={{0,16},{1,17},{2,18},{3,19},{4,20},{5,21},{6,22},{7,23},{8,24},{9,... | collective-permute-start | bytes 147464 | tf_op jit(solution)/shard_map/ppermute | solution.py:305
  10.3 7.7 %collective-permute-start.15 = (bf16[48,512]{1,0:T(8,128)(2,1)S(1)}, bf16[48,512]{1,0:T(8,128)(2,1)S(1)}, u32[]{:S(2)}, u32[]{:S(2)}) collective-permute-start(bf16[48,512]{1,0:T(8,128)(2,1)S(1)} %get-tuple-element.49), channel_id=1, source_target_pairs={{0,24},{1,25},{2,26},{3,27},{4,28},{5,29},{6,30},{7,31},{8,16},{9,... | collective-permute-start | bytes 147464 | tf_op jit(solution)/shard_map/ppermute | solution.py:305
  12.9 8.9 %collective-permute-start.3 = (bf16[48,512]{1,0:T(8,128)(2,1)S(1)}, bf16[48,512]{1,0:T(8,128)(2,1)S(1)}, u32[]{:S(2)}, u32[]{:S(2)}) collective-permute-start(bf16[48,512]{1,0:T(8,128)(2,1)S(1)} %get-tuple-element.36.after), channel_id=1, source_target_pairs={{0,3},{1,0},{2,1},{3,2},{4,7},{5,4},{6,5},{7,6},{8,11},{9,8},{10,9... | collective-permute-start | bytes 147464 | tf_op jit(solution)/shard_map/ppermute | solution.py:305
  12.9 10.3 %collective-permute-start.4 = (bf16[48,512]{1,0:T(8,128)(2,1)S(1)}, bf16[48,512]{1,0:T(8,128)(2,1)S(1)}, u32[]{:S(2)}, u32[]{:S(2)}) collective-permute-start(bf16[48,512]{1,0:T(8,128)(2,1)S(1)} %get-tuple-element.37), channel_id=1, source_target_pairs={{0,11},{1,8},{2,9},{3,10},{4,15},{5,12},{6,13},{7,14},{8,3},{9,0},... | collective-permute-start | bytes 147464 | tf_op jit(solution)/shard_map/ppermute | solution.py:305
  14.8 8.4 %collective-permute-start.5 = (bf16[48,512]{1,0:T(8,128)(2,1)S(1)}, bf16[48,512]{1,0:T(8,128)(2,1)S(1)}, u32[]{:S(2)}, u32[]{:S(2)}) collective-permute-start(bf16[48,512]{1,0:T(8,128)(2,1)S(1)} %get-tuple-element.38), channel_id=1, source_target_pairs={{0,19},{1,16},{2,17},{3,18},{4,23},{5,20},{6,21},{7,22},{8,27},{9,... | collective-permute-start | bytes 147464 | tf_op jit(solution)/shard_map/ppermute | solution.py:305
  18.0 5.5 %collective-permute-start.6 = (bf16[48,512]{1,0:T(8,128)(2,1)S(1)}, bf16[48,512]{1,0:T(8,128)(2,1)S(1)}, u32[]{:S(2)}, u32[]{:S(2)}) collective-permute-start(bf16[48,512]{1,0:T(8,128)(2,1)S(1)} %get-tuple-element.39), channel_id=1, source_target_pairs={{0,27},{1,24},{2,25},{3,26},{4,31},{5,28},{6,29},{7,30},{8,19},{9,... | collective-permute-start | bytes 147464 | tf_op jit(solution)/shard_map/ppermute | solution.py:305
  18.0 11.0 %collective-permute-start.10 = (bf16[48,512]{1,0:T(8,128)(2,1)S(1)}, bf16[48,512]{1,0:T(8,128)(2,1)S(1)}, u32[]{:S(2)}, u32[]{:S(2)}) collective-permute-start(bf16[48,512]{1,0:T(8,128)(2,1)S(1)} %get-tuple-element.43), channel_id=1, source_target_pairs={{0,25},{1,26},{2,27},{3,24},{4,29},{5,30},{6,31},{7,28},{8,17},{9,... | collective-permute-start | bytes 147464 | tf_op jit(solution)/shard_map/ppermute | solution.py:305
  21.8 7.7 %collective-permute-start.7 = (bf16[48,512]{1,0:T(8,128)(2,1)S(1)}, bf16[48,512]{1,0:T(8,128)(2,1)S(1)}, u32[]{:S(2)}, u32[]{:S(2)}) collective-permute-start(bf16[48,512]{1,0:T(8,128)(2,1)S(1)} %get-tuple-element.40), channel_id=1, source_target_pairs={{0,1},{1,2},{2,3},{3,0},{4,5},{5,6},{6,7},{7,4},{8,9},{9,10},{10,1... | collective-permute-start | bytes 147464 | tf_op jit(solution)/shard_map/ppermute | solution.py:305
  23.2 6.3 %collective-permute-start.8 = (bf16[48,512]{1,0:T(8,128)(2,1)S(1)}, bf16[48,512]{1,0:T(8,128)(2,1)S(1)}, u32[]{:S(2)}, u32[]{:S(2)}) collective-permute-start(bf16[48,512]{1,0:T(8,128)(2,1)S(1)} %get-tuple-element.41), channel_id=1, source_target_pairs={{0,9},{1,10},{2,11},{3,8},{4,13},{5,14},{6,15},{7,12},{8,1},{9,2},... | collective-permute-start | bytes 147464 | tf_op jit(solution)/shard_map/ppermute | solution.py:305
  23.2 6.3 %collective-permute-start.9 = (bf16[48,512]{1,0:T(8,128)(2,1)S(1)}, bf16[48,512]{1,0:T(8,128)(2,1)S(1)}, u32[]{:S(2)}, u32[]{:S(2)}) collective-permute-start(bf16[48,512]{1,0:T(8,128)(2,1)S(1)} %get-tuple-element.42), channel_id=1, source_target_pairs={{0,17},{1,18},{2,19},{3,16},{4,21},{5,22},{6,23},{7,20},{8,25},{9,... | collective-permute-start | bytes 147464 | tf_op jit(solution)/shard_map/ppermute | solution.py:305
  23.5 8.9 %collective-permute-start.16 = (bf16[48,2048]{1,0:T(8,128)(2,1)S(1)}, bf16[48,2048]{1,0:T(8,128)(2,1)S(1)}, u32[]{:S(2)}, u32[]{:S(2)}) collective-permute-start(bf16[48,2048]{1,0:T(8,128)(2,1)S(1)} %unpick_saved.1.refs_0_), channel_id=1, source_target_pairs={{0,4},{4,0},{8,12},{12,8},{16,20},{20,16},{24,28},{28,24},{1,5},{5... | collective-permute-start | bytes 589832 | tf_op jit(solution)/shard_map/ppermute | solution.py:312
  25.2 4.3 %copy-start = (bf16[1,192,2048]{2,1,0:T(8,128)(2,1)S(1)}, bf16[1,192,2048]{2,1,0:T(8,128)(2,1)}, u32[]{:S(2)}) copy-start(bf16[1,192,2048]{2,1,0:T(8,128)(2,1)} %param.11) | copy-start | bytes 2359300
  25.2 7.2 %copy-start.1 = (bf16[1,192,2048]{2,1,0:T(8,128)(2,1)S(1)}, bf16[1,192,2048]{2,1,0:T(8,128)(2,1)}, u32[]{:S(2)}) copy-start(bf16[1,192,2048]{2,1,0:T(8,128)(2,1)} %param.10) | copy-start | bytes 2359300
  29.1 10.9 %collective-permute-start.22 = (bf16[48,2048]{1,0:T(8,128)(2,1)S(1)}, bf16[48,2048]{1,0:T(8,128)(2,1)S(1)}, u32[]{:S(2)}, u32[]{:S(2)}) collective-permute-start(bf16[48,2048]{1,0:T(8,128)(2,1)S(1)} %unpick_gradients.1.refs_0_), channel_id=1, source_target_pairs={{0,4},{4,0},{8,12},{12,8},{16,20},{20,16},{24,28},{28,24},{1,5},{5... | collective-permute-start | bytes 589832 | tf_op jit(solution)/shard_map/ppermute | solution.py:312
  29.5 39.1 %collective-permute-start.21 = (bf16[192,2048]{1,0:T(8,128)(2,1)S(1)}, bf16[192,2048]{1,0:T(8,128)(2,1)S(1)}, u32[]{:S(2)}, u32[]{:S(2)}) collective-permute-start(bf16[192,2048]{1,0:T(8,128)(2,1)S(1)} %bitcast.37), channel_id=1, source_target_pairs={{0,3},{1,0},{2,1},{3,2},{4,7},{5,4},{6,5},{7,6},{8,11},{9,8},{10,9... | collective-permute-start | bytes 2359304 | tf_op jit(solution)/shard_map/ppermute | solution.py:297
  30.8 15.3 %collective-permute-start.12 = (bf16[48,2048]{1,0:T(8,128)(2,1)S(1)}, bf16[48,2048]{1,0:T(8,128)(2,1)S(1)}, u32[]{:S(2)}, u32[]{:S(2)}) collective-permute-start(bf16[48,2048]{1,0:T(8,128)(2,1)S(1)} %unpick_acts.1.refs_0_), channel_id=1, source_target_pairs={{0,4},{4,0},{8,12},{12,8},{16,20},{20,16},{24,28},{28,24},{1,5},{5... | collective-permute-start | bytes 589832 | tf_op jit(solution)/shard_map/ppermute | solution.py:312
  32.4 38.4 %collective-permute-start.11 = (bf16[192,2048]{1,0:T(8,128)(2,1)S(1)}, bf16[192,2048]{1,0:T(8,128)(2,1)S(1)}, u32[]{:S(2)}, u32[]{:S(2)}) collective-permute-start(bf16[192,2048]{1,0:T(8,128)(2,1)S(1)} %bitcast.39), channel_id=1, source_target_pairs={{0,1},{1,2},{2,3},{3,0},{4,5},{5,6},{6,7},{7,4},{8,9},{9,10},{10,1... | collective-permute-start | bytes 2359304 | tf_op jit(solution)/shard_map/ppermute | solution.py:297
  45.6 9.0 %collective-permute-start.23 = (bf16[48,2048]{1,0:T(8,128)(2,1)S(1)}, bf16[48,2048]{1,0:T(8,128)(2,1)S(1)}, u32[]{:S(2)}, u32[]{:S(2)}) collective-permute-start(bf16[48,2048]{1,0:T(8,128)(2,1)S(1)} %get-tuple-element.63), channel_id=1, source_target_pairs={{0,4},{4,0},{8,12},{12,8},{16,20},{20,16},{24,28},{28,24},{1,5},{5... | collective-permute-start | bytes 589832 | tf_op jit(solution)/shard_map/ppermute | solution.py:312
  51.4 7.6 %collective-permute-start.17 = (bf16[48,2048]{1,0:T(8,128)(2,1)S(1)}, bf16[48,2048]{1,0:T(8,128)(2,1)S(1)}, u32[]{:S(2)}, u32[]{:S(2)}) collective-permute-start(bf16[48,2048]{1,0:T(8,128)(2,1)S(1)} %get-tuple-element.53), channel_id=1, source_target_pairs={{0,4},{4,0},{8,12},{12,8},{16,20},{20,16},{24,28},{28,24},{1,5},{5... | collective-permute-start | bytes 589832 | tf_op jit(solution)/shard_map/ppermute | solution.py:312
  54.9 8.6 %collective-permute-start.24 = (bf16[48,512]{1,0:T(8,128)(2,1)S(1)}, bf16[48,512]{1,0:T(8,128)(2,1)S(1)}, u32[]{:S(2)}, u32[]{:S(2)}) collective-permute-start(bf16[48,512]{1,0:T(8,128)(2,1)S(1)} %get-tuple-element.65), channel_id=1, source_target_pairs={{0,8},{1,9},{2,10},{3,11},{4,12},{5,13},{6,14},{7,15},{8,0},{9,1},... | collective-permute-start | bytes 147464 | tf_op jit(solution)/shard_map/ppermute | solution.py:305
  56.4 7.2 %collective-permute-start.25 = (bf16[48,512]{1,0:T(8,128)(2,1)S(1)}, bf16[48,512]{1,0:T(8,128)(2,1)S(1)}, u32[]{:S(2)}, u32[]{:S(2)}) collective-permute-start(bf16[48,512]{1,0:T(8,128)(2,1)S(1)} %get-tuple-element.66), channel_id=1, source_target_pairs={{0,16},{1,17},{2,18},{3,19},{4,20},{5,21},{6,22},{7,23},{8,24},{9,... | collective-permute-start | bytes 147464 | tf_op jit(solution)/shard_map/ppermute | solution.py:305
  59.0 5.9 %collective-permute-start.26 = (bf16[48,512]{1,0:T(8,128)(2,1)S(1)}, bf16[48,512]{1,0:T(8,128)(2,1)S(1)}, u32[]{:S(2)}, u32[]{:S(2)}) collective-permute-start(bf16[48,512]{1,0:T(8,128)(2,1)S(1)} %get-tuple-element.67), channel_id=1, source_target_pairs={{0,24},{1,25},{2,26},{3,27},{4,28},{5,29},{6,30},{7,31},{8,16},{9,... | collective-permute-start | bytes 147464 | tf_op jit(solution)/shard_map/ppermute | solution.py:305
  63.5 6.4 %collective-permute-start.18 = (bf16[48,512]{1,0:T(8,128)(2,1)S(1)}, bf16[48,512]{1,0:T(8,128)(2,1)S(1)}, u32[]{:S(2)}, u32[]{:S(2)}) collective-permute-start(bf16[48,512]{1,0:T(8,128)(2,1)S(1)} %get-tuple-element.55), channel_id=1, source_target_pairs={{0,8},{1,9},{2,10},{3,11},{4,12},{5,13},{6,14},{7,15},{8,0},{9,1},... | collective-permute-start | bytes 147464 | tf_op jit(solution)/shard_map/ppermute | solution.py:305
  63.6 6.3 %collective-permute-start.19 = (bf16[48,512]{1,0:T(8,128)(2,1)S(1)}, bf16[48,512]{1,0:T(8,128)(2,1)S(1)}, u32[]{:S(2)}, u32[]{:S(2)}) collective-permute-start(bf16[48,512]{1,0:T(8,128)(2,1)S(1)} %get-tuple-element.56), channel_id=1, source_target_pairs={{0,16},{1,17},{2,18},{3,19},{4,20},{5,21},{6,22},{7,23},{8,24},{9,... | collective-permute-start | bytes 147464 | tf_op jit(solution)/shard_map/ppermute | solution.py:305
  64.9 5.9 %collective-permute-start.20 = (bf16[48,512]{1,0:T(8,128)(2,1)S(1)}, bf16[48,512]{1,0:T(8,128)(2,1)S(1)}, u32[]{:S(2)}, u32[]{:S(2)}) collective-permute-start(bf16[48,512]{1,0:T(8,128)(2,1)S(1)} %get-tuple-element.57), channel_id=1, source_target_pairs={{0,24},{1,25},{2,26},{3,27},{4,28},{5,29},{6,30},{7,31},{8,16},{9,... | collective-permute-start | bytes 147464 | tf_op jit(solution)/shard_map/ppermute | solution.py:305

commit v2 on v1

v2 whole, which is shorter than its diff:
```python
import functools
import jax
import jax.numpy as jnp
from jax import lax
from jax.experimental import pallas as pl
from jax.experimental.pallas import tpu as pltpu
from jax.sharding import PartitionSpec as P

N_ROUTED = 256
TOP = 8
E_WIN = 4
F32 = jnp.float32
BF16 = jnp.bfloat16
VMEM_LIMIT = 8 << 20


def mm(a, b, ca=1, cb=0, precision=None):
    dims = (((ca,), (cb,)), ((), ()))
    return lax.dot_general(a, b, dims, precision=precision, preferred_element_type=F32)


class Sizes:
    def __init__(self, count, width, hidden, split):
        self.count, self.width, self.hidden, self.split = count, width, hidden, split
        self.cap = count * TOP * 2 // N_ROUTED
        self.slots = E_WIN * self.cap
        self.parts = min(4, width // 128)
        self.cols = width // self.parts
        self.piece = self.parts * self.cap
        self.spread = E_WIN * self.piece


def place_of(sz, i):
    piece = sum([(i >= sz.piece * n).astype(jnp.int32) for n in range(1, E_WIN)])
    i = i - sz.piece * piece
    part = sum([(i >= sz.cap * n).astype(jnp.int32) for n in range(1, sz.parts)])
    return piece, part, i - sz.cap * part


def one_hot(mask):
    return jnp.where(mask, 1.0, 0.0).astype(BF16)


def route_masks(routes, probs, expert, place, earlier):
    chosen = jnp.zeros(expert.shape, F32)
    weight = jnp.zeros(expert.shape, F32)
    for c in range(TOP):
        hit = routes[c : c + 1, :] == expert
        chosen += jnp.where(hit, 1.0, 0.0)
        if probs is not None:
            weight += jnp.where(hit, probs[c : c + 1, :], 0.0)
    before = mm(chosen.astype(BF16), earlier)
    mask = (chosen > 0.5) & (jnp.abs(before - place.astype(F32)) < 0.5)
    return mask, weight


def my_group(ref, group, count):
    block = ref[:, :count]
    for n in range(1, E_WIN):
        block = jnp.where(group == n, ref[:, n * count : (n + 1) * count], block)
    return block


def earlier_tokens(sz):
    shape = (sz.count, sz.count)
    return one_hot(lax.broadcasted_iota(jnp.int32, shape, 0) < lax.broadcasted_iota(jnp.int32, shape, 1))


def piece_masks(sz, routes_ref, probs_ref):
    group = lax.axis_index("expert") // sz.split
    shape = (sz.spread, sz.count)
    piece, part, place = place_of(sz, lax.broadcasted_iota(jnp.int32, shape, 0))
    routes = my_group(routes_ref, group, sz.count)
    probs = None if probs_ref is None else my_group(probs_ref, group, sz.count)
    mask, weight = route_masks(routes, probs, piece ^ group, place, earlier_tokens(sz))
    return mask, weight, part


def pick(sz, mask, part, values):
    picked = jnp.zeros((sz.spread, sz.cols), F32)
    for q in range(sz.parts):
        picked += mm(one_hot(mask & (part == q)), values[:, q * sz.cols : (q + 1) * sz.cols])
    return picked


def put_pieces(values, outs):
    step = values.shape[0] // len(outs)
    for n, out in enumerate(outs):
        out[...] = values[n * step : (n + 1) * step].astype(BF16)


def fetch(pairs, sems):
    copies = [pltpu.make_async_copy(src, dst, sems.at[n]) for n, (src, dst) in enumerate(pairs)]
    for c in copies:
        c.start()
    return copies


def local_kernel(sz, fr, fp, br, bp, saved, w_f, m_f, m_b, scale, *rest):
    pieces, (fr_v, fp_v, br_v, bp_v, saved_v, sems) = rest[:E_WIN], rest[E_WIN:]
    pairs = [(br, br_v), (bp, bp_v), (fr, fr_v), (fp, fp_v), (saved, saved_v)]
    copies = fetch(pairs, sems)
    for c in copies[:4]:
        c.wait()
    mask, weight, part = piece_masks(sz, br_v, bp_v)
    m_b[...] = one_hot(mask)
    total = jnp.sum(jnp.where(mask, weight, 0.0), axis=1, keepdims=True)
    scale[...] = jnp.broadcast_to(total, scale.shape)
    copies[4].wait()
    put_pieces(pick(sz, mask, part, saved_v), pieces)
    mask, weight, _ = piece_masks(sz, fr_v, fp_v)
    m_f[...] = one_hot(mask)
    w_f[...] = jnp.where(mask, weight, 0.0)


def pick_again_kernel(sz, scaled, chosen, *refs):
    values, pieces = refs[scaled], refs[scaled + 1 :]
    _, part, _ = place_of(sz, lax.broadcasted_iota(jnp.int32, (sz.spread, sz.count), 0))
    picked = pick(sz, chosen[...].astype(F32) > 0.5, part, values)
    put_pieces(picked * refs[0][:, 0:1] if scaled else picked, pieces)


def end_to_end(pieces):
    return jnp.concatenate([p[...] for p in (pieces[0], *pieces[:0:-1])], axis=0)


def unpick(sz, cat, rows):
    shape = (sz.slots, sz.spread)
    slot = lax.broadcasted_iota(jnp.int32, shape, 0)
    piece, part, place = place_of(sz, lax.broadcasted_iota(jnp.int32, shape, 1))
    here = slot == piece * sz.cap + place
    for q in range(sz.parts):
        rows[:, q * sz.cols : (q + 1) * sz.cols] = mm(one_hot(here & (part == q)), cat).astype(BF16)


def unpick_kernel(sz, *refs):
    unpick(sz, end_to_end(refs[:-1]), refs[-1])


def fold_kernel(sz, *refs):
    slices, pieces = refs[: sz.split], refs[sz.split :]
    rows = slices[0][...].astype(F32)
    for s in slices[1:]:
        rows += s[...].astype(F32)
    rows = rows.astype(BF16)
    shape = (sz.spread, sz.slots)
    piece, part, place = place_of(sz, lax.broadcasted_iota(jnp.int32, shape, 0))
    here = lax.broadcasted_iota(jnp.int32, shape, 1) == piece * sz.cap + place
    out = jnp.zeros((sz.spread, sz.cols), F32)
    for q in range(sz.parts):
        out += mm(one_hot(here & (part == q)), rows[:, q * sz.cols : (q + 1) * sz.cols])
    put_pieces(out, pieces)


def combine_kernel(sz, copies, values, w, *refs):
    pieces, (out, done, sems) = refs[:E_WIN], refs[E_WIN:]
    cat = end_to_end(pieces)
    stores = []
    for q in range(sz.parts):
        columns = pl.ds(q * sz.cols, sz.cols)
        total = values[:, columns].astype(F32)
        for n in range(copies):
            total += mm(w[q * copies + n], cat)
        done[:, columns] = total.astype(BF16)
        stores.append(pltpu.make_async_copy(done.at[:, columns], out.at[:, columns], sems.at[q]))
        stores[-1].start()
    for store in stores:
        store.wait()


def lay_rows(sz, slices, rows):
    me = lax.rem(lax.axis_index("expert"), sz.split)
    for j, s in enumerate(slices):
        at = lax.rem(me + sz.split - j, sz.split) * sz.width
        rows[:, pl.ds(pl.multiple_of(at, 128), sz.width)] = s[...]


def load_kernel(sz, w_f, w_b, wg, wu, wg_near, wu_near, f_turned, b_turned, sems):
    copies = fetch([(wg, wg_near), (wu.at[: wu_near.shape[0]], wu_near)], sems)
    _, part, _ = place_of(sz, lax.broadcasted_iota(jnp.int32, (sz.count, sz.spread), 1))
    f = w_f[...].T
    b = w_b[...].astype(F32).T
    for q in range(sz.parts):
        mine = jnp.where(part == q, f, 0.0)
        high = mine.astype(BF16)
        f_turned[2 * q] = high
        f_turned[2 * q + 1] = (mine - high.astype(F32)).astype(BF16)
        b_turned[q] = jnp.where(part == q, b, 0.0).astype(BF16)
    for c in copies:
        c.wait()


def load_one_kernel(weight, held, sems):
    half = weight.shape[0] // 2
    for c in fetch([(weight.at[cut], held.at[cut]) for cut in (pl.ds(0, half), pl.ds(half, half))], sems):
        c.wait()


def by_halves(weight, turned, out):
    half = weight.shape[0] // 2
    for cut in (slice(0, half), slice(half, None)):
        out[cut, :] = mm(weight[cut, :], turned[...])


def first_kernel(sz, *refs):
    n, m, half = sz.split, sz.slots, sz.hidden // 2
    b_slices, x_slices, (wg, wu_0, wu, wd), refs = refs[:n], refs[n : 2 * n], refs[2 * n : 2 * n + 4], refs[2 * n + 4 :]
    wu_1, gate, up, hidden, *outs = refs[:-5]
    rows, turned, gate_all, up_all, sems = refs[-5:]
    (copy,) = fetch([(wu.at[half:], wu_1)], sems)
    lay_rows(sz, b_slices, rows)
    turned[:, :m] = rows[...].T
    lay_rows(sz, x_slices, rows)
    turned[:, m:] = rows[...].T
    by_halves(wg, turned, gate_all)
    up_all[:half, :] = mm(wu_0[...], turned[...])

    @pl.when(lax.axis_index("expert") >= 0)
    def _():
        copy.wait()
        up_all[half:, :] = mm(wu_1[...], turned[...])

    g = gate_all[:, m:]
    hidden[...] = (g * jax.nn.sigmoid(g) * up_all[:, m:]).T.astype(BF16)
    gate[...] = gate_all[:, :m]
    up[...] = up_all[:, :m]
    forward_slices(sz, range(1, n), hidden, wd, outs)


def columns_of(sz, j):
    me = lax.rem(lax.axis_index("expert"), sz.split)
    at = lax.rem(me + j, sz.split) * sz.width
    block = min(512, sz.width)
    return [
        (pl.ds(n * block, block), pl.ds(pl.multiple_of(at + n * block, 128), block))
        for n in range(sz.width // block)
    ]


def backward_slices(sz, js, d_gate, d_up, wg, wu_0, wu_1, outs):
    half = wu_0.shape[0]
    for j, out in zip(js, outs):
        for here, there in columns_of(sz, j):
            total = mm(d_gate[...], wg[:, there]) + mm(d_up[:, :half], wu_0[:, there]) + mm(d_up[:, half:], wu_1[:, there])
            out[:, here] = total.astype(BF16)


def forward_slices(sz, js, hidden, wd, outs):
    for j, out in zip(js, outs):
        for here, there in columns_of(sz, j):
            out[:, here] = mm(hidden[...], wd[:, there]).astype(BF16)


def backward_kernel(sz, *refs):
    n = sz.split
    slices, (gate, up, wg, wu_0, wu_1, wd), refs = refs[:n], refs[n : n + 6], refs[n + 6 :]
    d_gate, d_up, *outs = refs[:-3]
    rows, turned, dh = refs[-3:]
    lay_rows(sz, slices, rows)
    turned[...] = rows[...].T
    by_halves(wd, turned, dh)
    dh = dh[...]
    g = gate[...]
    sig = jax.nn.sigmoid(g)
    d_up[...] = (dh * (g * sig)).T.astype(BF16)
    d_gate[...] = (dh * up[...] * sig * (1.0 + g * (1.0 - sig))).T.astype(BF16)
    backward_slices(sz, range(1, n), d_gate, d_up, wg, wu_0, wu_1, outs)


def backward_own_kernel(sz, d_gate, d_up, wg, wu_0, wu_1, out):
    backward_slices(sz, (0,), d_gate, d_up, wg, wu_0, wu_1, (out,))


def forward_own_kernel(sz, hidden, wd, out):
    forward_slices(sz, (0,), hidden, wd, (out,))


def near(kernel, outs, args, name, us=0.3, far=(), scratch=(), after=(), far_outs=False):
    spaces = [pltpu.HBM if i in far else pltpu.VMEM for i in range(len(args))] + [pl.ANY] * len(after)
    args = [pltpu.with_memory_space_constraint(a, pltpu.HBM) if i in far else a for i, a in enumerate(args)]

    def body(*refs):
        kernel(*refs[: len(args)], *refs[len(args) + len(after) :])

    return pl.pallas_call(
        body,
        out_shape=[jax.ShapeDtypeStruct(s, d) for s, d in outs],
        name=name,
        in_specs=[pl.BlockSpec(memory_space=s) for s in spaces],
        out_specs=[pl.BlockSpec(memory_space=pltpu.HBM if far_outs else pltpu.VMEM) for _ in outs],
        scratch_shapes=list(scratch),
        compiler_params=pltpu.CompilerParams(vmem_limit_bytes=VMEM_LIMIT),
        cost_estimate=pl.CostEstimate(flops=int(us * 1.1e9), bytes_accessed=1 << 16, transcendentals=0),
    )(*args, *after)


def shards(
    section_acts,
    section_input_gradients,
    saved_input,
    fwd_routes,
    fwd_probs,
    back_routes,
    back_probs,
    w_gate,
    w_up,
    w_down,
):
    experts = lax.axis_size("expert")
    sections = lax.axis_size("section")
    split = experts // E_WIN
    acts, grads, saved = section_acts[0], section_input_gradients[0], saved_input[0]
    wg, wu, wd = w_gate[0], w_up[0], w_down[0]
    count, width = acts.shape
    sz = Sizes(count, width, wg.shape[0], split)
    full = width * split
    piece = ((sz.piece, sz.cols), BF16)
    rows = ((sz.slots, width), BF16)

    def by_section(x, by):
        return lax.ppermute(x, "section", [(i, (i + by) % sections) for i in range(sections)])

    def exchange(pieces):
        pairs = lambda o: [(e, (e // split ^ o) * split + e % split) for e in range(experts)]
        return [pieces[0]] + [lax.ppermute(pieces[o], "expert", pairs(o)) for o in range(E_WIN - 1, 0, -1)]

    def along_group(x, by):
        pairs = [(e, e // split * split + (e + by) % split) for e in range(experts)]
        return lax.ppermute(x, "expert", pairs)

    def gather(x):
        return [x] + [along_group(x, j) for j in range(1, split)]

    def scatter(slices):
        return tuple(along_group(s, j) for j, s in enumerate(slices, 1))

    part = functools.partial
    pieces = [piece] * E_WIN
    block = ((count, width), BF16)
    held = ((sz.spread, sz.cols), BF16)
    route_scratch = [pltpu.VMEM(fwd_routes.shape[:0:-1], d) for d in (jnp.int32, F32)]
    block_scratch = pltpu.VMEM((count, width), BF16)
    rows_scratch = pltpu.VMEM((sz.slots, full), BF16)

    fr, fp, br, bp = fwd_routes[0].T, fwd_probs[0].T, back_routes[0].T, back_probs[0].T
    x_full = by_section(acts, 1)
    half_weight = ((sz.hidden // 2, full), BF16)
    table = (sz.spread, count)
    w_f, m_f, m_b, scale, *b_out = near(
        part(local_kernel, sz),
        [(table, F32), (table, BF16), (table, BF16), ((sz.spread, 128), F32)] + pieces,
        (fr, fp, br, bp, saved),
        "local",
        2.0,
        far=range(5),
        scratch=route_scratch * 2 + [block_scratch, pltpu.SemaphoreType.DMA((5,))],
    )
    b_in = exchange(b_out)
    grads, m_b = lax.optimization_barrier((grads, m_b))
    dy_full = by_section(grads, -1)
    wg_near, wu_0, f_turned, b_turned = near(
        part(load_kernel, sz),
        [(wg.shape, BF16), half_weight] + [((n * sz.parts, count, sz.spread), BF16) for n in (2, 1)],
        (w_f, m_b, wg, wu),
        "load",
        4.0,
        far=(2, 3),
        scratch=[pltpu.SemaphoreType.DMA((2,))],
    )
    unpicked = lambda pieces, name, after=(): near(part(unpick_kernel, sz), [rows], pieces, name, after=after)[0]
    b_near = unpicked(b_in, "unpick_saved", (f_turned,))
    x_out = near(part(pick_again_kernel, sz, 0), pieces, (m_f, x_full), "pick_acts", 0.5, after=(b_near,))
    x_in = exchange(x_out)
    g_out = near(
        part(pick_again_kernel, sz, 1), pieces, (m_b, scale, dy_full), "pick_gradients", 0.5, after=x_out[:1]
    )
    x_near = unpicked(x_in, "unpick_acts", g_out[:1])
    wd_near = near(
        load_one_kernel, [(wd.shape, BF16)], (wd,), "load_down", 3.0, far=(0,), scratch=[pltpu.SemaphoreType.DMA((2,))], after=(x_near,)
    )[0]
    g_in = exchange(g_out)
    g_near = unpicked(g_in, "unpick_gradients", (wd_near,))
    b_rows, x_rows, g_rows = gather(b_near), gather(x_near), gather(g_near)

    hidden_f32 = ((sz.hidden, sz.slots), F32)
    hidden_bf16 = ((sz.slots, sz.hidden), BF16)
    both = pltpu.VMEM((sz.hidden, 2 * sz.slots), F32)
    wu_1, gate, up, hidden, *made = near(
        part(first_kernel, sz),
        [half_weight] + [hidden_f32] * 2 + [hidden_bf16] + [rows] * (split - 1),
        (*b_rows, *x_rows, wg_near, wu_0, wu, wd_near),
        "first",
        6.0,
        far=(2 * split + 2,),
        scratch=[rows_scratch, pltpu.VMEM((full, 2 * sz.slots), BF16), both, both, pltpu.SemaphoreType.DMA((1,))],
        after=(g_near,),
    )
    made_in = scatter(made)
    up_weights = (wg_near, wu_0, wu_1)
    d_gate, d_up, *back = near(
        part(backward_kernel, sz),
        [hidden_bf16] * 2 + [rows] * (split - 1),
        (*g_rows, gate, up, *up_weights, wd_near),
        "backward",
        4.0,
        scratch=[rows_scratch, pltpu.VMEM((full, sz.slots), BF16), pltpu.VMEM((sz.hidden, sz.slots), F32)],
    )
    back_in = scatter(back)
    made_own = near(part(forward_own_kernel, sz), [rows], (hidden, wd_near), "forward_own", 1.0, after=(d_gate,))
    made_pieces = near(part(fold_kernel, sz), pieces, (*made_own, *made_in), "fold_forward")
    back_own = near(
        part(backward_own_kernel, sz), [rows], (d_gate, d_up, *up_weights), "backward_own", 1.5, after=made_pieces[:1]
    )
    made_pieces = exchange(made_pieces)
    back_pieces = exchange(near(part(fold_kernel, sz), pieces, (*back_own, *back_in), "fold_backward"))

    combine = lambda copies, args, name, after: near(
        part(combine_kernel, sz, copies),
        [block],
        args,
        name,
        1.2,
        scratch=[block_scratch, pltpu.SemaphoreType.DMA((sz.parts,))],
        after=after,
        far_outs=True,
    )[0]
    section_out = combine(2, (x_full, f_turned, *made_pieces), "combine_acts", back_pieces[:1])
    input_grads = combine(1, (dy_full, b_turned, *back_pieces), "combine_gradients", ())
    return (section_out[None], input_grads[None])


def solution(mesh):
    return jax.shard_map(
        shards,
        mesh=mesh,
        in_specs=(
            P("section", "expert", None),
            P("section", "expert", None),
            P("section", "expert", None),
            P("section", None, None),
            P("section", None, None),
            P("section", None, None),
            P("section", None, None),
            P("section", "expert", None),
            P("section", "expert", None),
            P("section", "expert", None),
        ),
        out_specs=(P("section", "expert", None), P("section", "expert", None)),
        check_vma=False,
    )
```

time: 72.5 us -> 65.3 us (0.901); the launches traced: 72.4 us -> 64.2 us
  Pallas kernels: 33.1 us -> 27.8 us
  starting transfers between devices: 37 us -> 33.3 us
    pallas_call x15 -> x16, Pallas kernels: 33.1 us -> 27.8 us  [near(): pl.pallas_call(body, out_shape=[jax.ShapeDtypeStruct(s, d) for s, d in ou...]
    ppermute x17 -> x15, starting transfers between devices: 26.9 us -> 24.5 us  [exchange(): lax.ppermute(pieces[o], 'expert', pairs(o))]
    ppermute x5 -> x2, starting transfers between devices: 4.21 us -> 2.5 us  [by_section(): lax.ppermute(x, 'section', [(i, (i + by) % sections) for i in range(secti...]
    ppermute x17 -> x15, waiting for transfers between devices: 1.25 us -> 2.05 us  [exchange(): lax.ppermute(pieces[o], 'expert', pairs(o))]
  transfers between devices with their start and end apart: 27 -> 22, of which waited for: 3 -> 3; matrix products, arithmetic and copies ran while one was open for 0% -> 0% of each run, Pallas kernels for 44% -> 42%
where the time goes in v2:
time: 65.3 us; the launch traced here: 64.2 us
  starting transfers between devices  33.3 us (51%)
  Pallas kernels  27.8 us (43%)
  waiting for transfers between devices  2.07 us (3%)
  between operations  1.01 us (2%)
    pallas_call x16, Pallas kernels, near(): pl.pallas_call(body, out_shape=[jax.ShapeDtypeStruct(s, d) for s, d in ou...  27.8 us
    ppermute x15, starting transfers between devices, exchange(): lax.ppermute(pieces[o], 'expert', pairs(o))  24.5 us
    ppermute x5, starting transfers between devices, along_group(): return lax.ppermute(x, 'expert', pairs)  6.27 us
    ppermute x2, starting transfers between devices, by_section(): lax.ppermute(x, 'section', [(i, (i + by) % sections) for i in range(secti...  2.5 us
    ppermute x15, waiting for transfers between devices, exchange(): lax.ppermute(pieces[o], 'expert', pairs(o))  2.05 us
  transfers between devices with their start and end apart: 22, of which 3 were waited for; matrix products, arithmetic and copies ran while one was open for 0% of the time, Pallas kernels for 42%

profile of v2, /device:TPU:0, one launch (start us, length us, event | category | flops | bytes accessed | tf_op | source)
XLA Modules:
  0.0 64.2 jit_solution(1370863801545449534)
XLA Ops:
  0.6 0.5 collective-permute-start
  1.1 2.2 %local.1 = (f32[192,192]{1,0:T(8,128)S(1)}, bf16[192,192]{1,0:T(8,128)(2,1)S(1)}, bf16[192,192]{1,0:T(8,128)(2,1)S(1)}, f32[192,128]{1,0:T(8,128)S(1)}, bf16[48,...) custom-call(s32[8,768]{1,0:T(8,128)} %bitcast.27, ...), custom_call_target="tpu_custom_call" | custom-call | flops 2200000000 | bytes 65536 | tf_op jit(solution)/shard_map/local/pallas_call | solution.py:285
  3.4 2.0 %collective-permute-start.8 = (bf16[192,2048]{1,0:T(8,128)(2,1)}, bf16[192,2048]{1,0:T(8,128)(2,1)S(1)}, u32[]{:S(2)}, u32[]{:S(2)}) collective-permute-start(bf16[192,2048]{1,0:T(8,128)(2,1)} %bitcast.26), channel_id=1, source_target_pairs={{0,3},{1,0},{2,1},{3,2},{4,7},{5,4},{6,5},{7,6},{8,11},{9,8},{10,9... | collective-permute-start | bytes 2359304 | tf_op jit(solution)/shard_map/ppermute | solution.py:321
  5.4 4.4 %collective-permute-start.1 = (bf16[48,512]{1,0:T(8,128)(2,1)S(1)}, bf16[48,512]{1,0:T(8,128)(2,1)S(1)}, u32[]{:S(2)}, u32[]{:S(2)}) collective-permute-start(bf16[48,512]{1,0:T(8,128)(2,1)S(1)} %get-tuple-element.45), channel_id=1, source_target_pairs={{0,24},{4,28},{8,16},{12,20},{16,8},{20,12},{24,0},{28,4},{1,25},{... | collective-permute-start | bytes 147464 | tf_op jit(solution)/shard_map/ppermute | solution.py:325
  9.8 0.6 collective-permute-start.3
  10.3 4.6 %load.1 = (bf16[1024,4096]{1,0:T(8,128)(2,1)S(1)}, bf16[512,4096]{1,0:T(8,128)(2,1)S(1)}, bf16[8,192,192]{2,1,0:T(8,128)(2,1)S(1)}, bf16[4,192,192]{2,1,0:T(8,128)(2,1)S(1)}) custom-call(f32[192,192]{1,0:T(8,128)S(1)} %get-tuple-element.40.refs_0_, bf16[192,192]{1,0:T(8,128)(2,1)S(1)} %get-tuple-element.42.refs_1_.refs_0_, bf16[1024,4096]{1,0:T(8,128)(2,1)} %bitcast.22, ...), custom_call_target="tpu_custom_call" | custom-call | flops 4400000000 | bytes 65536 | tf_op jit(solution)/shard_map/load/pallas_call | solution.py:285
  15.2 1.8 %collective-permute-start.4 = (bf16[48,2048]{1,0:T(8,128)(2,1)S(1)}, bf16[48,2048]{1,0:T(8,128)(2,1)S(1)}, u32[]{:S(2)}, u32[]{:S(2)}) collective-permute-start(bf16[48,2048]{1,0:T(8,128)(2,1)S(1)} %unpick_saved.1.refs_2_.refs_0_), channel_id=1, source_target_pairs={{0,4},{4,0},{8,12},{12,8},{16,20},{20,16},{24,28},{28,24},{1,5},{5... | collective-permute-start | bytes 589832 | tf_op jit(solution)/shard_map/ppermute | solution.py:329
  17.0 0.4 pick_acts.1
  17.4 4.7 %collective-permute-start.5 = (bf16[48,512]{1,0:T(8,128)(2,1)S(1)}, bf16[48,512]{1,0:T(8,128)(2,1)S(1)}, u32[]{:S(2)}, u32[]{:S(2)}) collective-permute-start(bf16[48,512]{1,0:T(8,128)(2,1)S(1)} %get-tuple-element.50), channel_id=1, source_target_pairs={{0,24},{4,28},{8,16},{12,20},{16,8},{20,12},{24,0},{28,4},{1,25},{... | collective-permute-start | bytes 147464 | tf_op jit(solution)/shard_map/ppermute | solution.py:325
  22.1 0.6 collective-permute-start.7
  22.7 0.4 pick_gradients.1
  23.1 3.8 %collective-permute-start.10 = (bf16[48,512]{1,0:T(8,128)(2,1)S(1)}, bf16[48,512]{1,0:T(8,128)(2,1)S(1)}, u32[]{:S(2)}, u32[]{:S(2)}) collective-permute-start(bf16[48,512]{1,0:T(8,128)(2,1)S(1)} %get-tuple-element.58), channel_id=1, source_target_pairs={{0,24},{4,28},{8,16},{12,20},{16,8},{20,12},{24,0},{28,4},{1,25},{... | collective-permute-start | bytes 147464 | tf_op jit(solution)/shard_map/ppermute | solution.py:325
  26.9 0.7 %collective-permute-done.6.refs_2_ = bf16[48,512]{1,0:T(8,128)(2,1)S(1)} collective-permute-done((bf16[48,512]{1,0:T(8,128)(2,1)S(1)}, bf16[48,512]{1,0:T(8,128)(2,1)S(1)}, u32[]{:S(2)}, u32[]{:S(2)}) %collective-permute-start.6) | collective-permute-done | bytes 49184 | tf_op jit(solution)/shard_map/ppermute | solution.py:325
  27.6 1.5 %collective-permute-start.12 = (bf16[48,512]{1,0:T(8,128)(2,1)S(1)}, bf16[48,512]{1,0:T(8,128)(2,1)S(1)}, u32[]{:S(2)}, u32[]{:S(2)}) collective-permute-start(bf16[48,512]{1,0:T(8,128)(2,1)S(1)} %get-tuple-element.60), channel_id=1, source_target_pairs={{0,8},{4,12},{8,0},{12,4},{16,24},{20,28},{24,16},{28,20},{1,9},{5... | collective-permute-start | bytes 147464 | tf_op jit(solution)/shard_map/ppermute | solution.py:325
  29.4 1.5 %collective-permute-start.9 = (bf16[48,2048]{1,0:T(8,128)(2,1)S(1)}, bf16[48,2048]{1,0:T(8,128)(2,1)S(1)}, u32[]{:S(2)}, u32[]{:S(2)}) collective-permute-start(bf16[48,2048]{1,0:T(8,128)(2,1)S(1)} %unpick_acts.1.refs_1_.refs_2_), channel_id=1, source_target_pairs={{0,4},{4,0},{8,12},{12,8},{16,20},{20,16},{24,28},{28,24},{1,5},{5... | collective-permute-start | bytes 589832 | tf_op jit(solution)/shard_map/ppermute | solution.py:329
  30.9 3.5 %load_down.1.refs_4_.refs_7_.refs_1_ = bf16[1024,4096]{1,0:T(8,128)(2,1)S(1)} custom-call(bf16[1024,4096]{1,0:T(8,128)(2,1)} %bitcast.23, bf16[48,2048]{1,0:T(8,128)(2,1)S(1)} %unpick_acts.1.refs_1_.refs_2_), custom_call_target="tpu_custom_call" | custom-call | flops 3300000000 | bytes 65536 | tf_op jit(solution)/shard_map/load_down/pallas_call | solution.py:285
  34.7 0.6 collective-permute-start.13
  35.3 6.5 %first.1 = (bf16[512,4096]{1,0:T(8,128)(2,1)S(1)}, f32[1024,48]{1,0:T(8,128)S(1)}, f32[1024,48]{1,0:T(8,128)S(1)}, bf16[48,1024]{1,0:T(8,128)(2,1)S(1)}, bf16[48,2048]{1,0:T(8,128)(2,1)S(1)}) custom-call(bf16[48,2048]{1,0:T(8,128)(2,1)S(1)} %unpick_saved.1.refs_2_.refs_0_, bf16[48,2048]{1,0:T(8,128)(2,1)S(1)} %collective-permute-done.4.refs_1_, ...), custom_call_target="tpu_custom_call" | custom-call | flops 6600000000 | bytes 65536 | tf_op jit(solution)/shard_map/first/pallas_call | solution.py:285
  41.8 2.2 %collective-permute-start.14 = (bf16[48,2048]{1,0:T(8,128)(2,1)S(1)}, bf16[48,2048]{1,0:T(8,128)(2,1)S(1)}, u32[]{:S(2)}, u32[]{:S(2)}) collective-permute-start(bf16[48,2048]{1,0:T(8,128)(2,1)S(1)} %get-tuple-element.66), channel_id=1, source_target_pairs={{0,4},{4,0},{8,12},{12,8},{16,20},{20,16},{24,28},{28,24},{1,5},{5... | collective-permute-start | bytes 589832 | tf_op jit(solution)/shard_map/ppermute | solution.py:329
  44.0 4.1 %backward.1 = (bf16[48,1024]{1,0:T(8,128)(2,1)S(1)}, bf16[48,1024]{1,0:T(8,128)(2,1)S(1)}, bf16[48,2048]{1,0:T(8,128)(2,1)S(1)}) custom-call(bf16[48,2048]{1,0:T(8,128)(2,1)S(1)} %unpick_gradients.1.refs_8_.refs_0_, bf16[48,2048]{1,0:T(8,128)(2,1)S(1)} %collective-permute-done.13.refs_1_, f32[1024,48]{1,0:T(8,128)S(1)} %get-tuple-element.62.refs_2_, ...), custom_call_target="tpu_custom_call" | custom-call | flops 4400000000 | bytes 65536 | tf_op jit(solution)/shard_map/backward/pallas_call | solution.py:285
  48.2 0.8 %forward_own.1.refs_0_ = bf16[48,2048]{1,0:T(8,128)(2,1)S(1)} custom-call(bf16[48,1024]{1,0:T(8,128)(2,1)S(1)} %get-tuple-element.61.refs_0_, bf16[1024,4096]{1,0:T(8,128)(2,1)S(1)} %load_down.1.refs_4_.refs_7_.refs_1_, bf16[48,1024]{1,0:T(8,128)(2,1)S(1)} %get-tuple-element.65.refs_2_.refs_0_), custom_call_target="tpu_custom_call" | custom-call | flops 1100000000 | bytes 65536 | tf_op jit(solution)/shard_map/forward_own/pallas_call | solution.py:285
  49.1 0.3 fold_forward.1
  49.4 2.1 %collective-permute-start.15 = (bf16[48,512]{1,0:T(8,128)(2,1)S(1)}, bf16[48,512]{1,0:T(8,128)(2,1)S(1)}, u32[]{:S(2)}, u32[]{:S(2)}) collective-permute-start(bf16[48,512]{1,0:T(8,128)(2,1)S(1)} %get-tuple-element.68), channel_id=1, source_target_pairs={{0,24},{4,28},{8,16},{12,20},{16,8},{20,12},{24,0},{28,4},{1,25},{... | collective-permute-start | bytes 147464 | tf_op jit(solution)/shard_map/ppermute | solution.py:325
  51.5 0.7 %collective-permute-start.16 = (bf16[48,512]{1,0:T(8,128)(2,1)S(1)}, bf16[48,512]{1,0:T(8,128)(2,1)S(1)}, u32[]{:S(2)}, u32[]{:S(2)}) collective-permute-start(bf16[48,512]{1,0:T(8,128)(2,1)S(1)} %get-tuple-element.69), channel_id=1, source_target_pairs={{0,16},{4,20},{8,24},{12,28},{16,0},{20,4},{24,8},{28,12},{1,17},{... | collective-permute-start | bytes 147464 | tf_op jit(solution)/shard_map/ppermute | solution.py:325
  52.3 1.6 %collective-permute-start.17 = (bf16[48,512]{1,0:T(8,128)(2,1)S(1)}, bf16[48,512]{1,0:T(8,128)(2,1)S(1)}, u32[]{:S(2)}, u32[]{:S(2)}) collective-permute-start(bf16[48,512]{1,0:T(8,128)(2,1)S(1)} %get-tuple-element.70), channel_id=1, source_target_pairs={{0,8},{4,12},{8,0},{12,4},{16,24},{20,28},{24,16},{28,20},{1,9},{5... | collective-permute-start | bytes 147464 | tf_op jit(solution)/shard_map/ppermute | solution.py:325
  53.9 1.6 %backward_own.1.refs_0_ = bf16[48,2048]{1,0:T(8,128)(2,1)S(1)} custom-call(bf16[48,1024]{1,0:T(8,128)(2,1)S(1)} %get-tuple-element.65.refs_2_.refs_0_, bf16[48,1024]{1,0:T(8,128)(2,1)S(1)} %get-tuple-element.71.refs_1_, bf16[1024,4096]{1,0:T(8,128)(2,1)S(1)} %get-tuple-element.56.refs_4_.refs_2_, bf16[512,4096]{1,0:T(8,128)(2,1)S(1)} %get-tuple-element.57.refs_5_.refs_3_, ...), custom_call_target="tpu_custom_call" | custom-call | flops 1650000000 | bytes 65536 | tf_op jit(solution)/shard_map/backward_own/pallas_call | solution.py:285
  55.5 0.3 fold_backward.1
  55.8 2.1 %collective-permute-start.19 = (bf16[48,512]{1,0:T(8,128)(2,1)S(1)}, bf16[48,512]{1,0:T(8,128)(2,1)S(1)}, u32[]{:S(2)}, u32[]{:S(2)}) collective-permute-start(bf16[48,512]{1,0:T(8,128)(2,1)S(1)} %get-tuple-element.75), channel_id=1, source_target_pairs={{0,24},{4,28},{8,16},{12,20},{16,8},{20,12},{24,0},{28,4},{1,25},{... | collective-permute-start | bytes 147464 | tf_op jit(solution)/shard_map/ppermute | solution.py:325
  57.9 2.4 %collective-permute-start.21 = (bf16[48,512]{1,0:T(8,128)(2,1)S(1)}, bf16[48,512]{1,0:T(8,128)(2,1)S(1)}, u32[]{:S(2)}, u32[]{:S(2)}) collective-permute-start(bf16[48,512]{1,0:T(8,128)(2,1)S(1)} %get-tuple-element.77), channel_id=1, source_target_pairs={{0,8},{4,12},{8,0},{12,4},{16,24},{20,28},{24,16},{28,20},{1,9},{5... | collective-permute-start | bytes 147464 | tf_op jit(solution)/shard_map/ppermute | solution.py:325
  60.3 1.3 %combine_acts.1 = bf16[192,2048]{1,0:T(8,128)(2,1)} custom-call(bf16[192,2048]{1,0:T(8,128)(2,1)S(1)} %collective-permute-done.refs_1_.refs_0_, bf16[8,192,192]{2,1,0:T(8,128)(2,1)S(1)} %get-tuple-element.43.refs_4_.refs_1_, bf16[48,512]{1,0:T(8,128)(2,1)S(1)} %get-tuple-element.67.refs_5_.refs_2_, bf16[48,512]{1,0:T(8,128)(2,1)S(1)} %collective-permute-done.15.refs_3_, ...), custom_call_target="tpu_custom_call" | custom-call | flops 1320000000 | bytes 65536 | tf_op jit(solution)/shard_map/combine_acts/pallas_call | solution.py:285
  61.8 1.1 %collective-permute-done.20.refs_4_ = bf16[48,512]{1,0:T(8,128)(2,1)S(1)} collective-permute-done((bf16[48,512]{1,0:T(8,128)(2,1)S(1)}, bf16[48,512]{1,0:T(8,128)(2,1)S(1)}, u32[]{:S(2)}, u32[]{:S(2)}) %collective-permute-start.20) | collective-permute-done | bytes 49184 | tf_op jit(solution)/shard_map/ppermute | solution.py:325
  62.9 1.1 %combine_gradients.1 = bf16[192,2048]{1,0:T(8,128)(2,1)} custom-call(bf16[192,2048]{1,0:T(8,128)(2,1)S(1)} %collective-permute-done.8.refs_2_.refs_0_, bf16[4,192,192]{2,1,0:T(8,128)(2,1)S(1)} %get-tuple-element.74.refs_1_, bf16[48,512]{1,0:T(8,128)(2,1)S(1)} %get-tuple-element.73.refs_6_.refs_2_, bf16[48,512]{1,0:T(8,128)(2,1)S(1)} %collective-permute-done.19.refs_3_, ...), custom_call_target="tpu_custom_call" | custom-call | flops 1320000000 | bytes 65536 | tf_op jit(solution)/shard_map/combine_gradients/pallas_call | solution.py:285
  (28 shorter events, 1.1 us)
Async XLA Ops:
  0.6 16.4 %collective-permute-start = (bf16[192,2048]{1,0:T(8,128)(2,1)}, bf16[192,2048]{1,0:T(8,128)(2,1)S(1)}, u32[]{:S(2)}, u32[]{:S(2)}) collective-permute-start(bf16[192,2048]{1,0:T(8,128)(2,1)} %bitcast.25), channel_id=1, source_target_pairs={{0,1},{1,2},{2,3},{3,0},{4,5},{5,6},{6,7},{7,4},{8,9},{9,10},{10,1... | collective-permute-start | bytes 2359304 | tf_op jit(solution)/shard_map/ppermute | solution.py:321
  3.4 19.3 %collective-permute-start.8 = (bf16[192,2048]{1,0:T(8,128)(2,1)}, bf16[192,2048]{1,0:T(8,128)(2,1)S(1)}, u32[]{:S(2)}, u32[]{:S(2)}) collective-permute-start(bf16[192,2048]{1,0:T(8,128)(2,1)} %bitcast.26), channel_id=1, source_target_pairs={{0,3},{1,0},{2,1},{3,2},{4,7},{5,4},{6,5},{7,6},{8,11},{9,8},{10,9... | collective-permute-start | bytes 2359304 | tf_op jit(solution)/shard_map/ppermute | solution.py:321
  5.4 9.6 %collective-permute-start.1 = (bf16[48,512]{1,0:T(8,128)(2,1)S(1)}, bf16[48,512]{1,0:T(8,128)(2,1)S(1)}, u32[]{:S(2)}, u32[]{:S(2)}) collective-permute-start(bf16[48,512]{1,0:T(8,128)(2,1)S(1)} %get-tuple-element.45), channel_id=1, source_target_pairs={{0,24},{4,28},{8,16},{12,20},{16,8},{20,12},{24,0},{28,4},{1,25},{... | collective-permute-start | bytes 147464 | tf_op jit(solution)/shard_map/ppermute | solution.py:325
  9.8 5.2 %collective-permute-start.2 = (bf16[48,512]{1,0:T(8,128)(2,1)S(1)}, bf16[48,512]{1,0:T(8,128)(2,1)S(1)}, u32[]{:S(2)}, u32[]{:S(2)}) collective-permute-start(bf16[48,512]{1,0:T(8,128)(2,1)S(1)} %get-tuple-element.46), channel_id=1, source_target_pairs={{0,16},{4,20},{8,24},{12,28},{16,0},{20,4},{24,8},{28,12},{1,17},{... | collective-permute-start | bytes 147464 | tf_op jit(solution)/shard_map/ppermute | solution.py:325
  9.8 5.2 %collective-permute-start.3 = (bf16[48,512]{1,0:T(8,128)(2,1)S(1)}, bf16[48,512]{1,0:T(8,128)(2,1)S(1)}, u32[]{:S(2)}, u32[]{:S(2)}) collective-permute-start(bf16[48,512]{1,0:T(8,128)(2,1)S(1)} %get-tuple-element.47), channel_id=1, source_target_pairs={{0,8},{4,12},{8,0},{12,4},{16,24},{20,28},{24,16},{28,20},{1,9},{5... | collective-permute-start | bytes 147464 | tf_op jit(solution)/shard_map/ppermute | solution.py:325
  15.2 20.1 %collective-permute-start.4 = (bf16[48,2048]{1,0:T(8,128)(2,1)S(1)}, bf16[48,2048]{1,0:T(8,128)(2,1)S(1)}, u32[]{:S(2)}, u32[]{:S(2)}) collective-permute-start(bf16[48,2048]{1,0:T(8,128)(2,1)S(1)} %unpick_saved.1.refs_2_.refs_0_), channel_id=1, source_target_pairs={{0,4},{4,0},{8,12},{12,8},{16,20},{20,16},{24,28},{28,24},{1,5},{5... | collective-permute-start | bytes 589832 | tf_op jit(solution)/shard_map/ppermute | solution.py:329
  17.4 9.5 %collective-permute-start.5 = (bf16[48,512]{1,0:T(8,128)(2,1)S(1)}, bf16[48,512]{1,0:T(8,128)(2,1)S(1)}, u32[]{:S(2)}, u32[]{:S(2)}) collective-permute-start(bf16[48,512]{1,0:T(8,128)(2,1)S(1)} %get-tuple-element.50), channel_id=1, source_target_pairs={{0,24},{4,28},{8,16},{12,20},{16,8},{20,12},{24,0},{28,4},{1,25},{... | collective-permute-start | bytes 147464 | tf_op jit(solution)/shard_map/ppermute | solution.py:325
  22.1 5.5 %collective-permute-start.6 = (bf16[48,512]{1,0:T(8,128)(2,1)S(1)}, bf16[48,512]{1,0:T(8,128)(2,1)S(1)}, u32[]{:S(2)}, u32[]{:S(2)}) collective-permute-start(bf16[48,512]{1,0:T(8,128)(2,1)S(1)} %get-tuple-element.51), channel_id=1, source_target_pairs={{0,16},{4,20},{8,24},{12,28},{16,0},{20,4},{24,8},{28,12},{1,17},{... | collective-permute-start | bytes 147464 | tf_op jit(solution)/shard_map/ppermute | solution.py:325
  22.1 7.0 %collective-permute-start.7 = (bf16[48,512]{1,0:T(8,128)(2,1)S(1)}, bf16[48,512]{1,0:T(8,128)(2,1)S(1)}, u32[]{:S(2)}, u32[]{:S(2)}) collective-permute-start(bf16[48,512]{1,0:T(8,128)(2,1)S(1)} %get-tuple-element.52), channel_id=1, source_target_pairs={{0,8},{4,12},{8,0},{12,4},{16,24},{20,28},{24,16},{28,20},{1,9},{5... | collective-permute-start | bytes 147464 | tf_op jit(solution)/shard_map/ppermute | solution.py:325
  23.1 11.3 %collective-permute-start.10 = (bf16[48,512]{1,0:T(8,128)(2,1)S(1)}, bf16[48,512]{1,0:T(8,128)(2,1)S(1)}, u32[]{:S(2)}, u32[]{:S(2)}) collective-permute-start(bf16[48,512]{1,0:T(8,128)(2,1)S(1)} %get-tuple-element.58), channel_id=1, source_target_pairs={{0,24},{4,28},{8,16},{12,20},{16,8},{20,12},{24,0},{28,4},{1,25},{... | collective-permute-start | bytes 147464 | tf_op jit(solution)/shard_map/ppermute | solution.py:325
  26.9 7.5 %collective-permute-start.11 = (bf16[48,512]{1,0:T(8,128)(2,1)S(1)}, bf16[48,512]{1,0:T(8,128)(2,1)S(1)}, u32[]{:S(2)}, u32[]{:S(2)}) collective-permute-start(bf16[48,512]{1,0:T(8,128)(2,1)S(1)} %get-tuple-element.59), channel_id=1, source_target_pairs={{0,16},{4,20},{8,24},{12,28},{16,0},{20,4},{24,8},{28,12},{1,17},{... | collective-permute-start | bytes 147464 | tf_op jit(solution)/shard_map/ppermute | solution.py:325
  27.6 6.8 %collective-permute-start.12 = (bf16[48,512]{1,0:T(8,128)(2,1)S(1)}, bf16[48,512]{1,0:T(8,128)(2,1)S(1)}, u32[]{:S(2)}, u32[]{:S(2)}) collective-permute-start(bf16[48,512]{1,0:T(8,128)(2,1)S(1)} %get-tuple-element.60), channel_id=1, source_target_pairs={{0,8},{4,12},{8,0},{12,4},{16,24},{20,28},{24,16},{28,20},{1,9},{5... | collective-permute-start | bytes 147464 | tf_op jit(solution)/shard_map/ppermute | solution.py:325
  29.4 5.9 %collective-permute-start.9 = (bf16[48,2048]{1,0:T(8,128)(2,1)S(1)}, bf16[48,2048]{1,0:T(8,128)(2,1)S(1)}, u32[]{:S(2)}, u32[]{:S(2)}) collective-permute-start(bf16[48,2048]{1,0:T(8,128)(2,1)S(1)} %unpick_acts.1.refs_1_.refs_2_), channel_id=1, source_target_pairs={{0,4},{4,0},{8,12},{12,8},{16,20},{20,16},{24,28},{28,24},{1,5},{5... | collective-permute-start | bytes 589832 | tf_op jit(solution)/shard_map/ppermute | solution.py:329
  34.7 9.3 %collective-permute-start.13 = (bf16[48,2048]{1,0:T(8,128)(2,1)S(1)}, bf16[48,2048]{1,0:T(8,128)(2,1)S(1)}, u32[]{:S(2)}, u32[]{:S(2)}) collective-permute-start(bf16[48,2048]{1,0:T(8,128)(2,1)S(1)} %unpick_gradients.1.refs_8_.refs_0_), channel_id=1, source_target_pairs={{0,4},{4,0},{8,12},{12,8},{16,20},{20,16},{24,28},{28,24},{1,5},{5... | collective-permute-start | bytes 589832 | tf_op jit(solution)/shard_map/ppermute | solution.py:329
  41.8 7.3 %collective-permute-start.14 = (bf16[48,2048]{1,0:T(8,128)(2,1)S(1)}, bf16[48,2048]{1,0:T(8,128)(2,1)S(1)}, u32[]{:S(2)}, u32[]{:S(2)}) collective-permute-start(bf16[48,2048]{1,0:T(8,128)(2,1)S(1)} %get-tuple-element.66), channel_id=1, source_target_pairs={{0,4},{4,0},{8,12},{12,8},{16,20},{20,16},{24,28},{28,24},{1,5},{5... | collective-permute-start | bytes 589832 | tf_op jit(solution)/shard_map/ppermute | solution.py:329
  48.1 7.3 %collective-permute-start.18 = (bf16[48,2048]{1,0:T(8,128)(2,1)S(1)}, bf16[48,2048]{1,0:T(8,128)(2,1)S(1)}, u32[]{:S(2)}, u32[]{:S(2)}) collective-permute-start(bf16[48,2048]{1,0:T(8,128)(2,1)S(1)} %get-tuple-element.72), channel_id=1, source_target_pairs={{0,4},{4,0},{8,12},{12,8},{16,20},{20,16},{24,28},{28,24},{1,5},{5... | collective-permute-start | bytes 589832 | tf_op jit(solution)/shard_map/ppermute | solution.py:329
  49.4 8.5 %collective-permute-start.15 = (bf16[48,512]{1,0:T(8,128)(2,1)S(1)}, bf16[48,512]{1,0:T(8,128)(2,1)S(1)}, u32[]{:S(2)}, u32[]{:S(2)}) collective-permute-start(bf16[48,512]{1,0:T(8,128)(2,1)S(1)} %get-tuple-element.68), channel_id=1, source_target_pairs={{0,24},{4,28},{8,16},{12,20},{16,8},{20,12},{24,0},{28,4},{1,25},{... | collective-permute-start | bytes 147464 | tf_op jit(solution)/shard_map/ppermute | solution.py:325
  51.5 8.7 %collective-permute-start.16 = (bf16[48,512]{1,0:T(8,128)(2,1)S(1)}, bf16[48,512]{1,0:T(8,128)(2,1)S(1)}, u32[]{:S(2)}, u32[]{:S(2)}) collective-permute-start(bf16[48,512]{1,0:T(8,128)(2,1)S(1)} %get-tuple-element.69), channel_id=1, source_target_pairs={{0,16},{4,20},{8,24},{12,28},{16,0},{20,4},{24,8},{28,12},{1,17},{... | collective-permute-start | bytes 147464 | tf_op jit(solution)/shard_map/ppermute | solution.py:325
  52.3 8.0 %collective-permute-start.17 = (bf16[48,512]{1,0:T(8,128)(2,1)S(1)}, bf16[48,512]{1,0:T(8,128)(2,1)S(1)}, u32[]{:S(2)}, u32[]{:S(2)}) collective-permute-start(bf16[48,512]{1,0:T(8,128)(2,1)S(1)} %get-tuple-element.70), channel_id=1, source_target_pairs={{0,8},{4,12},{8,0},{12,4},{16,24},{20,28},{24,16},{28,20},{1,9},{5... | collective-permute-start | bytes 147464 | tf_op jit(solution)/shard_map/ppermute | solution.py:325
  55.8 6.0 %collective-permute-start.19 = (bf16[48,512]{1,0:T(8,128)(2,1)S(1)}, bf16[48,512]{1,0:T(8,128)(2,1)S(1)}, u32[]{:S(2)}, u32[]{:S(2)}) collective-permute-start(bf16[48,512]{1,0:T(8,128)(2,1)S(1)} %get-tuple-element.75), channel_id=1, source_target_pairs={{0,24},{4,28},{8,16},{12,20},{16,8},{20,12},{24,0},{28,4},{1,25},{... | collective-permute-start | bytes 147464 | tf_op jit(solution)/shard_map/ppermute | solution.py:325
  57.9 5.0 %collective-permute-start.20 = (bf16[48,512]{1,0:T(8,128)(2,1)S(1)}, bf16[48,512]{1,0:T(8,128)(2,1)S(1)}, u32[]{:S(2)}, u32[]{:S(2)}) collective-permute-start(bf16[48,512]{1,0:T(8,128)(2,1)S(1)} %get-tuple-element.76), channel_id=1, source_target_pairs={{0,16},{4,20},{8,24},{12,28},{16,0},{20,4},{24,8},{28,12},{1,17},{... | collective-permute-start | bytes 147464 | tf_op jit(solution)/shard_map/ppermute | solution.py:325
  57.9 5.0 %collective-permute-start.21 = (bf16[48,512]{1,0:T(8,128)(2,1)S(1)}, bf16[48,512]{1,0:T(8,128)(2,1)S(1)}, u32[]{:S(2)}, u32[]{:S(2)}) collective-permute-start(bf16[48,512]{1,0:T(8,128)(2,1)S(1)} %get-tuple-element.77), channel_id=1, source_target_pairs={{0,8},{4,12},{8,0},{12,4},{16,24},{20,28},{24,16},{28,20},{1,9},{5... | collective-permute-start | bytes 147464 | tf_op jit(solution)/shard_map/ppermute | solution.py:325

commit v3 on v2

--- a/solution.py
+++ b/solution.py
@@ -168,15 +168,7 @@
         store.wait()
 
 
-def lay_rows(sz, slices, rows):
-    me = lax.rem(lax.axis_index("expert"), sz.split)
-    for j, s in enumerate(slices):
-        at = lax.rem(me + sz.split - j, sz.split) * sz.width
-        rows[:, pl.ds(pl.multiple_of(at, 128), sz.width)] = s[...]
-
-
-def load_kernel(sz, w_f, w_b, wg, wu, wg_near, wu_near, f_turned, b_turned, sems):
-    copies = fetch([(wg, wg_near), (wu.at[: wu_near.shape[0]], wu_near)], sems)
+def turn_kernel(sz, w_f, w_b, f_turned, b_turned):
     _, part, _ = place_of(sz, lax.broadcasted_iota(jnp.int32, (sz.count, sz.spread), 1))
     f = w_f[...].T
     b = w_b[...].astype(F32).T
@@ -186,45 +178,39 @@
         f_turned[2 * q] = high
         f_turned[2 * q + 1] = (mine - high.astype(F32)).astype(BF16)
         b_turned[q] = jnp.where(part == q, b, 0.0).astype(BF16)
-    for c in copies:
-        c.wait()
-
-
-def load_one_kernel(weight, held, sems):
-    half = weight.shape[0] // 2
-    for c in fetch([(weight.at[cut], held.at[cut]) for cut in (pl.ds(0, half), pl.ds(half, half))], sems):
-        c.wait()
-
-
-def by_halves(weight, turned, out):
+
+
+def add_product(sz, weight, behind, turned, before, out):
+    at = lax.rem(lax.axis_index("expert") + sz.split - behind, sz.split) * sz.width
+    columns = pl.ds(pl.multiple_of(at, 128), sz.width)
     half = weight.shape[0] // 2
     for cut in (slice(0, half), slice(half, None)):
-        out[cut, :] = mm(weight[cut, :], turned[...])
+        product = mm(weight[cut, columns], turned[...])
+        out[cut, :] = product if before is None else before[cut, :] + product
+
+
+def first_own_kernel(sz, b, x, wg, wu, gate_all, up_all, turned):
+    turned[:, : sz.slots] = b[...].T
+    turned[:, sz.slots :] = x[...].T
+    add_product(sz, wg, 0, turned, None, gate_all)
+    add_product(sz, wu, 0, turned, None, up_all)
 
 
 def first_kernel(sz, *refs):
-    n, m, half = sz.split, sz.slots, sz.hidden // 2
-    b_slices, x_slices, (wg, wu_0, wu, wd), refs = refs[:n], refs[n : 2 * n], refs[2 * n : 2 * n + 4], refs[2 * n + 4 :]
-    wu_1, gate, up, hidden, *outs = refs[:-5]
-    rows, turned, gate_all, up_all, sems = refs[-5:]
-    (copy,) = fetch([(wu.at[half:], wu_1)], sems)
-    lay_rows(sz, b_slices, rows)
-    turned[:, :m] = rows[...].T
-    lay_rows(sz, x_slices, rows)
-    turned[:, m:] = rows[...].T
-    by_halves(wg, turned, gate_all)
-    up_all[:half, :] = mm(wu_0[...], turned[...])
-
-    @pl.when(lax.axis_index("expert") >= 0)
-    def _():
-        copy.wait()
-        up_all[half:, :] = mm(wu_1[...], turned[...])
-
+    n, m = sz.split - 1, sz.slots
+    b_slices, x_slices, (gate_own, up_own, wg, wu, wd), refs = refs[:n], refs[n : 2 * n], refs[2 * n : 2 * n + 5], refs[2 * n + 5 :]
+    gate, up, hidden, *outs = refs[:-3]
+    turned, gate_all, up_all = refs[-3:]
+    for j, (b, x) in enumerate(zip(b_slices, x_slices)):
+        turned[:, :m] = b[...].T
+        turned[:, m:] = x[...].T
+        add_product(sz, wg, j + 1, turned, gate_own if j == 0 else gate_all, gate_all)
+        add_product(sz, wu, j + 1, turned, up_own if j == 0 else up_all, up_all)
     g = gate_all[:, m:]
     hidden[...] = (g * jax.nn.sigmoid(g) * up_all[:, m:]).T.astype(BF16)
     gate[...] = gate_all[:, :m]
     up[...] = up_all[:, :m]
-    forward_slices(sz, range(1, n), hidden, wd, outs)
+    forward_slices(sz, range(1, sz.split), hidden, wd, outs)
 
 
 def columns_of(sz, j):
@@ -237,12 +223,10 @@
     ]
 
 
-def backward_slices(sz, js, d_gate, d_up, wg, wu_0, wu_1, outs):
-    half = wu_0.shape[0]
+def backward_slices(sz, js, d_gate, d_up, wg, wu, outs):
     for j, out in zip(js, outs):
         for here, there in columns_of(sz, j):
-            total = mm(d_gate[...], wg[:, there]) + mm(d_up[:, :half], wu_0[:, there]) + mm(d_up[:, half:], wu_1[:, there])
-            out[:, here] = total.astype(BF16)
+            out[:, here] = (mm(d_gate[...], wg[:, there]) + mm(d_up[...], wu[:, there])).astype(BF16)
 
 
 def forward_slices(sz, js, hidden, wd, outs):
@@ -251,24 +235,29 @@
             out[:, here] = mm(hidden[...], wd[:, there]).astype(BF16)
 
 
+def hidden_gradient_own_kernel(sz, g, wd, dh, turned):
+    turned[...] = g[...].T
+    add_product(sz, wd, 0, turned, None, dh)
+
+
 def backward_kernel(sz, *refs):
-    n = sz.split
-    slices, (gate, up, wg, wu_0, wu_1, wd), refs = refs[:n], refs[n : n + 6], refs[n + 6 :]
-    d_gate, d_up, *outs = refs[:-3]
-    rows, turned, dh = refs[-3:]
-    lay_rows(sz, slices, rows)
-    turned[...] = rows[...].T
-    by_halves(wd, turned, dh)
-    dh = dh[...]
+    n = sz.split - 1
+    slices, (dh_own, gate, up, wg, wu, wd), refs = refs[:n], refs[n : n + 6], refs[n + 6 :]
+    d_gate, d_up, *outs = refs[:-2]
+    turned, dh_all = refs[-2:]
+    for j, s in enumerate(slices):
+        turned[...] = s[...].T
+        add_product(sz, wd, j + 1, turned, dh_own if j == 0 else dh_all, dh_all)
+    dh = dh_all[...]
     g = gate[...]
     sig = jax.nn.sigmoid(g)
     d_up[...] = (dh * (g * sig)).T.astype(BF16)
     d_gate[...] = (dh * up[...] * sig * (1.0 + g * (1.0 - sig))).T.astype(BF16)
-    backward_slices(sz, range(1, n), d_gate, d_up, wg, wu_0, wu_1, outs)
-
-
-def backward_own_kernel(sz, d_gate, d_up, wg, wu_0, wu_1, out):
-    backward_slices(sz, (0,), d_gate, d_up, wg, wu_0, wu_1, (out,))
+    backward_slices(sz, range(1, sz.split), d_gate, d_up, wg, wu, outs)
+
+
+def backward_own_kernel(sz, d_gate, d_up, wg, wu, out):
+    backward_slices(sz, (0,), d_gate, d_up, wg, wu, (out,))
 
 
 def forward_own_kernel(sz, hidden, wd, out):
@@ -340,11 +329,9 @@
     held = ((sz.spread, sz.cols), BF16)
     route_scratch = [pltpu.VMEM(fwd_routes.shape[:0:-1], d) for d in (jnp.int32, F32)]
     block_scratch = pltpu.VMEM((count, width), BF16)
-    rows_scratch = pltpu.VMEM((sz.slots, full), BF16)
 
     fr, fp, br, bp = fwd_routes[0].T, fwd_probs[0].T, back_routes[0].T, back_probs[0].T
     x_full = by_section(acts, 1)
-    half_weight = ((sz.hidden // 2, full), BF16)
     table = (sz.spread, count)
     w_f, m_f, m_b, scale, *b_out = near(
         part(local_kernel, sz),
@@ -358,58 +345,63 @@
     b_in = exchange(b_out)
     grads, m_b = lax.optimization_barrier((grads, m_b))
     dy_full = by_section(grads, -1)
-    wg_near, wu_0, f_turned, b_turned = near(
-        part(load_kernel, sz),
-        [(wg.shape, BF16), half_weight] + [((n * sz.parts, count, sz.spread), BF16) for n in (2, 1)],
-        (w_f, m_b, wg, wu),
-        "load",
-        4.0,
-        far=(2, 3),
-        scratch=[pltpu.SemaphoreType.DMA((2,))],
+    f_turned, b_turned = near(
+        part(turn_kernel, sz), [((n * sz.parts, count, sz.spread), BF16) for n in (2, 1)], (w_f, m_b), "turn", 4.0
     )
     unpicked = lambda pieces, name, after=(): near(part(unpick_kernel, sz), [rows], pieces, name, after=after)[0]
     b_near = unpicked(b_in, "unpick_saved", (f_turned,))
-    x_out = near(part(pick_again_kernel, sz, 0), pieces, (m_f, x_full), "pick_acts", 0.5, after=(b_near,))
+    x_out = near(part(pick_again_kernel, sz, 0), pieces, (m_f, x_full), "pick_acts", 4.5, after=(b_near,))
     x_in = exchange(x_out)
     g_out = near(
         part(pick_again_kernel, sz, 1), pieces, (m_b, scale, dy_full), "pick_gradients", 0.5, after=x_out[:1]
     )
     x_near = unpicked(x_in, "unpick_acts", g_out[:1])
-    wd_near = near(
-        load_one_kernel, [(wd.shape, BF16)], (wd,), "load_down", 3.0, far=(0,), scratch=[pltpu.SemaphoreType.DMA((2,))], after=(x_near,)
-    )[0]
+    both = (sz.hidden, 2 * sz.slots)
+    gate_own, up_own = near(
+        part(first_own_kernel, sz),
+        [(both, F32)] * 2,
+        (b_near, x_near, wg, wu),
+        "first_own",
+        3.0,
+        scratch=[pltpu.VMEM((width, 2 * sz.slots), BF16)],
+    )
     g_in = exchange(g_out)
-    g_near = unpicked(g_in, "unpick_gradients", (wd_near,))
+    g_near = unpicked(g_in, "unpick_gradients", (gate_own,))
     b_rows, x_rows, g_rows = gather(b_near), gather(x_near), gather(g_near)
 
     hidden_f32 = ((sz.hidden, sz.slots), F32)
     hidden_bf16 = ((sz.slots, sz.hidden), BF16)
-    both = pltpu.VMEM((sz.hidden, 2 * sz.slots), F32)
-    wu_1, gate, up, hidden, *made = near(
+    (dh_own,) = near(
+        part(hidden_gradient_own_kernel, sz),
+        [hidden_f32],
+        (g_near, wd),
+        "hidden_gradient_own",
+        1.0,
+        scratch=[pltpu.VMEM((width, sz.slots), BF16)],
+    )
+    gate, up, hidden, *made = near(
         part(first_kernel, sz),
-        [half_weight] + [hidden_f32] * 2 + [hidden_bf16] + [rows] * (split - 1),
-        (*b_rows, *x_rows, wg_near, wu_0, wu, wd_near),
+        [hidden_f32] * 2 + [hidden_bf16] + [rows] * (split - 1),
+        (*b_rows[1:], *x_rows[1:], gate_own, up_own, wg, wu, wd),
         "first",
-        6.0,
-        far=(2 * split + 2,),
-        scratch=[rows_scratch, pltpu.VMEM((full, 2 * sz.slots), BF16), both, both, pltpu.SemaphoreType.DMA((1,))],
-        after=(g_near,),
+        4.0,
+        scratch=[pltpu.VMEM((width, 2 * sz.slots), BF16), pltpu.VMEM(both, F32), pltpu.VMEM(both, F32)],
+        after=(dh_own,),
     )
     made_in = scatter(made)
-    up_weights = (wg_near, wu_0, wu_1)
     d_gate, d_up, *back = near(
         part(backward_kernel, sz),
         [hidden_bf16] * 2 + [rows] * (split - 1),
-        (*g_rows, gate, up, *up_weights, wd_near),
+        (*g_rows[1:], dh_own, gate, up, wg, wu, wd),
         "backward",
-        4.0,
-        scratch=[rows_scratch, pltpu.VMEM((full, sz.slots), BF16), pltpu.VMEM((sz.hidden, sz.slots), F32)],
+        3.0,
+        scratch=[pltpu.VMEM((width, sz.slots), BF16), pltpu.VMEM((sz.hidden, sz.slots), F32)],
     )
     back_in = scatter(back)
-    made_own = near(part(forward_own_kernel, sz), [rows], (hidden, wd_near), "forward_own", 1.0, after=(d_gate,))
+    made_own = near(part(forward_own_kernel, sz), [rows], (hidden, wd), "forward_own", 1.0, after=(d_gate,))
     made_pieces = near(part(fold_kernel, sz), pieces, (*made_own, *made_in), "fold_forward")
     back_own = near(
-        part(backward_own_kernel, sz), [rows], (d_gate, d_up, *up_weights), "backward_own", 1.5, after=made_pieces[:1]
+        part(backward_own_kernel, sz), [rows], (d_gate, d_up, wg, wu), "backward_own", 1.5, after=made_pieces[:1]
     )
     made_pieces = exchange(made_pieces)
     back_pieces = exchange(near(part(fold_kernel, sz), pieces, (*back_own, *back_in), "fold_backward"))

time: 65.3 us -> 60.2 us (0.922); the launches traced: 64.2 us -> 60 us
  Pallas kernels: 27.8 us -> 20.4 us
  waiting for transfers between devices: 2.07 us -> 7.15 us
  starting transfers between devices: 33.3 us -> 31.5 us
    pallas_call x16 -> x17, Pallas kernels: 27.8 us -> 20.4 us  [near(): pl.pallas_call(body, out_shape=[jax.ShapeDtypeStruct(s, d) for s, d in ou...]
    ppermute x15, waiting for transfers between devices: 2.05 us -> 5.3 us  [exchange(): lax.ppermute(pieces[o], 'expert', pairs(o))]
    ppermute x15, starting transfers between devices: 24.5 us -> 23.1 us  [exchange(): lax.ppermute(pieces[o], 'expert', pairs(o))]
    ppermute x2, waiting for transfers between devices: 0.01 us -> 1.22 us  [by_section(): lax.ppermute(x, 'section', [(i, (i + by) % sections) for i in range(secti...]
    ppermute x2, starting transfers between devices: 2.5 us -> 1.68 us  [by_section(): lax.ppermute(x, 'section', [(i, (i + by) % sections) for i in range(secti...]
  transfers between devices with their start and end apart: 22 -> 22, of which waited for: 3 -> 6; matrix products, arithmetic and copies ran while one was open for 0% -> 0% of each run, Pallas kernels for 42% -> 32%
where the time goes in v3:
time: 60.2 us; the launch traced here: 60 us
  starting transfers between devices  31.5 us (52%)
  Pallas kernels  20.4 us (34%)
  waiting for transfers between devices  7.15 us (12%)
  between operations  0.88 us (1%)
    ppermute x15, starting transfers between devices, exchange(): lax.ppermute(pieces[o], 'expert', pairs(o))  23.1 us
    pallas_call x17, Pallas kernels, near(): pl.pallas_call(body, out_shape=[jax.ShapeDtypeStruct(s, d) for s, d in ou...  20.4 us
    ppermute x5, starting transfers between devices, along_group(): return lax.ppermute(x, 'expert', pairs)  6.73 us
    ppermute x15, waiting for transfers between devices, exchange(): lax.ppermute(pieces[o], 'expert', pairs(o))  5.3 us
    ppermute x2, starting transfers between devices, by_section(): lax.ppermute(x, 'section', [(i, (i + by) % sections) for i in range(secti...  1.68 us
    ppermute x2, waiting for transfers between devices, by_section(): lax.ppermute(x, 'section', [(i, (i + by) % sections) for i in range(secti...  1.22 us
  transfers between devices with their start and end apart: 22, of which 6 were waited for; matrix products, arithmetic and copies ran while one was open for 0% of the time, Pallas kernels for 32%

profile of v3, /device:TPU:0, one launch (start us, length us, event | category | flops | bytes accessed | tf_op | source)
XLA Modules:
  0.0 60.0 jit_solution(15118303204143699687)
XLA Ops:
  0.6 0.5 collective-permute-start
  1.1 2.2 %local.1 = (f32[192,192]{1,0:T(8,128)S(1)}, bf16[192,192]{1,0:T(8,128)(2,1)S(1)}, bf16[192,192]{1,0:T(8,128)(2,1)S(1)}, f32[192,128]{1,0:T(8,128)S(1)}, bf16[48,...) custom-call(s32[8,768]{1,0:T(8,128)} %bitcast.41, ...), custom_call_target="tpu_custom_call" | custom-call | flops 2200000000 | bytes 65536 | tf_op jit(solution)/shard_map/local/pallas_call | solution.py:274
  3.4 4.7 %collective-permute-start.1 = (bf16[48,512]{1,0:T(8,128)(2,1)S(1)}, bf16[48,512]{1,0:T(8,128)(2,1)S(1)}, u32[]{:S(2)}, u32[]{:S(2)}) collective-permute-start(bf16[48,512]{1,0:T(8,128)(2,1)S(1)} %get-tuple-element.44), channel_id=1, source_target_pairs={{0,24},{4,28},{8,16},{12,20},{16,8},{20,12},{24,0},{28,4},{1,25},{... | collective-permute-start | bytes 147464 | tf_op jit(solution)/shard_map/ppermute | solution.py:314
  8.1 0.6 %collective-permute-start.3 = (bf16[48,512]{1,0:T(8,128)(2,1)S(1)}, bf16[48,512]{1,0:T(8,128)(2,1)S(1)}, u32[]{:S(2)}, u32[]{:S(2)}) collective-permute-start(bf16[48,512]{1,0:T(8,128)(2,1)S(1)} %get-tuple-element.46), channel_id=1, source_target_pairs={{0,8},{4,12},{8,0},{12,4},{16,24},{20,28},{24,16},{28,20},{1,9},{5... | collective-permute-start | bytes 147464 | tf_op jit(solution)/shard_map/ppermute | solution.py:314
  8.7 1.2 %collective-permute-start.8 = (bf16[192,2048]{1,0:T(8,128)(2,1)}, bf16[192,2048]{1,0:T(8,128)(2,1)S(1)}, u32[]{:S(2)}, u32[]{:S(2)}) collective-permute-start(bf16[192,2048]{1,0:T(8,128)(2,1)} %bitcast.40), channel_id=1, source_target_pairs={{0,3},{1,0},{2,1},{3,2},{4,7},{5,4},{6,5},{7,6},{8,11},{9,8},{10,9... | collective-permute-start | bytes 2359304 | tf_op jit(solution)/shard_map/ppermute | solution.py:310
  10.2 3.2 %collective-permute-done.2.refs_2_ = bf16[48,512]{1,0:T(8,128)(2,1)S(1)} collective-permute-done((bf16[48,512]{1,0:T(8,128)(2,1)S(1)}, bf16[48,512]{1,0:T(8,128)(2,1)S(1)}, u32[]{:S(2)}, u32[]{:S(2)}) %collective-permute-start.2) | collective-permute-done | bytes 49184 | tf_op jit(solution)/shard_map/ppermute | solution.py:314
  13.7 1.6 %collective-permute-start.4 = (bf16[48,2048]{1,0:T(8,128)(2,1)S(1)}, bf16[48,2048]{1,0:T(8,128)(2,1)S(1)}, u32[]{:S(2)}, u32[]{:S(2)}) collective-permute-start(bf16[48,2048]{1,0:T(8,128)(2,1)S(1)} %unpick_saved.1.refs_2_.refs_0_), channel_id=1, source_target_pairs={{0,4},{4,0},{8,12},{12,8},{16,20},{20,16},{24,28},{28,24},{1,5},{5... | collective-permute-start | bytes 589832 | tf_op jit(solution)/shard_map/ppermute | solution.py:318
  15.6 2.9 %collective-permute-start.5 = (bf16[48,512]{1,0:T(8,128)(2,1)S(1)}, bf16[48,512]{1,0:T(8,128)(2,1)S(1)}, u32[]{:S(2)}, u32[]{:S(2)}) collective-permute-start(bf16[48,512]{1,0:T(8,128)(2,1)S(1)} %get-tuple-element.49), channel_id=1, source_target_pairs={{0,24},{4,28},{8,16},{12,20},{16,8},{20,12},{24,0},{28,4},{1,25},{... | collective-permute-start | bytes 147464 | tf_op jit(solution)/shard_map/ppermute | solution.py:314
  18.5 1.6 %collective-permute-start.7 = (bf16[48,512]{1,0:T(8,128)(2,1)S(1)}, bf16[48,512]{1,0:T(8,128)(2,1)S(1)}, u32[]{:S(2)}, u32[]{:S(2)}) collective-permute-start(bf16[48,512]{1,0:T(8,128)(2,1)S(1)} %get-tuple-element.51), channel_id=1, source_target_pairs={{0,8},{4,12},{8,0},{12,4},{16,24},{20,28},{24,16},{28,20},{1,9},{5... | collective-permute-start | bytes 147464 | tf_op jit(solution)/shard_map/ppermute | solution.py:314
  20.1 1.2 %collective-permute-done.8.refs_2_.refs_0_ = bf16[192,2048]{1,0:T(8,128)(2,1)S(1)} collective-permute-done((bf16[192,2048]{1,0:T(8,128)(2,1)}, bf16[192,2048]{1,0:T(8,128)(2,1)S(1)}, u32[]{:S(2)}, u32[]{:S(2)}) %collective-permute-start.8) | collective-permute-done | bytes 786464 | tf_op jit(solution)/shard_map/ppermute | solution.py:310
  21.7 3.7 %collective-permute-start.10 = (bf16[48,512]{1,0:T(8,128)(2,1)S(1)}, bf16[48,512]{1,0:T(8,128)(2,1)S(1)}, u32[]{:S(2)}, u32[]{:S(2)}) collective-permute-start(bf16[48,512]{1,0:T(8,128)(2,1)S(1)} %get-tuple-element.57), channel_id=1, source_target_pairs={{0,24},{4,28},{8,16},{12,20},{16,8},{20,12},{24,0},{28,4},{1,25},{... | collective-permute-start | bytes 147464 | tf_op jit(solution)/shard_map/ppermute | solution.py:314
  25.3 0.8 %collective-permute-start.12 = (bf16[48,512]{1,0:T(8,128)(2,1)S(1)}, bf16[48,512]{1,0:T(8,128)(2,1)S(1)}, u32[]{:S(2)}, u32[]{:S(2)}) collective-permute-start(bf16[48,512]{1,0:T(8,128)(2,1)S(1)} %get-tuple-element.59), channel_id=1, source_target_pairs={{0,8},{4,12},{8,0},{12,4},{16,24},{20,28},{24,16},{28,20},{1,9},{5... | collective-permute-start | bytes 147464 | tf_op jit(solution)/shard_map/ppermute | solution.py:314
  26.4 1.6 %collective-permute-start.9 = (bf16[48,2048]{1,0:T(8,128)(2,1)S(1)}, bf16[48,2048]{1,0:T(8,128)(2,1)S(1)}, u32[]{:S(2)}, u32[]{:S(2)}) collective-permute-start(bf16[48,2048]{1,0:T(8,128)(2,1)S(1)} %unpick_acts.1.refs_1_), channel_id=1, source_target_pairs={{0,4},{4,0},{8,12},{12,8},{16,20},{20,16},{24,28},{28,24},{1,5},{5... | collective-permute-start | bytes 589832 | tf_op jit(solution)/shard_map/ppermute | solution.py:318
  28.0 3.0 %first_own.1 = (f32[1024,96]{1,0:T(8,128)S(1)}, f32[1024,96]{1,0:T(8,128)S(1)}) custom-call(bf16[48,2048]{1,0:T(8,128)(2,1)S(1)} %unpick_saved.1.refs_2_.refs_0_, bf16[48,2048]{1,0:T(8,128)(2,1)S(1)} %unpick_acts.1.refs_1_, bf16[1024,4096]{1,0:T(8,128)(2,1)S(1)} %bitcast.28, bf16[1024,4096]{1,0:T(8,128)(2,1)S(1)} %bitcast.34), custom_call_target="tpu_custom_call" | custom-call | flops 3300000000 | bytes 65536 | tf_op jit(solution)/shard_map/first_own/pallas_call | solution.py:274
  31.3 1.4 %collective-permute-start.13 = (bf16[48,2048]{1,0:T(8,128)(2,1)S(1)}, bf16[48,2048]{1,0:T(8,128)(2,1)S(1)}, u32[]{:S(2)}, u32[]{:S(2)}) collective-permute-start(bf16[48,2048]{1,0:T(8,128)(2,1)S(1)} %unpick_gradients.1.refs_0_), channel_id=1, source_target_pairs={{0,4},{4,0},{8,12},{12,8},{16,20},{20,16},{24,28},{28,24},{1,5},{5... | collective-permute-start | bytes 589832 | tf_op jit(solution)/shard_map/ppermute | solution.py:318
  32.7 1.3 %hidden_gradient_own.1.refs_7_.refs_1_ = f32[1024,48]{1,0:T(8,128)S(1)} custom-call(bf16[48,2048]{1,0:T(8,128)(2,1)S(1)} %unpick_gradients.1.refs_0_, bf16[1024,4096]{1,0:T(8,128)(2,1)S(1)} %bitcast.22), custom_call_target="tpu_custom_call" | custom-call | flops 1100000000 | bytes 65536 | tf_op jit(solution)/shard_map/hidden_gradient_own/pallas_call | solution.py:274
  34.0 3.8 %first.1 = (f32[1024,48]{1,0:T(8,128)S(1)}, f32[1024,48]{1,0:T(8,128)S(1)}, bf16[48,1024]{1,0:T(8,128)(2,1)S(1)}, bf16[48,2048]{1,0:T(8,128)(2,1)S(1)}) custom-call(bf16[48,2048]{1,0:T(8,128)(2,1)S(1)} %collective-permute-done.4.refs_0_, bf16[48,2048]{1,0:T(8,128)(2,1)S(1)} %collective-permute-done.9.refs_1_, ...), custom_call_target="tpu_custom_call" | custom-call | flops 4400000000 | bytes 65536 | tf_op jit(solution)/shard_map/first/pallas_call | solution.py:274
  37.8 1.1 %collective-permute-start.14 = (bf16[48,2048]{1,0:T(8,128)(2,1)S(1)}, bf16[48,2048]{1,0:T(8,128)(2,1)S(1)}, u32[]{:S(2)}, u32[]{:S(2)}) collective-permute-start(bf16[48,2048]{1,0:T(8,128)(2,1)S(1)} %get-tuple-element.64), channel_id=1, source_target_pairs={{0,4},{4,0},{8,12},{12,8},{16,20},{20,16},{24,28},{28,24},{1,5},{5... | collective-permute-start | bytes 589832 | tf_op jit(solution)/shard_map/ppermute | solution.py:318
  39.0 3.0 %backward.1 = (bf16[48,1024]{1,0:T(8,128)(2,1)S(1)}, bf16[48,1024]{1,0:T(8,128)(2,1)S(1)}, bf16[48,2048]{1,0:T(8,128)(2,1)S(1)}) custom-call(bf16[48,2048]{1,0:T(8,128)(2,1)S(1)} %collective-permute-done.13.refs_0_, f32[1024,48]{1,0:T(8,128)S(1)} %hidden_gradient_own.1.refs_7_.refs_1_, f32[1024,48]{1,0:T(8,128)S(1)} %get-tuple-element.61.refs_2_, ...), custom_call_target="tpu_custom_call" | custom-call | flops 3300000000 | bytes 65536 | tf_op jit(solution)/shard_map/backward/pallas_call | solution.py:274
  42.0 1.0 %collective-permute-start.18 = (bf16[48,2048]{1,0:T(8,128)(2,1)S(1)}, bf16[48,2048]{1,0:T(8,128)(2,1)S(1)}, u32[]{:S(2)}, u32[]{:S(2)}) collective-permute-start(bf16[48,2048]{1,0:T(8,128)(2,1)S(1)} %get-tuple-element.70), channel_id=1, source_target_pairs={{0,4},{4,0},{8,12},{12,8},{16,20},{20,16},{24,28},{28,24},{1,5},{5... | collective-permute-start | bytes 589832 | tf_op jit(solution)/shard_map/ppermute | solution.py:318
  43.0 0.8 %forward_own.1.refs_0_ = bf16[48,2048]{1,0:T(8,128)(2,1)S(1)} custom-call(bf16[48,1024]{1,0:T(8,128)(2,1)S(1)} %get-tuple-element.60.refs_0_, bf16[1024,4096]{1,0:T(8,128)(2,1)S(1)} %bitcast.25, bf16[48,1024]{1,0:T(8,128)(2,1)S(1)} %get-tuple-element.63.refs_2_.refs_0_), custom_call_target="tpu_custom_call" | custom-call | flops 1100000000 | bytes 65536 | tf_op jit(solution)/shard_map/forward_own/pallas_call | solution.py:274
  43.8 0.6 %collective-permute-done.14.refs_1_ = bf16[48,2048]{1,0:T(8,128)(2,1)S(1)} collective-permute-done((bf16[48,2048]{1,0:T(8,128)(2,1)S(1)}, bf16[48,2048]{1,0:T(8,128)(2,1)S(1)}, u32[]{:S(2)}, u32[]{:S(2)}) %collective-permute-start.14) | collective-permute-done | bytes 196640 | tf_op jit(solution)/shard_map/ppermute | solution.py:318
  44.8 2.7 %collective-permute-start.15 = (bf16[48,512]{1,0:T(8,128)(2,1)S(1)}, bf16[48,512]{1,0:T(8,128)(2,1)S(1)}, u32[]{:S(2)}, u32[]{:S(2)}) collective-permute-start(bf16[48,512]{1,0:T(8,128)(2,1)S(1)} %get-tuple-element.66), channel_id=1, source_target_pairs={{0,24},{4,28},{8,16},{12,20},{16,8},{20,12},{24,0},{28,4},{1,25},{... | collective-permute-start | bytes 147464 | tf_op jit(solution)/shard_map/ppermute | solution.py:314
  47.5 0.6 collective-permute-start.16
  48.1 1.2 %collective-permute-start.17 = (bf16[48,512]{1,0:T(8,128)(2,1)S(1)}, bf16[48,512]{1,0:T(8,128)(2,1)S(1)}, u32[]{:S(2)}, u32[]{:S(2)}) collective-permute-start(bf16[48,512]{1,0:T(8,128)(2,1)S(1)} %get-tuple-element.68), channel_id=1, source_target_pairs={{0,8},{4,12},{8,0},{12,4},{16,24},{20,28},{24,16},{28,20},{1,9},{5... | collective-permute-start | bytes 147464 | tf_op jit(solution)/shard_map/ppermute | solution.py:314
  49.2 1.6 %backward_own.1.refs_0_ = bf16[48,2048]{1,0:T(8,128)(2,1)S(1)} custom-call(bf16[48,1024]{1,0:T(8,128)(2,1)S(1)} %get-tuple-element.63.refs_2_.refs_0_, bf16[48,1024]{1,0:T(8,128)(2,1)S(1)} %get-tuple-element.69.refs_1_, bf16[1024,4096]{1,0:T(8,128)(2,1)S(1)} %bitcast.31, bf16[1024,4096]{1,0:T(8,128)(2,1)S(1)} %bitcast.37, ...), custom_call_target="tpu_custom_call" | custom-call | flops 1650000000 | bytes 65536 | tf_op jit(solution)/shard_map/backward_own/pallas_call | solution.py:274
  51.2 2.7 %collective-permute-start.19 = (bf16[48,512]{1,0:T(8,128)(2,1)S(1)}, bf16[48,512]{1,0:T(8,128)(2,1)S(1)}, u32[]{:S(2)}, u32[]{:S(2)}) collective-permute-start(bf16[48,512]{1,0:T(8,128)(2,1)S(1)} %get-tuple-element.73), channel_id=1, source_target_pairs={{0,24},{4,28},{8,16},{12,20},{16,8},{20,12},{24,0},{28,4},{1,25},{... | collective-permute-start | bytes 147464 | tf_op jit(solution)/shard_map/ppermute | solution.py:314
  53.9 1.7 %collective-permute-start.21 = (bf16[48,512]{1,0:T(8,128)(2,1)S(1)}, bf16[48,512]{1,0:T(8,128)(2,1)S(1)}, u32[]{:S(2)}, u32[]{:S(2)}) collective-permute-start(bf16[48,512]{1,0:T(8,128)(2,1)S(1)} %get-tuple-element.75), channel_id=1, source_target_pairs={{0,8},{4,12},{8,0},{12,4},{16,24},{20,28},{24,16},{28,20},{1,9},{5... | collective-permute-start | bytes 147464 | tf_op jit(solution)/shard_map/ppermute | solution.py:314
  55.6 1.3 %combine_acts.1 = bf16[192,2048]{1,0:T(8,128)(2,1)} custom-call(bf16[192,2048]{1,0:T(8,128)(2,1)S(1)} %collective-permute-done.refs_1_.refs_0_, bf16[8,192,192]{2,1,0:T(8,128)(2,1)S(1)} %get-tuple-element.42.refs_4_.refs_1_, bf16[48,512]{1,0:T(8,128)(2,1)S(1)} %get-tuple-element.65.refs_4_.refs_2_, bf16[48,512]{1,0:T(8,128)(2,1)S(1)} %collective-permute-done.15.refs_3_, ...), custom_call_target="tpu_custom_call" | custom-call | flops 1320000000 | bytes 65536 | tf_op jit(solution)/shard_map/combine_acts/pallas_call | solution.py:274
  56.9 0.4 collective-permute-done.19.refs_3_
  57.3 1.5 %collective-permute-done.20.refs_4_ = bf16[48,512]{1,0:T(8,128)(2,1)S(1)} collective-permute-done((bf16[48,512]{1,0:T(8,128)(2,1)S(1)}, bf16[48,512]{1,0:T(8,128)(2,1)S(1)}, u32[]{:S(2)}, u32[]{:S(2)}) %collective-permute-start.20) | collective-permute-done | bytes 49184 | tf_op jit(solution)/shard_map/ppermute | solution.py:314
  58.9 1.1 %combine_gradients.1 = bf16[192,2048]{1,0:T(8,128)(2,1)} custom-call(bf16[192,2048]{1,0:T(8,128)(2,1)S(1)} %collective-permute-done.8.refs_2_.refs_0_, bf16[4,192,192]{2,1,0:T(8,128)(2,1)S(1)} %get-tuple-element.72.refs_1_, bf16[48,512]{1,0:T(8,128)(2,1)S(1)} %get-tuple-element.71.refs_6_.refs_2_, bf16[48,512]{1,0:T(8,128)(2,1)S(1)} %collective-permute-done.19.refs_3_, ...), custom_call_target="tpu_custom_call" | custom-call | flops 1320000000 | bytes 65536 | tf_op jit(solution)/shard_map/combine_gradients/pallas_call | solution.py:274
  (44 shorter events, 2.5 us)
Async XLA Ops:
  0.6 14.6 %collective-permute-start = (bf16[192,2048]{1,0:T(8,128)(2,1)}, bf16[192,2048]{1,0:T(8,128)(2,1)S(1)}, u32[]{:S(2)}, u32[]{:S(2)}) collective-permute-start(bf16[192,2048]{1,0:T(8,128)(2,1)} %bitcast.39), channel_id=1, source_target_pairs={{0,1},{1,2},{2,3},{3,0},{4,5},{5,6},{6,7},{7,4},{8,9},{9,10},{10,1... | collective-permute-start | bytes 2359304 | tf_op jit(solution)/shard_map/ppermute | solution.py:310
  3.4 6.8 %collective-permute-start.1 = (bf16[48,512]{1,0:T(8,128)(2,1)S(1)}, bf16[48,512]{1,0:T(8,128)(2,1)S(1)}, u32[]{:S(2)}, u32[]{:S(2)}) collective-permute-start(bf16[48,512]{1,0:T(8,128)(2,1)S(1)} %get-tuple-element.44), channel_id=1, source_target_pairs={{0,24},{4,28},{8,16},{12,20},{16,8},{20,12},{24,0},{28,4},{1,25},{... | collective-permute-start | bytes 147464 | tf_op jit(solution)/shard_map/ppermute | solution.py:314
  8.1 5.4 %collective-permute-start.2 = (bf16[48,512]{1,0:T(8,128)(2,1)S(1)}, bf16[48,512]{1,0:T(8,128)(2,1)S(1)}, u32[]{:S(2)}, u32[]{:S(2)}) collective-permute-start(bf16[48,512]{1,0:T(8,128)(2,1)S(1)} %get-tuple-element.45), channel_id=1, source_target_pairs={{0,16},{4,20},{8,24},{12,28},{16,0},{20,4},{24,8},{28,12},{1,17},{... | collective-permute-start | bytes 147464 | tf_op jit(solution)/shard_map/ppermute | solution.py:314
  8.1 5.4 %collective-permute-start.3 = (bf16[48,512]{1,0:T(8,128)(2,1)S(1)}, bf16[48,512]{1,0:T(8,128)(2,1)S(1)}, u32[]{:S(2)}, u32[]{:S(2)}) collective-permute-start(bf16[48,512]{1,0:T(8,128)(2,1)S(1)} %get-tuple-element.46), channel_id=1, source_target_pairs={{0,8},{4,12},{8,0},{12,4},{16,24},{20,28},{24,16},{28,20},{1,9},{5... | collective-permute-start | bytes 147464 | tf_op jit(solution)/shard_map/ppermute | solution.py:314
  8.7 12.6 %collective-permute-start.8 = (bf16[192,2048]{1,0:T(8,128)(2,1)}, bf16[192,2048]{1,0:T(8,128)(2,1)S(1)}, u32[]{:S(2)}, u32[]{:S(2)}) collective-permute-start(bf16[192,2048]{1,0:T(8,128)(2,1)} %bitcast.40), channel_id=1, source_target_pairs={{0,3},{1,0},{2,1},{3,2},{4,7},{5,4},{6,5},{7,6},{8,11},{9,8},{10,9... | collective-permute-start | bytes 2359304 | tf_op jit(solution)/shard_map/ppermute | solution.py:310
  9.9 18.1 %slice-start.4 = ((s8[8388608]{0:T(1024)(128)(4,1)}), s8[4194304]{0:T(1024)(128)(4,1)S(1)}, s32[]{:S(2)}) async-start(s8[8388608]{0:T(1024)(128)(4,1)} %bitcast.32), calls=%async_computation.4 | async-start | bytes 8388608
  13.4 14.5 %slice-start.2 = ((s8[8388608]{0:T(1024)(128)(4,1)}), s8[4194304]{0:T(1024)(128)(4,1)S(1)}, s32[]{:S(2)}) async-start(s8[8388608]{0:T(1024)(128)(4,1)} %bitcast.26), calls=%async_computation.2 | async-start | bytes 8388608
  13.7 20.4 %collective-permute-start.4 = (bf16[48,2048]{1,0:T(8,128)(2,1)S(1)}, bf16[48,2048]{1,0:T(8,128)(2,1)S(1)}, u32[]{:S(2)}, u32[]{:S(2)}) collective-permute-start(bf16[48,2048]{1,0:T(8,128)(2,1)S(1)} %unpick_saved.1.refs_2_.refs_0_), channel_id=1, source_target_pairs={{0,4},{4,0},{8,12},{12,8},{16,20},{20,16},{24,28},{28,24},{1,5},{5... | collective-permute-start | bytes 589832 | tf_op jit(solution)/shard_map/ppermute | solution.py:318
  15.3 12.7 %slice-start.3 = ((s8[8388608]{0:T(1024)(128)(4,1)}), s8[4194304]{0:T(1024)(128)(4,1)S(1)}, s32[]{:S(2)}) async-start(s8[8388608]{0:T(1024)(128)(4,1)} %bitcast.26), calls=%async_computation.3 | async-start | bytes 8388608
  15.3 12.7 %slice-start.5 = ((s8[8388608]{0:T(1024)(128)(4,1)}), s8[4194304]{0:T(1024)(128)(4,1)S(1)}, s32[]{:S(2)}) async-start(s8[8388608]{0:T(1024)(128)(4,1)} %bitcast.32), calls=%async_computation.5 | async-start | bytes 8388608
  15.6 9.7 %collective-permute-start.5 = (bf16[48,512]{1,0:T(8,128)(2,1)S(1)}, bf16[48,512]{1,0:T(8,128)(2,1)S(1)}, u32[]{:S(2)}, u32[]{:S(2)}) collective-permute-start(bf16[48,512]{1,0:T(8,128)(2,1)S(1)} %get-tuple-element.49), channel_id=1, source_target_pairs={{0,24},{4,28},{8,16},{12,20},{16,8},{20,12},{24,0},{28,4},{1,25},{... | collective-permute-start | bytes 147464 | tf_op jit(solution)/shard_map/ppermute | solution.py:314
  18.5 6.8 %collective-permute-start.6 = (bf16[48,512]{1,0:T(8,128)(2,1)S(1)}, bf16[48,512]{1,0:T(8,128)(2,1)S(1)}, u32[]{:S(2)}, u32[]{:S(2)}) collective-permute-start(bf16[48,512]{1,0:T(8,128)(2,1)S(1)} %get-tuple-element.50), channel_id=1, source_target_pairs={{0,16},{4,20},{8,24},{12,28},{16,0},{20,4},{24,8},{28,12},{1,17},{... | collective-permute-start | bytes 147464 | tf_op jit(solution)/shard_map/ppermute | solution.py:314
  18.5 7.6 %collective-permute-start.7 = (bf16[48,512]{1,0:T(8,128)(2,1)S(1)}, bf16[48,512]{1,0:T(8,128)(2,1)S(1)}, u32[]{:S(2)}, u32[]{:S(2)}) collective-permute-start(bf16[48,512]{1,0:T(8,128)(2,1)S(1)} %get-tuple-element.51), channel_id=1, source_target_pairs={{0,8},{4,12},{8,0},{12,4},{16,24},{20,28},{24,16},{28,20},{1,9},{5... | collective-permute-start | bytes 147464 | tf_op jit(solution)/shard_map/ppermute | solution.py:314
  21.7 9.3 %collective-permute-start.10 = (bf16[48,512]{1,0:T(8,128)(2,1)S(1)}, bf16[48,512]{1,0:T(8,128)(2,1)S(1)}, u32[]{:S(2)}, u32[]{:S(2)}) collective-permute-start(bf16[48,512]{1,0:T(8,128)(2,1)S(1)} %get-tuple-element.57), channel_id=1, source_target_pairs={{0,24},{4,28},{8,16},{12,20},{16,8},{20,12},{24,0},{28,4},{1,25},{... | collective-permute-start | bytes 147464 | tf_op jit(solution)/shard_map/ppermute | solution.py:314
  25.3 5.6 %collective-permute-start.11 = (bf16[48,512]{1,0:T(8,128)(2,1)S(1)}, bf16[48,512]{1,0:T(8,128)(2,1)S(1)}, u32[]{:S(2)}, u32[]{:S(2)}) collective-permute-start(bf16[48,512]{1,0:T(8,128)(2,1)S(1)} %get-tuple-element.58), channel_id=1, source_target_pairs={{0,16},{4,20},{8,24},{12,28},{16,0},{20,4},{24,8},{28,12},{1,17},{... | collective-permute-start | bytes 147464 | tf_op jit(solution)/shard_map/ppermute | solution.py:314
  25.3 5.7 %collective-permute-start.12 = (bf16[48,512]{1,0:T(8,128)(2,1)S(1)}, bf16[48,512]{1,0:T(8,128)(2,1)S(1)}, u32[]{:S(2)}, u32[]{:S(2)}) collective-permute-start(bf16[48,512]{1,0:T(8,128)(2,1)S(1)} %get-tuple-element.59), channel_id=1, source_target_pairs={{0,8},{4,12},{8,0},{12,4},{16,24},{20,28},{24,16},{28,20},{1,9},{5... | collective-permute-start | bytes 147464 | tf_op jit(solution)/shard_map/ppermute | solution.py:314
  26.1 6.5 %slice-start = ((s8[8388608]{0:T(1024)(128)(4,1)}), s8[4194304]{0:T(1024)(128)(4,1)S(1)}, s32[]{:S(2)}) async-start(s8[8388608]{0:T(1024)(128)(4,1)} %bitcast.20), calls=%async_computation | async-start | bytes 8388608
  26.4 7.7 %collective-permute-start.9 = (bf16[48,2048]{1,0:T(8,128)(2,1)S(1)}, bf16[48,2048]{1,0:T(8,128)(2,1)S(1)}, u32[]{:S(2)}, u32[]{:S(2)}) collective-permute-start(bf16[48,2048]{1,0:T(8,128)(2,1)S(1)} %unpick_acts.1.refs_1_), channel_id=1, source_target_pairs={{0,4},{4,0},{8,12},{12,8},{16,20},{20,16},{24,28},{28,24},{1,5},{5... | collective-permute-start | bytes 589832 | tf_op jit(solution)/shard_map/ppermute | solution.py:318
  28.0 4.7 %slice-start.1 = ((s8[8388608]{0:T(1024)(128)(4,1)}), s8[4194304]{0:T(1024)(128)(4,1)S(1)}, s32[]{:S(2)}) async-start(s8[8388608]{0:T(1024)(128)(4,1)} %bitcast.20), calls=%async_computation.1 | async-start | bytes 8388608
  31.3 7.7 %collective-permute-start.13 = (bf16[48,2048]{1,0:T(8,128)(2,1)S(1)}, bf16[48,2048]{1,0:T(8,128)(2,1)S(1)}, u32[]{:S(2)}, u32[]{:S(2)}) collective-permute-start(bf16[48,2048]{1,0:T(8,128)(2,1)S(1)} %unpick_gradients.1.refs_0_), channel_id=1, source_target_pairs={{0,4},{4,0},{8,12},{12,8},{16,20},{20,16},{24,28},{28,24},{1,5},{5... | collective-permute-start | bytes 589832 | tf_op jit(solution)/shard_map/ppermute | solution.py:318
  37.8 6.6 %collective-permute-start.14 = (bf16[48,2048]{1,0:T(8,128)(2,1)S(1)}, bf16[48,2048]{1,0:T(8,128)(2,1)S(1)}, u32[]{:S(2)}, u32[]{:S(2)}) collective-permute-start(bf16[48,2048]{1,0:T(8,128)(2,1)S(1)} %get-tuple-element.64), channel_id=1, source_target_pairs={{0,4},{4,0},{8,12},{12,8},{16,20},{20,16},{24,28},{28,24},{1,5},{5... | collective-permute-start | bytes 589832 | tf_op jit(solution)/shard_map/ppermute | solution.py:318
  42.0 8.9 %collective-permute-start.18 = (bf16[48,2048]{1,0:T(8,128)(2,1)S(1)}, bf16[48,2048]{1,0:T(8,128)(2,1)S(1)}, u32[]{:S(2)}, u32[]{:S(2)}) collective-permute-start(bf16[48,2048]{1,0:T(8,128)(2,1)S(1)} %get-tuple-element.70), channel_id=1, source_target_pairs={{0,4},{4,0},{8,12},{12,8},{16,20},{20,16},{24,28},{28,24},{1,5},{5... | collective-permute-start | bytes 589832 | tf_op jit(solution)/shard_map/ppermute | solution.py:318
  44.8 9.1 %collective-permute-start.15 = (bf16[48,512]{1,0:T(8,128)(2,1)S(1)}, bf16[48,512]{1,0:T(8,128)(2,1)S(1)}, u32[]{:S(2)}, u32[]{:S(2)}) collective-permute-start(bf16[48,512]{1,0:T(8,128)(2,1)S(1)} %get-tuple-element.66), channel_id=1, source_target_pairs={{0,24},{4,28},{8,16},{12,20},{16,8},{20,12},{24,0},{28,4},{1,25},{... | collective-permute-start | bytes 147464 | tf_op jit(solution)/shard_map/ppermute | solution.py:314
  47.5 8.1 %collective-permute-start.16 = (bf16[48,512]{1,0:T(8,128)(2,1)S(1)}, bf16[48,512]{1,0:T(8,128)(2,1)S(1)}, u32[]{:S(2)}, u32[]{:S(2)}) collective-permute-start(bf16[48,512]{1,0:T(8,128)(2,1)S(1)} %get-tuple-element.67), channel_id=1, source_target_pairs={{0,16},{4,20},{8,24},{12,28},{16,0},{20,4},{24,8},{28,12},{1,17},{... | collective-permute-start | bytes 147464 | tf_op jit(solution)/shard_map/ppermute | solution.py:314
  48.1 7.6 %collective-permute-start.17 = (bf16[48,512]{1,0:T(8,128)(2,1)S(1)}, bf16[48,512]{1,0:T(8,128)(2,1)S(1)}, u32[]{:S(2)}, u32[]{:S(2)}) collective-permute-start(bf16[48,512]{1,0:T(8,128)(2,1)S(1)} %get-tuple-element.68), channel_id=1, source_target_pairs={{0,8},{4,12},{8,0},{12,4},{16,24},{20,28},{24,16},{28,20},{1,9},{5... | collective-permute-start | bytes 147464 | tf_op jit(solution)/shard_map/ppermute | solution.py:314
  51.2 6.2 %collective-permute-start.19 = (bf16[48,512]{1,0:T(8,128)(2,1)S(1)}, bf16[48,512]{1,0:T(8,128)(2,1)S(1)}, u32[]{:S(2)}, u32[]{:S(2)}) collective-permute-start(bf16[48,512]{1,0:T(8,128)(2,1)S(1)} %get-tuple-element.73), channel_id=1, source_target_pairs={{0,24},{4,28},{8,16},{12,20},{16,8},{20,12},{24,0},{28,4},{1,25},{... | collective-permute-start | bytes 147464 | tf_op jit(solution)/shard_map/ppermute | solution.py:314
  53.9 5.0 %collective-permute-start.20 = (bf16[48,512]{1,0:T(8,128)(2,1)S(1)}, bf16[48,512]{1,0:T(8,128)(2,1)S(1)}, u32[]{:S(2)}, u32[]{:S(2)}) collective-permute-start(bf16[48,512]{1,0:T(8,128)(2,1)S(1)} %get-tuple-element.74), channel_id=1, source_target_pairs={{0,16},{4,20},{8,24},{12,28},{16,0},{20,4},{24,8},{28,12},{1,17},{... | collective-permute-start | bytes 147464 | tf_op jit(solution)/shard_map/ppermute | solution.py:314
  53.9 5.0 %collective-permute-start.21 = (bf16[48,512]{1,0:T(8,128)(2,1)S(1)}, bf16[48,512]{1,0:T(8,128)(2,1)S(1)}, u32[]{:S(2)}, u32[]{:S(2)}) collective-permute-start(bf16[48,512]{1,0:T(8,128)(2,1)S(1)} %get-tuple-element.75), channel_id=1, source_target_pairs={{0,8},{4,12},{8,0},{12,4},{16,24},{20,28},{24,16},{28,20},{1,9},{5... | collective-permute-start | bytes 147464 | tf_op jit(solution)/shard_map/ppermute | solution.py:314

commit v4 on v3

--- a/solution.py
+++ b/solution.py
@@ -120,8 +120,17 @@
     put_pieces(picked * refs[0][:, 0:1] if scaled else picked, pieces)
 
 
-def end_to_end(pieces):
-    return jnp.concatenate([p[...] for p in (pieces[0], *pieces[:0:-1])], axis=0)
+def end_to_end(sz, pieces):
+    if len(pieces) == E_WIN:
+        return jnp.concatenate([p[...] for p in (pieces[0], *pieces[:0:-1])], axis=0)
+    n = sz.piece
+    low, high, relayed = pieces
+    return jnp.concatenate([low[:n], relayed[:n], high[:n], relayed[n:]], axis=0)
+
+
+def relay_kernel(sz, low, high, out):
+    out[: sz.piece] = low[sz.piece :]
+    out[sz.piece :] = high[sz.piece :]
 
 
 def unpick(sz, cat, rows):
@@ -134,7 +143,7 @@
 
 
 def unpick_kernel(sz, *refs):
-    unpick(sz, end_to_end(refs[:-1]), refs[-1])
+    unpick(sz, end_to_end(sz, refs[:-1]), refs[-1])
 
 
 def fold_kernel(sz, *refs):
@@ -152,9 +161,12 @@
     put_pieces(out, pieces)
 
 
-def combine_kernel(sz, copies, values, w, *refs):
-    pieces, (out, done, sems) = refs[:E_WIN], refs[E_WIN:]
-    cat = end_to_end(pieces)
+def token_kernel(token):
+    token[...] = jnp.zeros_like(token)
+
+
+def combine(sz, copies, values, w, pieces, out, done, sems):
+    cat = end_to_end(sz, pieces)
     stores = []
     for q in range(sz.parts):
         columns = pl.ds(q * sz.cols, sz.cols)
@@ -164,6 +176,14 @@
         done[:, columns] = total.astype(BF16)
         stores.append(pltpu.make_async_copy(done.at[:, columns], out.at[:, columns], sems.at[q]))
         stores[-1].start()
+    return stores
+
+
+def combine_kernel(sz, dy, w_b, x, w_f, *refs):
+    (low, high, relayed), back, refs = refs[:3], refs[3 : E_WIN + 3], refs[E_WIN + 3 :]
+    x_out, dy_out, dy_done, x_done, dy_sems, x_sems = refs
+    stores = combine(sz, 1, dy, w_b, back, dy_out, dy_done, dy_sems)
+    stores += combine(sz, 2, x, w_f, (low, high, relayed), x_out, x_done, x_sems)
     for store in stores:
         store.wait()
 
@@ -189,27 +209,27 @@
         out[cut, :] = product if before is None else before[cut, :] + product
 
 
-def first_own_kernel(sz, b, x, wg, wu, gate_all, up_all, turned):
-    turned[:, : sz.slots] = b[...].T
-    turned[:, sz.slots :] = x[...].T
-    add_product(sz, wg, 0, turned, None, gate_all)
-    add_product(sz, wu, 0, turned, None, up_all)
+def turn(above, below):
+    return jnp.concatenate([above[...], below[...]], axis=0).T
+
+
+def first_own_kernel(sz, b, x, wg, wu, gate, up, turned):
+    turned[...] = turn(b, x)
+    add_product(sz, wg, 0, turned, None, gate)
+    add_product(sz, wu, 0, turned, None, up)
 
 
 def first_kernel(sz, *refs):
     n, m = sz.split - 1, sz.slots
     b_slices, x_slices, (gate_own, up_own, wg, wu, wd), refs = refs[:n], refs[n : 2 * n], refs[2 * n : 2 * n + 5], refs[2 * n + 5 :]
-    gate, up, hidden, *outs = refs[:-3]
-    turned, gate_all, up_all = refs[-3:]
+    gate, up, hidden, *outs = refs[:-1]
+    turned = refs[-1]
     for j, (b, x) in enumerate(zip(b_slices, x_slices)):
-        turned[:, :m] = b[...].T
-        turned[:, m:] = x[...].T
-        add_product(sz, wg, j + 1, turned, gate_own if j == 0 else gate_all, gate_all)
-        add_product(sz, wu, j + 1, turned, up_own if j == 0 else up_all, up_all)
-    g = gate_all[:, m:]
-    hidden[...] = (g * jax.nn.sigmoid(g) * up_all[:, m:]).T.astype(BF16)
-    gate[...] = gate_all[:, :m]
-    up[...] = up_all[:, :m]
+        turned[...] = turn(b, x)
+        add_product(sz, wg, j + 1, turned, gate_own if j == 0 else gate, gate)
+        add_product(sz, wu, j + 1, turned, up_own if j == 0 else up, up)
+    g = gate[...]
+    hidden[...] = (g * jax.nn.sigmoid(g) * up[...]).T[m:].astype(BF16)
     forward_slices(sz, range(1, sz.split), hidden, wd, outs)
 
 
@@ -249,10 +269,10 @@
         turned[...] = s[...].T
         add_product(sz, wd, j + 1, turned, dh_own if j == 0 else dh_all, dh_all)
     dh = dh_all[...]
-    g = gate[...]
+    g = gate[:, : sz.slots]
     sig = jax.nn.sigmoid(g)
     d_up[...] = (dh * (g * sig)).T.astype(BF16)
-    d_gate[...] = (dh * up[...] * sig * (1.0 + g * (1.0 - sig))).T.astype(BF16)
+    d_gate[...] = (dh * up[:, : sz.slots] * sig * (1.0 + g * (1.0 - sig))).T.astype(BF16)
     backward_slices(sz, range(1, sz.split), d_gate, d_up, wg, wu, outs)
 
 
@@ -313,6 +333,12 @@
         pairs = lambda o: [(e, (e // split ^ o) * split + e % split) for e in range(experts)]
         return [pieces[0]] + [lax.ppermute(pieces[o], "expert", pairs(o)) for o in range(E_WIN - 1, 0, -1)]
 
+    def exchange_by_halves(low, high, after):
+        send = lambda x, o: lax.ppermute(x, "expert", [(e, (e // split ^ o) * split + e % split) for e in range(experts)])
+        high = send(high, 2)
+        relay = near(functools.partial(relay_kernel, sz), [(low.shape, BF16)], (low, high), "relay", 0.1, after=after)
+        return low, high, relay[0], lambda x: send(x, 1)
+
     def along_group(x, by):
         pairs = [(e, e // split * split + (e + by) % split) for e in range(experts)]
         return lax.ppermute(x, "expert", pairs)
@@ -381,11 +407,11 @@
     )
     gate, up, hidden, *made = near(
         part(first_kernel, sz),
-        [hidden_f32] * 2 + [hidden_bf16] + [rows] * (split - 1),
+        [(both, F32)] * 2 + [hidden_bf16] + [rows] * (split - 1),
         (*b_rows[1:], *x_rows[1:], gate_own, up_own, wg, wu, wd),
         "first",
         4.0,
-        scratch=[pltpu.VMEM((width, 2 * sz.slots), BF16), pltpu.VMEM(both, F32), pltpu.VMEM(both, F32)],
+        scratch=[pltpu.VMEM((width, 2 * sz.slots), BF16)],
         after=(dh_own,),
     )
     made_in = scatter(made)
@@ -399,25 +425,27 @@
     )
     back_in = scatter(back)
     made_own = near(part(forward_own_kernel, sz), [rows], (hidden, wd), "forward_own", 1.0, after=(d_gate,))
-    made_pieces = near(part(fold_kernel, sz), pieces, (*made_own, *made_in), "fold_forward")
+    half = ((2 * sz.piece, sz.cols), BF16)
+    made_halves = near(part(fold_kernel, sz), [half, half], (*made_own, *made_in), "fold_forward")
     back_own = near(
-        part(backward_own_kernel, sz), [rows], (d_gate, d_up, wg, wu), "backward_own", 1.5, after=made_pieces[:1]
-    )
-    made_pieces = exchange(made_pieces)
-    back_pieces = exchange(near(part(fold_kernel, sz), pieces, (*back_own, *back_in), "fold_backward"))
-
-    combine = lambda copies, args, name, after: near(
-        part(combine_kernel, sz, copies),
-        [block],
-        args,
-        name,
-        1.2,
-        scratch=[block_scratch, pltpu.SemaphoreType.DMA((sz.parts,))],
-        after=after,
+        part(backward_own_kernel, sz), [rows], (d_gate, d_up, wg, wu), "backward_own", 1.5, after=made_halves[:1]
+    )
+    back_pieces = near(part(fold_kernel, sz), pieces, (*back_own, *back_in), "fold_backward")
+    low, high, relay, send_on = exchange_by_halves(*made_halves, back_pieces[:1])
+    last, relay = lax.optimization_barrier((back_pieces[1], relay))
+    back_pieces = exchange([back_pieces[0], last, *back_pieces[2:]])
+    made_pieces = (low, high, send_on(relay))
+    (arrived,) = near(token_kernel, [((8, 128), F32)], (), "arrived", 1.2, after=back_pieces[1:3])
+    section_out, input_grads = near(
+        part(combine_kernel, sz),
+        [block, block],
+        (dy_full, b_turned, x_full, f_turned, *made_pieces, *back_pieces),
+        "combine",
+        2.0,
+        scratch=[block_scratch, block_scratch] + [pltpu.SemaphoreType.DMA((sz.parts,))] * 2,
         far_outs=True,
-    )[0]
-    section_out = combine(2, (x_full, f_turned, *made_pieces), "combine_acts", back_pieces[:1])
-    input_grads = combine(1, (dy_full, b_turned, *back_pieces), "combine_gradients", ())
+        after=(arrived,),
+    )
     return (section_out[None], input_grads[None])
 
 

time: 60.2 us -> 59.5 us (0.988)
  waiting for transfers between devices: 7.15 us -> 9.69 us
  Pallas kernels: 20.4 us -> 18.5 us
  starting transfers between devices: 31.5 us -> 30.3 us
    ppermute x15 -> x12, starting transfers between devices: 23.1 us -> 18.8 us  [exchange(): lax.ppermute(pieces[o], 'expert', pairs(o))]
    ppermute x0 -> x2, starting transfers between devices: none -> 2.88 us  [exchange_by_halves(): lax.ppermute(x, 'expert', [(e, (e // split ^ o) * split + e % split) for...]
    pallas_call x17 -> x18, Pallas kernels: 20.4 us -> 18.5 us  [near(): pl.pallas_call(body, out_shape=[jax.ShapeDtypeStruct(s, d) for s, d in ou...]
    ppermute x15 -> x12, waiting for transfers between devices: 5.3 us -> 6.62 us  [exchange(): lax.ppermute(pieces[o], 'expert', pairs(o))]
    ppermute x0 -> x2, waiting for transfers between devices: none -> 1.01 us  [exchange_by_halves(): lax.ppermute(x, 'expert', [(e, (e // split ^ o) * split + e % split) for...]
  transfers between devices with their start and end apart: 22 -> 21, of which waited for: 6 -> 10; matrix products, arithmetic and copies ran while one was open for 0% -> 0% of each run, Pallas kernels for 32% -> 29%
where the time goes in v4:
time: 59.5 us; the launch traced here: 59.4 us
  starting transfers between devices  30.3 us (51%)
  Pallas kernels  18.5 us (31%)
  waiting for transfers between devices  9.69 us (16%)
  between operations  0.85 us (1%)
    ppermute x12, starting transfers between devices, exchange(): lax.ppermute(pieces[o], 'expert', pairs(o))  18.8 us
    pallas_call x18, Pallas kernels, near(): pl.pallas_call(body, out_shape=[jax.ShapeDtypeStruct(s, d) for s, d in ou...  18.5 us
    ppermute x5, starting transfers between devices, along_group(): return lax.ppermute(x, 'expert', pairs)  6.91 us
    ppermute x12, waiting for transfers between devices, exchange(): lax.ppermute(pieces[o], 'expert', pairs(o))  6.62 us
    ppermute x2, starting transfers between devices, exchange_by_halves(): lax.ppermute(x, 'expert', [(e, (e // split ^ o) * split + e % split) for...  2.88 us
    ppermute x2, starting transfers between devices, by_section(): lax.ppermute(x, 'section', [(i, (i + by) % sections) for i in range(secti...  1.68 us
    ppermute x2, waiting for transfers between devices, by_section(): lax.ppermute(x, 'section', [(i, (i + by) % sections) for i in range(secti...  1.23 us
  transfers between devices with their start and end apart: 21, of which 10 were waited for; matrix products, arithmetic and copies ran while one was open for 0% of the time, Pallas kernels for 29%

profile of v4, /device:TPU:0, one launch (start us, length us, event | category | flops | bytes accessed | tf_op | source)
XLA Modules:
  0.0 59.4 jit_solution(7075542507024006920)
XLA Ops:
  0.6 0.5 collective-permute-start.1
  1.1 2.2 %local.1 = (f32[192,192]{1,0:T(8,128)S(1)}, bf16[192,192]{1,0:T(8,128)(2,1)S(1)}, bf16[192,192]{1,0:T(8,128)(2,1)S(1)}, f32[192,128]{1,0:T(8,128)S(1)}, bf16[48,...) custom-call(s32[8,768]{1,0:T(8,128)} %bitcast.41, ...), custom_call_target="tpu_custom_call" | custom-call | flops 2200000000 | bytes 65536 | tf_op jit(solution)/shard_map/local/pallas_call | solution.py:294
  3.4 4.7 %collective-permute-start.2 = (bf16[48,512]{1,0:T(8,128)(2,1)S(1)}, bf16[48,512]{1,0:T(8,128)(2,1)S(1)}, u32[]{:S(2)}, u32[]{:S(2)}) collective-permute-start(bf16[48,512]{1,0:T(8,128)(2,1)S(1)} %get-tuple-element.48), channel_id=1, source_target_pairs={{0,24},{4,28},{8,16},{12,20},{16,8},{20,12},{24,0},{28,4},{1,25},{... | collective-permute-start | bytes 147464 | tf_op jit(solution)/shard_map/ppermute | solution.py:334
  8.1 0.6 %collective-permute-start.4 = (bf16[48,512]{1,0:T(8,128)(2,1)S(1)}, bf16[48,512]{1,0:T(8,128)(2,1)S(1)}, u32[]{:S(2)}, u32[]{:S(2)}) collective-permute-start(bf16[48,512]{1,0:T(8,128)(2,1)S(1)} %get-tuple-element.50), channel_id=1, source_target_pairs={{0,8},{4,12},{8,0},{12,4},{16,24},{20,28},{24,16},{28,20},{1,9},{5... | collective-permute-start | bytes 147464 | tf_op jit(solution)/shard_map/ppermute | solution.py:334
  8.7 1.2 %collective-permute-start = (bf16[192,2048]{1,0:T(8,128)(2,1)}, bf16[192,2048]{1,0:T(8,128)(2,1)S(1)}, u32[]{:S(2)}, u32[]{:S(2)}) collective-permute-start(bf16[192,2048]{1,0:T(8,128)(2,1)} %bitcast.40), channel_id=1, source_target_pairs={{0,3},{1,0},{2,1},{3,2},{4,7},{5,4},{6,5},{7,6},{8,11},{9,8},{10,9... | collective-permute-start | bytes 2359304 | tf_op jit(solution)/shard_map/ppermute | solution.py:330
  10.2 3.2 %collective-permute-done.3.refs_2_ = bf16[48,512]{1,0:T(8,128)(2,1)S(1)} collective-permute-done((bf16[48,512]{1,0:T(8,128)(2,1)S(1)}, bf16[48,512]{1,0:T(8,128)(2,1)S(1)}, u32[]{:S(2)}, u32[]{:S(2)}) %collective-permute-start.3) | collective-permute-done | bytes 49184 | tf_op jit(solution)/shard_map/ppermute | solution.py:334
  13.7 1.6 %collective-permute-start.5 = (bf16[48,2048]{1,0:T(8,128)(2,1)S(1)}, bf16[48,2048]{1,0:T(8,128)(2,1)S(1)}, u32[]{:S(2)}, u32[]{:S(2)}) collective-permute-start(bf16[48,2048]{1,0:T(8,128)(2,1)S(1)} %unpick_saved.1.refs_2_.refs_0_), channel_id=1, source_target_pairs={{0,4},{4,0},{8,12},{12,8},{16,20},{20,16},{24,28},{28,24},{1,5},{5... | collective-permute-start | bytes 589832 | tf_op jit(solution)/shard_map/ppermute | solution.py:344
  15.3 0.4 pick_acts.1
  15.6 2.9 %collective-permute-start.6 = (bf16[48,512]{1,0:T(8,128)(2,1)S(1)}, bf16[48,512]{1,0:T(8,128)(2,1)S(1)}, u32[]{:S(2)}, u32[]{:S(2)}) collective-permute-start(bf16[48,512]{1,0:T(8,128)(2,1)S(1)} %get-tuple-element.53), channel_id=1, source_target_pairs={{0,24},{4,28},{8,16},{12,20},{16,8},{20,12},{24,0},{28,4},{1,25},{... | collective-permute-start | bytes 147464 | tf_op jit(solution)/shard_map/ppermute | solution.py:334
  18.5 1.6 %collective-permute-start.8 = (bf16[48,512]{1,0:T(8,128)(2,1)S(1)}, bf16[48,512]{1,0:T(8,128)(2,1)S(1)}, u32[]{:S(2)}, u32[]{:S(2)}) collective-permute-start(bf16[48,512]{1,0:T(8,128)(2,1)S(1)} %get-tuple-element.55), channel_id=1, source_target_pairs={{0,8},{4,12},{8,0},{12,4},{16,24},{20,28},{24,16},{28,20},{1,9},{5... | collective-permute-start | bytes 147464 | tf_op jit(solution)/shard_map/ppermute | solution.py:334
  20.1 1.2 %collective-permute-done.refs_2_.refs_0_ = bf16[192,2048]{1,0:T(8,128)(2,1)S(1)} collective-permute-done((bf16[192,2048]{1,0:T(8,128)(2,1)}, bf16[192,2048]{1,0:T(8,128)(2,1)S(1)}, u32[]{:S(2)}, u32[]{:S(2)}) %collective-permute-start) | collective-permute-done | bytes 786464 | tf_op jit(solution)/shard_map/ppermute | solution.py:330
  21.7 3.7 %collective-permute-start.10 = (bf16[48,512]{1,0:T(8,128)(2,1)S(1)}, bf16[48,512]{1,0:T(8,128)(2,1)S(1)}, u32[]{:S(2)}, u32[]{:S(2)}) collective-permute-start(bf16[48,512]{1,0:T(8,128)(2,1)S(1)} %get-tuple-element.60), channel_id=1, source_target_pairs={{0,24},{4,28},{8,16},{12,20},{16,8},{20,12},{24,0},{28,4},{1,25},{... | collective-permute-start | bytes 147464 | tf_op jit(solution)/shard_map/ppermute | solution.py:334
  25.3 0.8 %collective-permute-start.12 = (bf16[48,512]{1,0:T(8,128)(2,1)S(1)}, bf16[48,512]{1,0:T(8,128)(2,1)S(1)}, u32[]{:S(2)}, u32[]{:S(2)}) collective-permute-start(bf16[48,512]{1,0:T(8,128)(2,1)S(1)} %get-tuple-element.62), channel_id=1, source_target_pairs={{0,8},{4,12},{8,0},{12,4},{16,24},{20,28},{24,16},{28,20},{1,9},{5... | collective-permute-start | bytes 147464 | tf_op jit(solution)/shard_map/ppermute | solution.py:334
  26.4 1.6 %collective-permute-start.9 = (bf16[48,2048]{1,0:T(8,128)(2,1)S(1)}, bf16[48,2048]{1,0:T(8,128)(2,1)S(1)}, u32[]{:S(2)}, u32[]{:S(2)}) collective-permute-start(bf16[48,2048]{1,0:T(8,128)(2,1)S(1)} %unpick_acts.1.refs_1_), channel_id=1, source_target_pairs={{0,4},{4,0},{8,12},{12,8},{16,20},{20,16},{24,28},{28,24},{1,5},{5... | collective-permute-start | bytes 589832 | tf_op jit(solution)/shard_map/ppermute | solution.py:344
  28.0 2.4 %first_own.1 = (f32[1024,96]{1,0:T(8,128)S(1)}, f32[1024,96]{1,0:T(8,128)S(1)}) custom-call(bf16[48,2048]{1,0:T(8,128)(2,1)S(1)} %unpick_saved.1.refs_2_.refs_0_, bf16[48,2048]{1,0:T(8,128)(2,1)S(1)} %unpick_acts.1.refs_1_, bf16[1024,4096]{1,0:T(8,128)(2,1)S(1)} %bitcast.28, bf16[1024,4096]{1,0:T(8,128)(2,1)S(1)} %bitcast.34), custom_call_target="tpu_custom_call" | custom-call | flops 3300000000 | bytes 65536 | tf_op jit(solution)/shard_map/first_own/pallas_call | solution.py:294
  31.1 1.6 %collective-permute-start.13 = (bf16[48,2048]{1,0:T(8,128)(2,1)S(1)}, bf16[48,2048]{1,0:T(8,128)(2,1)S(1)}, u32[]{:S(2)}, u32[]{:S(2)}) collective-permute-start(bf16[48,2048]{1,0:T(8,128)(2,1)S(1)} %unpick_gradients.1.refs_0_), channel_id=1, source_target_pairs={{0,4},{4,0},{8,12},{12,8},{16,20},{20,16},{24,28},{28,24},{1,5},{5... | collective-permute-start | bytes 589832 | tf_op jit(solution)/shard_map/ppermute | solution.py:344
  32.7 1.3 %hidden_gradient_own.1.refs_7_.refs_1_ = f32[1024,48]{1,0:T(8,128)S(1)} custom-call(bf16[48,2048]{1,0:T(8,128)(2,1)S(1)} %unpick_gradients.1.refs_0_, bf16[1024,4096]{1,0:T(8,128)(2,1)S(1)} %bitcast.22), custom_call_target="tpu_custom_call" | custom-call | flops 1100000000 | bytes 65536 | tf_op jit(solution)/shard_map/hidden_gradient_own/pallas_call | solution.py:294
  34.0 3.3 %first.1 = (f32[1024,96]{1,0:T(8,128)S(1)}, f32[1024,96]{1,0:T(8,128)S(1)}, bf16[48,1024]{1,0:T(8,128)(2,1)S(1)}, bf16[48,2048]{1,0:T(8,128)(2,1)S(1)}) custom-call(bf16[48,2048]{1,0:T(8,128)(2,1)S(1)} %collective-permute-done.5.refs_0_, bf16[48,2048]{1,0:T(8,128)(2,1)S(1)} %collective-permute-done.9.refs_1_, ...), custom_call_target="tpu_custom_call" | custom-call | flops 4400000000 | bytes 65536 | tf_op jit(solution)/shard_map/first/pallas_call | solution.py:294
  37.3 1.1 %collective-permute-start.14 = (bf16[48,2048]{1,0:T(8,128)(2,1)S(1)}, bf16[48,2048]{1,0:T(8,128)(2,1)S(1)}, u32[]{:S(2)}, u32[]{:S(2)}) collective-permute-start(bf16[48,2048]{1,0:T(8,128)(2,1)S(1)} %get-tuple-element.67), channel_id=1, source_target_pairs={{0,4},{4,0},{8,12},{12,8},{16,20},{20,16},{24,28},{28,24},{1,5},{5... | collective-permute-start | bytes 589832 | tf_op jit(solution)/shard_map/ppermute | solution.py:344
  38.4 3.0 %backward.1 = (bf16[48,1024]{1,0:T(8,128)(2,1)S(1)}, bf16[48,1024]{1,0:T(8,128)(2,1)S(1)}, bf16[48,2048]{1,0:T(8,128)(2,1)S(1)}) custom-call(bf16[48,2048]{1,0:T(8,128)(2,1)S(1)} %collective-permute-done.13.refs_0_, f32[1024,48]{1,0:T(8,128)S(1)} %hidden_gradient_own.1.refs_7_.refs_1_, f32[1024,96]{1,0:T(8,128)S(1)} %get-tuple-element.64.refs_2_, ...), custom_call_target="tpu_custom_call" | custom-call | flops 3300000000 | bytes 65536 | tf_op jit(solution)/shard_map/backward/pallas_call | solution.py:294
  41.4 1.0 %collective-permute-start.16 = (bf16[48,2048]{1,0:T(8,128)(2,1)S(1)}, bf16[48,2048]{1,0:T(8,128)(2,1)S(1)}, u32[]{:S(2)}, u32[]{:S(2)}) collective-permute-start(bf16[48,2048]{1,0:T(8,128)(2,1)S(1)} %get-tuple-element.71), channel_id=1, source_target_pairs={{0,4},{4,0},{8,12},{12,8},{16,20},{20,16},{24,28},{28,24},{1,5},{5... | collective-permute-start | bytes 589832 | tf_op jit(solution)/shard_map/ppermute | solution.py:344
  42.4 0.8 %forward_own.1.refs_0_ = bf16[48,2048]{1,0:T(8,128)(2,1)S(1)} custom-call(bf16[48,1024]{1,0:T(8,128)(2,1)S(1)} %get-tuple-element.63.refs_0_, bf16[1024,4096]{1,0:T(8,128)(2,1)S(1)} %bitcast.25, bf16[48,1024]{1,0:T(8,128)(2,1)S(1)} %get-tuple-element.66.refs_2_.refs_0_), custom_call_target="tpu_custom_call" | custom-call | flops 1100000000 | bytes 65536 | tf_op jit(solution)/shard_map/forward_own/pallas_call | solution.py:294
  43.3 0.6 %collective-permute-done.14.refs_1_ = bf16[48,2048]{1,0:T(8,128)(2,1)S(1)} collective-permute-done((bf16[48,2048]{1,0:T(8,128)(2,1)S(1)}, bf16[48,2048]{1,0:T(8,128)(2,1)S(1)}, u32[]{:S(2)}, u32[]{:S(2)}) %collective-permute-start.14) | collective-permute-done | bytes 196640 | tf_op jit(solution)/shard_map/ppermute | solution.py:344
  44.2 1.8 %collective-permute-start.15 = (bf16[96,512]{1,0:T(8,128)(2,1)S(1)}, bf16[96,512]{1,0:T(8,128)(2,1)S(1)}, u32[]{:S(2)}, u32[]{:S(2)}) collective-permute-start(bf16[96,512]{1,0:T(8,128)(2,1)S(1)} %get-tuple-element.69), channel_id=1, source_target_pairs={{0,16},{4,20},{8,24},{12,28},{16,0},{20,4},{24,8},{28,12},{1,17},{... | collective-permute-start | bytes 294920 | tf_op jit(solution)/shard_map/ppermute | solution.py:337
  46.0 1.6 %backward_own.1.refs_0_ = bf16[48,2048]{1,0:T(8,128)(2,1)S(1)} custom-call(bf16[48,1024]{1,0:T(8,128)(2,1)S(1)} %get-tuple-element.66.refs_2_.refs_0_, bf16[48,1024]{1,0:T(8,128)(2,1)S(1)} %get-tuple-element.70.refs_1_, bf16[1024,4096]{1,0:T(8,128)(2,1)S(1)} %bitcast.31, bf16[1024,4096]{1,0:T(8,128)(2,1)S(1)} %bitcast.37, ...), custom_call_target="tpu_custom_call" | custom-call | flops 1650000000 | bytes 65536 | tf_op jit(solution)/shard_map/backward_own/pallas_call | solution.py:294
  48.2 3.6 %collective-permute-start.18 = (bf16[48,512]{1,0:T(8,128)(2,1)S(1)}, bf16[48,512]{1,0:T(8,128)(2,1)S(1)}, u32[]{:S(2)}, u32[]{:S(2)}) collective-permute-start(bf16[48,512]{1,0:T(8,128)(2,1)S(1)} %get-tuple-element.75), channel_id=1, source_target_pairs={{0,24},{4,28},{8,16},{12,20},{16,8},{20,12},{24,0},{28,4},{1,25},{... | collective-permute-start | bytes 147464 | tf_op jit(solution)/shard_map/ppermute | solution.py:334
  51.8 1.0 %collective-permute-start.20 = (bf16[48,512]{1,0:T(8,128)(2,1)S(1)}, bf16[48,512]{1,0:T(8,128)(2,1)S(1)}, u32[]{:S(2)}, u32[]{:S(2)}) collective-permute-start(bf16[48,512]{1,0:T(8,128)(2,1)S(1)} %get-tuple-element.77), channel_id=1, source_target_pairs={{0,8},{4,12},{8,0},{12,4},{16,24},{20,28},{24,16},{28,20},{1,9},{5... | collective-permute-start | bytes 147464 | tf_op jit(solution)/shard_map/ppermute | solution.py:334
  52.8 1.1 %collective-permute-start.17 = (bf16[96,512]{1,0:T(8,128)(2,1)S(1)}, bf16[96,512]{1,0:T(8,128)(2,1)S(1)}, u32[]{:S(2)}, u32[]{:S(2)}) collective-permute-start(bf16[96,512]{1,0:T(8,128)(2,1)S(1)} %relay.1), channel_id=1, source_target_pairs={{0,8},{4,12},{8,0},{12,4},{16,24},{20,28},{24,16},{28,20},{1,9},{5... | collective-permute-start | bytes 294920 | tf_op jit(solution)/shard_map/ppermute | solution.py:337
  53.9 0.4 collective-permute-done.18.refs_0_.refs_8_
  54.3 2.5 %collective-permute-done.19.refs_1_.refs_9_ = bf16[48,512]{1,0:T(8,128)(2,1)S(1)} collective-permute-done((bf16[48,512]{1,0:T(8,128)(2,1)S(1)}, bf16[48,512]{1,0:T(8,128)(2,1)S(1)}, u32[]{:S(2)}, u32[]{:S(2)}) %collective-permute-start.19) | collective-permute-done | bytes 49184 | tf_op jit(solution)/shard_map/ppermute | solution.py:334
  56.8 1.0 %collective-permute-done.17.refs_6_ = bf16[96,512]{1,0:T(8,128)(2,1)S(1)} collective-permute-done((bf16[96,512]{1,0:T(8,128)(2,1)S(1)}, bf16[96,512]{1,0:T(8,128)(2,1)S(1)}, u32[]{:S(2)}, u32[]{:S(2)}) %collective-permute-start.17) | collective-permute-done | bytes 98336 | tf_op jit(solution)/shard_map/ppermute | solution.py:337
  57.8 1.5 %combine.1 = (bf16[192,2048]{1,0:T(8,128)(2,1)}, bf16[192,2048]{1,0:T(8,128)(2,1)}) custom-call(bf16[192,2048]{1,0:T(8,128)(2,1)S(1)} %collective-permute-done.refs_2_.refs_0_, bf16[4,192,192]{2,1,0:T(8,128)(2,1)S(1)} %get-tuple-element.45.refs_1_, bf16[192,2048]{1,0:T(8,128)(2,1)S(1)} %collective-permute-done.1.refs_1_.refs_2_, ...), custom_call_target="tpu_custom_call" | custom-call | flops 2200000000 | bytes 65536 | tf_op jit(solution)/shard_map/combine/pallas_call | solution.py:294
  (43 shorter events, 2.7 us)
Async XLA Ops:
  0.6 14.6 %collective-permute-start.1 = (bf16[192,2048]{1,0:T(8,128)(2,1)}, bf16[192,2048]{1,0:T(8,128)(2,1)S(1)}, u32[]{:S(2)}, u32[]{:S(2)}) collective-permute-start(bf16[192,2048]{1,0:T(8,128)(2,1)} %bitcast.39), channel_id=1, source_target_pairs={{0,1},{1,2},{2,3},{3,0},{4,5},{5,6},{6,7},{7,4},{8,9},{9,10},{10,1... | collective-permute-start | bytes 2359304 | tf_op jit(solution)/shard_map/ppermute | solution.py:330
  3.4 6.8 %collective-permute-start.2 = (bf16[48,512]{1,0:T(8,128)(2,1)S(1)}, bf16[48,512]{1,0:T(8,128)(2,1)S(1)}, u32[]{:S(2)}, u32[]{:S(2)}) collective-permute-start(bf16[48,512]{1,0:T(8,128)(2,1)S(1)} %get-tuple-element.48), channel_id=1, source_target_pairs={{0,24},{4,28},{8,16},{12,20},{16,8},{20,12},{24,0},{28,4},{1,25},{... | collective-permute-start | bytes 147464 | tf_op jit(solution)/shard_map/ppermute | solution.py:334
  8.1 5.4 %collective-permute-start.3 = (bf16[48,512]{1,0:T(8,128)(2,1)S(1)}, bf16[48,512]{1,0:T(8,128)(2,1)S(1)}, u32[]{:S(2)}, u32[]{:S(2)}) collective-permute-start(bf16[48,512]{1,0:T(8,128)(2,1)S(1)} %get-tuple-element.49), channel_id=1, source_target_pairs={{0,16},{4,20},{8,24},{12,28},{16,0},{20,4},{24,8},{28,12},{1,17},{... | collective-permute-start | bytes 147464 | tf_op jit(solution)/shard_map/ppermute | solution.py:334
  8.1 5.4 %collective-permute-start.4 = (bf16[48,512]{1,0:T(8,128)(2,1)S(1)}, bf16[48,512]{1,0:T(8,128)(2,1)S(1)}, u32[]{:S(2)}, u32[]{:S(2)}) collective-permute-start(bf16[48,512]{1,0:T(8,128)(2,1)S(1)} %get-tuple-element.50), channel_id=1, source_target_pairs={{0,8},{4,12},{8,0},{12,4},{16,24},{20,28},{24,16},{28,20},{1,9},{5... | collective-permute-start | bytes 147464 | tf_op jit(solution)/shard_map/ppermute | solution.py:334
  8.7 12.6 %collective-permute-start = (bf16[192,2048]{1,0:T(8,128)(2,1)}, bf16[192,2048]{1,0:T(8,128)(2,1)S(1)}, u32[]{:S(2)}, u32[]{:S(2)}) collective-permute-start(bf16[192,2048]{1,0:T(8,128)(2,1)} %bitcast.40), channel_id=1, source_target_pairs={{0,3},{1,0},{2,1},{3,2},{4,7},{5,4},{6,5},{7,6},{8,11},{9,8},{10,9... | collective-permute-start | bytes 2359304 | tf_op jit(solution)/shard_map/ppermute | solution.py:330
  9.9 18.1 %slice-start.4 = ((s8[8388608]{0:T(1024)(128)(4,1)}), s8[4194304]{0:T(1024)(128)(4,1)S(1)}, s32[]{:S(2)}) async-start(s8[8388608]{0:T(1024)(128)(4,1)} %bitcast.32), calls=%async_computation.4 | async-start | bytes 8388608
  13.4 14.5 %slice-start.2 = ((s8[8388608]{0:T(1024)(128)(4,1)}), s8[4194304]{0:T(1024)(128)(4,1)S(1)}, s32[]{:S(2)}) async-start(s8[8388608]{0:T(1024)(128)(4,1)} %bitcast.26), calls=%async_computation.2 | async-start | bytes 8388608
  13.7 20.4 %collective-permute-start.5 = (bf16[48,2048]{1,0:T(8,128)(2,1)S(1)}, bf16[48,2048]{1,0:T(8,128)(2,1)S(1)}, u32[]{:S(2)}, u32[]{:S(2)}) collective-permute-start(bf16[48,2048]{1,0:T(8,128)(2,1)S(1)} %unpick_saved.1.refs_2_.refs_0_), channel_id=1, source_target_pairs={{0,4},{4,0},{8,12},{12,8},{16,20},{20,16},{24,28},{28,24},{1,5},{5... | collective-permute-start | bytes 589832 | tf_op jit(solution)/shard_map/ppermute | solution.py:344
  15.3 12.7 %slice-start.3 = ((s8[8388608]{0:T(1024)(128)(4,1)}), s8[4194304]{0:T(1024)(128)(4,1)S(1)}, s32[]{:S(2)}) async-start(s8[8388608]{0:T(1024)(128)(4,1)} %bitcast.26), calls=%async_computation.3 | async-start | bytes 8388608
  15.3 12.7 %slice-start.5 = ((s8[8388608]{0:T(1024)(128)(4,1)}), s8[4194304]{0:T(1024)(128)(4,1)S(1)}, s32[]{:S(2)}) async-start(s8[8388608]{0:T(1024)(128)(4,1)} %bitcast.32), calls=%async_computation.5 | async-start | bytes 8388608
  15.6 9.7 %collective-permute-start.6 = (bf16[48,512]{1,0:T(8,128)(2,1)S(1)}, bf16[48,512]{1,0:T(8,128)(2,1)S(1)}, u32[]{:S(2)}, u32[]{:S(2)}) collective-permute-start(bf16[48,512]{1,0:T(8,128)(2,1)S(1)} %get-tuple-element.53), channel_id=1, source_target_pairs={{0,24},{4,28},{8,16},{12,20},{16,8},{20,12},{24,0},{28,4},{1,25},{... | collective-permute-start | bytes 147464 | tf_op jit(solution)/shard_map/ppermute | solution.py:334
  18.5 6.8 %collective-permute-start.7 = (bf16[48,512]{1,0:T(8,128)(2,1)S(1)}, bf16[48,512]{1,0:T(8,128)(2,1)S(1)}, u32[]{:S(2)}, u32[]{:S(2)}) collective-permute-start(bf16[48,512]{1,0:T(8,128)(2,1)S(1)} %get-tuple-element.54), channel_id=1, source_target_pairs={{0,16},{4,20},{8,24},{12,28},{16,0},{20,4},{24,8},{28,12},{1,17},{... | collective-permute-start | bytes 147464 | tf_op jit(solution)/shard_map/ppermute | solution.py:334
  18.5 7.6 %collective-permute-start.8 = (bf16[48,512]{1,0:T(8,128)(2,1)S(1)}, bf16[48,512]{1,0:T(8,128)(2,1)S(1)}, u32[]{:S(2)}, u32[]{:S(2)}) collective-permute-start(bf16[48,512]{1,0:T(8,128)(2,1)S(1)} %get-tuple-element.55), channel_id=1, source_target_pairs={{0,8},{4,12},{8,0},{12,4},{16,24},{20,28},{24,16},{28,20},{1,9},{5... | collective-permute-start | bytes 147464 | tf_op jit(solution)/shard_map/ppermute | solution.py:334
  21.7 8.8 %collective-permute-start.10 = (bf16[48,512]{1,0:T(8,128)(2,1)S(1)}, bf16[48,512]{1,0:T(8,128)(2,1)S(1)}, u32[]{:S(2)}, u32[]{:S(2)}) collective-permute-start(bf16[48,512]{1,0:T(8,128)(2,1)S(1)} %get-tuple-element.60), channel_id=1, source_target_pairs={{0,24},{4,28},{8,16},{12,20},{16,8},{20,12},{24,0},{28,4},{1,25},{... | collective-permute-start | bytes 147464 | tf_op jit(solution)/shard_map/ppermute | solution.py:334
  25.3 5.4 %collective-permute-start.11 = (bf16[48,512]{1,0:T(8,128)(2,1)S(1)}, bf16[48,512]{1,0:T(8,128)(2,1)S(1)}, u32[]{:S(2)}, u32[]{:S(2)}) collective-permute-start(bf16[48,512]{1,0:T(8,128)(2,1)S(1)} %get-tuple-element.61), channel_id=1, source_target_pairs={{0,16},{4,20},{8,24},{12,28},{16,0},{20,4},{24,8},{28,12},{1,17},{... | collective-permute-start | bytes 147464 | tf_op jit(solution)/shard_map/ppermute | solution.py:334
  25.3 5.5 %collective-permute-start.12 = (bf16[48,512]{1,0:T(8,128)(2,1)S(1)}, bf16[48,512]{1,0:T(8,128)(2,1)S(1)}, u32[]{:S(2)}, u32[]{:S(2)}) collective-permute-start(bf16[48,512]{1,0:T(8,128)(2,1)S(1)} %get-tuple-element.62), channel_id=1, source_target_pairs={{0,8},{4,12},{8,0},{12,4},{16,24},{20,28},{24,16},{28,20},{1,9},{5... | collective-permute-start | bytes 147464 | tf_op jit(solution)/shard_map/ppermute | solution.py:334
  26.1 6.5 %slice-start = ((s8[8388608]{0:T(1024)(128)(4,1)}), s8[4194304]{0:T(1024)(128)(4,1)S(1)}, s32[]{:S(2)}) async-start(s8[8388608]{0:T(1024)(128)(4,1)} %bitcast.20), calls=%async_computation | async-start | bytes 8388608
  26.4 7.7 %collective-permute-start.9 = (bf16[48,2048]{1,0:T(8,128)(2,1)S(1)}, bf16[48,2048]{1,0:T(8,128)(2,1)S(1)}, u32[]{:S(2)}, u32[]{:S(2)}) collective-permute-start(bf16[48,2048]{1,0:T(8,128)(2,1)S(1)} %unpick_acts.1.refs_1_), channel_id=1, source_target_pairs={{0,4},{4,0},{8,12},{12,8},{16,20},{20,16},{24,28},{28,24},{1,5},{5... | collective-permute-start | bytes 589832 | tf_op jit(solution)/shard_map/ppermute | solution.py:344
  28.0 4.7 %slice-start.1 = ((s8[8388608]{0:T(1024)(128)(4,1)}), s8[4194304]{0:T(1024)(128)(4,1)S(1)}, s32[]{:S(2)}) async-start(s8[8388608]{0:T(1024)(128)(4,1)} %bitcast.20), calls=%async_computation.1 | async-start | bytes 8388608
  31.1 7.4 %collective-permute-start.13 = (bf16[48,2048]{1,0:T(8,128)(2,1)S(1)}, bf16[48,2048]{1,0:T(8,128)(2,1)S(1)}, u32[]{:S(2)}, u32[]{:S(2)}) collective-permute-start(bf16[48,2048]{1,0:T(8,128)(2,1)S(1)} %unpick_gradients.1.refs_0_), channel_id=1, source_target_pairs={{0,4},{4,0},{8,12},{12,8},{16,20},{20,16},{24,28},{28,24},{1,5},{5... | collective-permute-start | bytes 589832 | tf_op jit(solution)/shard_map/ppermute | solution.py:344
  37.3 6.6 %collective-permute-start.14 = (bf16[48,2048]{1,0:T(8,128)(2,1)S(1)}, bf16[48,2048]{1,0:T(8,128)(2,1)S(1)}, u32[]{:S(2)}, u32[]{:S(2)}) collective-permute-start(bf16[48,2048]{1,0:T(8,128)(2,1)S(1)} %get-tuple-element.67), channel_id=1, source_target_pairs={{0,4},{4,0},{8,12},{12,8},{16,20},{20,16},{24,28},{28,24},{1,5},{5... | collective-permute-start | bytes 589832 | tf_op jit(solution)/shard_map/ppermute | solution.py:344
  41.4 6.4 %collective-permute-start.16 = (bf16[48,2048]{1,0:T(8,128)(2,1)S(1)}, bf16[48,2048]{1,0:T(8,128)(2,1)S(1)}, u32[]{:S(2)}, u32[]{:S(2)}) collective-permute-start(bf16[48,2048]{1,0:T(8,128)(2,1)S(1)} %get-tuple-element.71), channel_id=1, source_target_pairs={{0,4},{4,0},{8,12},{12,8},{16,20},{20,16},{24,28},{28,24},{1,5},{5... | collective-permute-start | bytes 589832 | tf_op jit(solution)/shard_map/ppermute | solution.py:344
  44.2 7.5 %collective-permute-start.15 = (bf16[96,512]{1,0:T(8,128)(2,1)S(1)}, bf16[96,512]{1,0:T(8,128)(2,1)S(1)}, u32[]{:S(2)}, u32[]{:S(2)}) collective-permute-start(bf16[96,512]{1,0:T(8,128)(2,1)S(1)} %get-tuple-element.69), channel_id=1, source_target_pairs={{0,16},{4,20},{8,24},{12,28},{16,0},{20,4},{24,8},{28,12},{1,17},{... | collective-permute-start | bytes 294920 | tf_op jit(solution)/shard_map/ppermute | solution.py:337
  48.2 6.1 %collective-permute-start.18 = (bf16[48,512]{1,0:T(8,128)(2,1)S(1)}, bf16[48,512]{1,0:T(8,128)(2,1)S(1)}, u32[]{:S(2)}, u32[]{:S(2)}) collective-permute-start(bf16[48,512]{1,0:T(8,128)(2,1)S(1)} %get-tuple-element.75), channel_id=1, source_target_pairs={{0,24},{4,28},{8,16},{12,20},{16,8},{20,12},{24,0},{28,4},{1,25},{... | collective-permute-start | bytes 147464 | tf_op jit(solution)/shard_map/ppermute | solution.py:334
  51.8 5.0 %collective-permute-start.19 = (bf16[48,512]{1,0:T(8,128)(2,1)S(1)}, bf16[48,512]{1,0:T(8,128)(2,1)S(1)}, u32[]{:S(2)}, u32[]{:S(2)}) collective-permute-start(bf16[48,512]{1,0:T(8,128)(2,1)S(1)} %get-tuple-element.76), channel_id=1, source_target_pairs={{0,16},{4,20},{8,24},{12,28},{16,0},{20,4},{24,8},{28,12},{1,17},{... | collective-permute-start | bytes 147464 | tf_op jit(solution)/shard_map/ppermute | solution.py:334
  51.8 5.0 %collective-permute-start.20 = (bf16[48,512]{1,0:T(8,128)(2,1)S(1)}, bf16[48,512]{1,0:T(8,128)(2,1)S(1)}, u32[]{:S(2)}, u32[]{:S(2)}) collective-permute-start(bf16[48,512]{1,0:T(8,128)(2,1)S(1)} %get-tuple-element.77), channel_id=1, source_target_pairs={{0,8},{4,12},{8,0},{12,4},{16,24},{20,28},{24,16},{28,20},{1,9},{5... | collective-permute-start | bytes 147464 | tf_op jit(solution)/shard_map/ppermute | solution.py:334
  52.8 5.0 %collective-permute-start.17 = (bf16[96,512]{1,0:T(8,128)(2,1)S(1)}, bf16[96,512]{1,0:T(8,128)(2,1)S(1)}, u32[]{:S(2)}, u32[]{:S(2)}) collective-permute-start(bf16[96,512]{1,0:T(8,128)(2,1)S(1)} %relay.1), channel_id=1, source_target_pairs={{0,8},{4,12},{8,0},{12,4},{16,24},{20,28},{24,16},{28,20},{1,9},{5... | collective-permute-start | bytes 294920 | tf_op jit(solution)/shard_map/ppermute | solution.py:337

commit v5 on v4

--- a/solution.py
+++ b/solution.py
@@ -128,9 +128,11 @@
     return jnp.concatenate([low[:n], relayed[:n], high[:n], relayed[n:]], axis=0)
 
 
-def relay_kernel(sz, low, high, out):
-    out[: sz.piece] = low[sz.piece :]
-    out[sz.piece :] = high[sz.piece :]
+def relay_kernel(sz, low, high, back, out):
+    n = sz.piece
+    out[:n] = low[n:]
+    out[n : 2 * n] = high[n:]
+    out[2 * n :] = back[...]
 
 
 def unpick(sz, cat, rows):
@@ -166,7 +168,7 @@
 
 
 def combine(sz, copies, values, w, pieces, out, done, sems):
-    cat = end_to_end(sz, pieces)
+    cat = jnp.concatenate(pieces, axis=0)
     stores = []
     for q in range(sz.parts):
         columns = pl.ds(q * sz.cols, sz.cols)
@@ -180,10 +182,13 @@
 
 
 def combine_kernel(sz, dy, w_b, x, w_f, *refs):
-    (low, high, relayed), back, refs = refs[:3], refs[3 : E_WIN + 3], refs[E_WIN + 3 :]
-    x_out, dy_out, dy_done, x_done, dy_sems, x_sems = refs
+    own, far, mid, low, high, relayed = refs[:6]
+    x_out, dy_out, dy_done, x_done, dy_sems, x_sems = refs[6:]
+    n = sz.piece
+    back = (own[...], relayed[2 * n :], mid[...], far[...])
+    made = (low[:n], relayed[:n], high[:n], relayed[n : 2 * n])
     stores = combine(sz, 1, dy, w_b, back, dy_out, dy_done, dy_sems)
-    stores += combine(sz, 2, x, w_f, (low, high, relayed), x_out, x_done, x_sems)
+    stores += combine(sz, 2, x, w_f, made, x_out, x_done, x_sems)
     for store in stores:
         store.wait()
 
@@ -329,15 +334,11 @@
     def by_section(x, by):
         return lax.ppermute(x, "section", [(i, (i + by) % sections) for i in range(sections)])
 
+    def send(x, o):
+        return lax.ppermute(x, "expert", [(e, (e // split ^ o) * split + e % split) for e in range(experts)])
+
     def exchange(pieces):
-        pairs = lambda o: [(e, (e // split ^ o) * split + e % split) for e in range(experts)]
-        return [pieces[0]] + [lax.ppermute(pieces[o], "expert", pairs(o)) for o in range(E_WIN - 1, 0, -1)]
-
-    def exchange_by_halves(low, high, after):
-        send = lambda x, o: lax.ppermute(x, "expert", [(e, (e // split ^ o) * split + e % split) for e in range(experts)])
-        high = send(high, 2)
-        relay = near(functools.partial(relay_kernel, sz), [(low.shape, BF16)], (low, high), "relay", 0.1, after=after)
-        return low, high, relay[0], lambda x: send(x, 1)
+        return [pieces[0]] + [send(pieces[o], o) for o in range(E_WIN - 1, 0, -1)]
 
     def along_group(x, by):
         pairs = [(e, e // split * split + (e + by) % split) for e in range(experts)]
@@ -431,15 +432,15 @@
         part(backward_own_kernel, sz), [rows], (d_gate, d_up, wg, wu), "backward_own", 1.5, after=made_halves[:1]
     )
     back_pieces = near(part(fold_kernel, sz), pieces, (*back_own, *back_in), "fold_backward")
-    low, high, relay, send_on = exchange_by_halves(*made_halves, back_pieces[:1])
-    last, relay = lax.optimization_barrier((back_pieces[1], relay))
-    back_pieces = exchange([back_pieces[0], last, *back_pieces[2:]])
-    made_pieces = (low, high, send_on(relay))
-    (arrived,) = near(token_kernel, [((8, 128), F32)], (), "arrived", 1.2, after=back_pieces[1:3])
+    low, high = made_halves[0], send(made_halves[1], 2)
+    back_far, back_mid = send(back_pieces[3], 3), send(back_pieces[2], 2)
+    (relay,) = near(part(relay_kernel, sz), [((3 * sz.piece, sz.cols), BF16)], (low, high, back_pieces[1]), "relay", 0.1)
+    relayed = send(relay, 1)
+    (arrived,) = near(token_kernel, [((8, 128), F32)], (), "arrived", 3.0, after=(back_far, back_mid))
     section_out, input_grads = near(
         part(combine_kernel, sz),
         [block, block],
-        (dy_full, b_turned, x_full, f_turned, *made_pieces, *back_pieces),
+        (dy_full, b_turned, x_full, f_turned, back_pieces[0], back_far, back_mid, low, high, relayed),
         "combine",
         2.0,
         scratch=[block_scratch, block_scratch] + [pltpu.SemaphoreType.DMA((sz.parts,))] * 2,

time: 59.5 us -> 59.2 us (level)
  starting transfers between devices: 30.3 us -> 29.3 us
  waiting for transfers between devices: 9.69 us -> 10.4 us
    ppermute x14 -> x13, starting transfers between devices: 21.7 us -> 20.7 us  [send(): lax.ppermute(x, 'expert', [(e, (e // split ^ o) * split + e % split) for...]
    ppermute x14 -> x13, waiting for transfers between devices: 7.63 us -> 8.39 us  [send(): lax.ppermute(x, 'expert', [(e, (e // split ^ o) * split + e % split) for...]
  transfers between devices with their start and end apart: 21 -> 20, of which waited for: 10 -> 10; matrix products, arithmetic and copies ran while one was open for 0% -> 0% of each run, Pallas kernels for 29% -> 29%
where the time goes in v5:
time: 59.2 us; the launch traced here: 59.1 us
  starting transfers between devices  29.3 us (49%)
  Pallas kernels  18.5 us (31%)
  waiting for transfers between devices  10.4 us (18%)
  between operations  0.85 us (1%)
    ppermute x13, starting transfers between devices, send(): lax.ppermute(x, 'expert', [(e, (e // split ^ o) * split + e % split) for...  20.7 us
    pallas_call x18, Pallas kernels, near(): pl.pallas_call(body, out_shape=[jax.ShapeDtypeStruct(s, d) for s, d in ou...  18.5 us
    ppermute x13, waiting for transfers between devices, send(): lax.ppermute(x, 'expert', [(e, (e // split ^ o) * split + e % split) for...  8.39 us
    ppermute x5, starting transfers between devices, along_group(): return lax.ppermute(x, 'expert', pairs)  6.91 us
    ppermute x2, starting transfers between devices, by_section(): lax.ppermute(x, 'section', [(i, (i + by) % sections) for i in range(secti...  1.68 us
    ppermute x2, waiting for transfers between devices, by_section(): lax.ppermute(x, 'section', [(i, (i + by) % sections) for i in range(secti...  1.23 us
  transfers between devices with their start and end apart: 20, of which 10 were waited for; matrix products, arithmetic and copies ran while one was open for 0% of the time, Pallas kernels for 29%

profile of v5, /device:TPU:0, one launch (start us, length us, event | category | flops | bytes accessed | tf_op | source)
XLA Modules:
  0.0 59.1 jit_solution(12567733030162695800)
XLA Ops:
  0.6 0.5 collective-permute-start.1
  1.1 2.2 %local.1 = (f32[192,192]{1,0:T(8,128)S(1)}, bf16[192,192]{1,0:T(8,128)(2,1)S(1)}, bf16[192,192]{1,0:T(8,128)(2,1)S(1)}, f32[192,128]{1,0:T(8,128)S(1)}, bf16[48,...) custom-call(s32[8,768]{1,0:T(8,128)} %bitcast.41, ...), custom_call_target="tpu_custom_call" | custom-call | flops 2200000000 | bytes 65536 | tf_op jit(solution)/shard_map/local/pallas_call | solution.py:299
  3.4 4.7 %collective-permute-start.2 = (bf16[48,512]{1,0:T(8,128)(2,1)S(1)}, bf16[48,512]{1,0:T(8,128)(2,1)S(1)}, u32[]{:S(2)}, u32[]{:S(2)}) collective-permute-start(bf16[48,512]{1,0:T(8,128)(2,1)S(1)} %get-tuple-element.48), channel_id=1, source_target_pairs={{0,24},{4,28},{8,16},{12,20},{16,8},{20,12},{24,0},{28,4},{1,25},{... | collective-permute-start | bytes 147464 | tf_op jit(solution)/shard_map/ppermute | solution.py:338
  8.1 0.6 %collective-permute-start.4 = (bf16[48,512]{1,0:T(8,128)(2,1)S(1)}, bf16[48,512]{1,0:T(8,128)(2,1)S(1)}, u32[]{:S(2)}, u32[]{:S(2)}) collective-permute-start(bf16[48,512]{1,0:T(8,128)(2,1)S(1)} %get-tuple-element.50), channel_id=1, source_target_pairs={{0,8},{4,12},{8,0},{12,4},{16,24},{20,28},{24,16},{28,20},{1,9},{5... | collective-permute-start | bytes 147464 | tf_op jit(solution)/shard_map/ppermute | solution.py:338
  8.7 1.2 %collective-permute-start = (bf16[192,2048]{1,0:T(8,128)(2,1)}, bf16[192,2048]{1,0:T(8,128)(2,1)S(1)}, u32[]{:S(2)}, u32[]{:S(2)}) collective-permute-start(bf16[192,2048]{1,0:T(8,128)(2,1)} %bitcast.40), channel_id=1, source_target_pairs={{0,3},{1,0},{2,1},{3,2},{4,7},{5,4},{6,5},{7,6},{8,11},{9,8},{10,9... | collective-permute-start | bytes 2359304 | tf_op jit(solution)/shard_map/ppermute | solution.py:335
  10.2 3.2 %collective-permute-done.3.refs_2_ = bf16[48,512]{1,0:T(8,128)(2,1)S(1)} collective-permute-done((bf16[48,512]{1,0:T(8,128)(2,1)S(1)}, bf16[48,512]{1,0:T(8,128)(2,1)S(1)}, u32[]{:S(2)}, u32[]{:S(2)}) %collective-permute-start.3) | collective-permute-done | bytes 49184 | tf_op jit(solution)/shard_map/ppermute | solution.py:338
  13.7 1.6 %collective-permute-start.12 = (bf16[48,2048]{1,0:T(8,128)(2,1)S(1)}, bf16[48,2048]{1,0:T(8,128)(2,1)S(1)}, u32[]{:S(2)}, u32[]{:S(2)}) collective-permute-start(bf16[48,2048]{1,0:T(8,128)(2,1)S(1)} %unpick_saved.1.refs_2_.refs_0_), channel_id=1, source_target_pairs={{0,4},{4,0},{8,12},{12,8},{16,20},{20,16},{24,28},{28,24},{1,5},{5... | collective-permute-start | bytes 589832 | tf_op jit(solution)/shard_map/ppermute | solution.py:345
  15.3 0.4 pick_acts.1
  15.6 2.9 %collective-permute-start.8 = (bf16[48,512]{1,0:T(8,128)(2,1)S(1)}, bf16[48,512]{1,0:T(8,128)(2,1)S(1)}, u32[]{:S(2)}, u32[]{:S(2)}) collective-permute-start(bf16[48,512]{1,0:T(8,128)(2,1)S(1)} %get-tuple-element.56), channel_id=1, source_target_pairs={{0,24},{4,28},{8,16},{12,20},{16,8},{20,12},{24,0},{28,4},{1,25},{... | collective-permute-start | bytes 147464 | tf_op jit(solution)/shard_map/ppermute | solution.py:338
  18.5 1.6 %collective-permute-start.10 = (bf16[48,512]{1,0:T(8,128)(2,1)S(1)}, bf16[48,512]{1,0:T(8,128)(2,1)S(1)}, u32[]{:S(2)}, u32[]{:S(2)}) collective-permute-start(bf16[48,512]{1,0:T(8,128)(2,1)S(1)} %get-tuple-element.58), channel_id=1, source_target_pairs={{0,8},{4,12},{8,0},{12,4},{16,24},{20,28},{24,16},{28,20},{1,9},{5... | collective-permute-start | bytes 147464 | tf_op jit(solution)/shard_map/ppermute | solution.py:338
  20.1 1.2 %collective-permute-done.refs_2_.refs_0_ = bf16[192,2048]{1,0:T(8,128)(2,1)S(1)} collective-permute-done((bf16[192,2048]{1,0:T(8,128)(2,1)}, bf16[192,2048]{1,0:T(8,128)(2,1)S(1)}, u32[]{:S(2)}, u32[]{:S(2)}) %collective-permute-start) | collective-permute-done | bytes 786464 | tf_op jit(solution)/shard_map/ppermute | solution.py:335
  21.3 0.4 pick_gradients.1
  21.7 3.7 %collective-permute-start.5 = (bf16[48,512]{1,0:T(8,128)(2,1)S(1)}, bf16[48,512]{1,0:T(8,128)(2,1)S(1)}, u32[]{:S(2)}, u32[]{:S(2)}) collective-permute-start(bf16[48,512]{1,0:T(8,128)(2,1)S(1)} %get-tuple-element.53), channel_id=1, source_target_pairs={{0,24},{4,28},{8,16},{12,20},{16,8},{20,12},{24,0},{28,4},{1,25},{... | collective-permute-start | bytes 147464 | tf_op jit(solution)/shard_map/ppermute | solution.py:338
  25.3 0.8 %collective-permute-start.7 = (bf16[48,512]{1,0:T(8,128)(2,1)S(1)}, bf16[48,512]{1,0:T(8,128)(2,1)S(1)}, u32[]{:S(2)}, u32[]{:S(2)}) collective-permute-start(bf16[48,512]{1,0:T(8,128)(2,1)S(1)} %get-tuple-element.55), channel_id=1, source_target_pairs={{0,8},{4,12},{8,0},{12,4},{16,24},{20,28},{24,16},{28,20},{1,9},{5... | collective-permute-start | bytes 147464 | tf_op jit(solution)/shard_map/ppermute | solution.py:338
  26.4 1.6 %collective-permute-start.13 = (bf16[48,2048]{1,0:T(8,128)(2,1)S(1)}, bf16[48,2048]{1,0:T(8,128)(2,1)S(1)}, u32[]{:S(2)}, u32[]{:S(2)}) collective-permute-start(bf16[48,2048]{1,0:T(8,128)(2,1)S(1)} %unpick_acts.1.refs_1_), channel_id=1, source_target_pairs={{0,4},{4,0},{8,12},{12,8},{16,20},{20,16},{24,28},{28,24},{1,5},{5... | collective-permute-start | bytes 589832 | tf_op jit(solution)/shard_map/ppermute | solution.py:345
  28.0 2.4 %first_own.1 = (f32[1024,96]{1,0:T(8,128)S(1)}, f32[1024,96]{1,0:T(8,128)S(1)}) custom-call(bf16[48,2048]{1,0:T(8,128)(2,1)S(1)} %unpick_saved.1.refs_2_.refs_0_, bf16[48,2048]{1,0:T(8,128)(2,1)S(1)} %unpick_acts.1.refs_1_, bf16[1024,4096]{1,0:T(8,128)(2,1)S(1)} %bitcast.28, bf16[1024,4096]{1,0:T(8,128)(2,1)S(1)} %bitcast.34), custom_call_target="tpu_custom_call" | custom-call | flops 3300000000 | bytes 65536 | tf_op jit(solution)/shard_map/first_own/pallas_call | solution.py:299
  31.1 1.6 %collective-permute-start.11 = (bf16[48,2048]{1,0:T(8,128)(2,1)S(1)}, bf16[48,2048]{1,0:T(8,128)(2,1)S(1)}, u32[]{:S(2)}, u32[]{:S(2)}) collective-permute-start(bf16[48,2048]{1,0:T(8,128)(2,1)S(1)} %unpick_gradients.1.refs_0_), channel_id=1, source_target_pairs={{0,4},{4,0},{8,12},{12,8},{16,20},{20,16},{24,28},{28,24},{1,5},{5... | collective-permute-start | bytes 589832 | tf_op jit(solution)/shard_map/ppermute | solution.py:345
  32.7 1.3 %hidden_gradient_own.1.refs_7_.refs_1_ = f32[1024,48]{1,0:T(8,128)S(1)} custom-call(bf16[48,2048]{1,0:T(8,128)(2,1)S(1)} %unpick_gradients.1.refs_0_, bf16[1024,4096]{1,0:T(8,128)(2,1)S(1)} %bitcast.22), custom_call_target="tpu_custom_call" | custom-call | flops 1100000000 | bytes 65536 | tf_op jit(solution)/shard_map/hidden_gradient_own/pallas_call | solution.py:299
  34.0 3.3 %first.1 = (f32[1024,96]{1,0:T(8,128)S(1)}, f32[1024,96]{1,0:T(8,128)S(1)}, bf16[48,1024]{1,0:T(8,128)(2,1)S(1)}, bf16[48,2048]{1,0:T(8,128)(2,1)S(1)}) custom-call(bf16[48,2048]{1,0:T(8,128)(2,1)S(1)} %collective-permute-done.12.refs_0_, bf16[48,2048]{1,0:T(8,128)(2,1)S(1)} %collective-permute-done.13.refs_1_, ...), custom_call_target="tpu_custom_call" | custom-call | flops 4400000000 | bytes 65536 | tf_op jit(solution)/shard_map/first/pallas_call | solution.py:299
  37.3 1.1 %collective-permute-start.14 = (bf16[48,2048]{1,0:T(8,128)(2,1)S(1)}, bf16[48,2048]{1,0:T(8,128)(2,1)S(1)}, u32[]{:S(2)}, u32[]{:S(2)}) collective-permute-start(bf16[48,2048]{1,0:T(8,128)(2,1)S(1)} %get-tuple-element.66), channel_id=1, source_target_pairs={{0,4},{4,0},{8,12},{12,8},{16,20},{20,16},{24,28},{28,24},{1,5},{5... | collective-permute-start | bytes 589832 | tf_op jit(solution)/shard_map/ppermute | solution.py:345
  38.4 3.0 %backward.1 = (bf16[48,1024]{1,0:T(8,128)(2,1)S(1)}, bf16[48,1024]{1,0:T(8,128)(2,1)S(1)}, bf16[48,2048]{1,0:T(8,128)(2,1)S(1)}) custom-call(bf16[48,2048]{1,0:T(8,128)(2,1)S(1)} %collective-permute-done.11.refs_0_, f32[1024,48]{1,0:T(8,128)S(1)} %hidden_gradient_own.1.refs_7_.refs_1_, f32[1024,96]{1,0:T(8,128)S(1)} %get-tuple-element.61.refs_2_, ...), custom_call_target="tpu_custom_call" | custom-call | flops 3300000000 | bytes 65536 | tf_op jit(solution)/shard_map/backward/pallas_call | solution.py:299
  41.4 1.0 %collective-permute-start.15 = (bf16[48,2048]{1,0:T(8,128)(2,1)S(1)}, bf16[48,2048]{1,0:T(8,128)(2,1)S(1)}, u32[]{:S(2)}, u32[]{:S(2)}) collective-permute-start(bf16[48,2048]{1,0:T(8,128)(2,1)S(1)} %get-tuple-element.68), channel_id=1, source_target_pairs={{0,4},{4,0},{8,12},{12,8},{16,20},{20,16},{24,28},{28,24},{1,5},{5... | collective-permute-start | bytes 589832 | tf_op jit(solution)/shard_map/ppermute | solution.py:345
  42.4 0.8 %forward_own.1.refs_0_ = bf16[48,2048]{1,0:T(8,128)(2,1)S(1)} custom-call(bf16[48,1024]{1,0:T(8,128)(2,1)S(1)} %get-tuple-element.65.refs_0_, bf16[1024,4096]{1,0:T(8,128)(2,1)S(1)} %bitcast.25, bf16[48,1024]{1,0:T(8,128)(2,1)S(1)} %get-tuple-element.63.refs_2_.refs_0_), custom_call_target="tpu_custom_call" | custom-call | flops 1100000000 | bytes 65536 | tf_op jit(solution)/shard_map/forward_own/pallas_call | solution.py:299
  43.3 0.6 %collective-permute-done.14.refs_1_ = bf16[48,2048]{1,0:T(8,128)(2,1)S(1)} collective-permute-done((bf16[48,2048]{1,0:T(8,128)(2,1)S(1)}, bf16[48,2048]{1,0:T(8,128)(2,1)S(1)}, u32[]{:S(2)}, u32[]{:S(2)}) %collective-permute-start.14) | collective-permute-done | bytes 196640 | tf_op jit(solution)/shard_map/ppermute | solution.py:345
  44.2 1.8 %collective-permute-start.18 = (bf16[96,512]{1,0:T(8,128)(2,1)S(1)}, bf16[96,512]{1,0:T(8,128)(2,1)S(1)}, u32[]{:S(2)}, u32[]{:S(2)}) collective-permute-start(bf16[96,512]{1,0:T(8,128)(2,1)S(1)} %get-tuple-element.72), channel_id=1, source_target_pairs={{0,16},{4,20},{8,24},{12,28},{16,0},{20,4},{24,8},{28,12},{1,17},{... | collective-permute-start | bytes 294920 | tf_op jit(solution)/shard_map/ppermute | solution.py:338
  46.0 1.6 %backward_own.1.refs_0_ = bf16[48,2048]{1,0:T(8,128)(2,1)S(1)} custom-call(bf16[48,1024]{1,0:T(8,128)(2,1)S(1)} %get-tuple-element.63.refs_2_.refs_0_, bf16[48,1024]{1,0:T(8,128)(2,1)S(1)} %get-tuple-element.64.refs_1_, bf16[1024,4096]{1,0:T(8,128)(2,1)S(1)} %bitcast.31, bf16[1024,4096]{1,0:T(8,128)(2,1)S(1)} %bitcast.37, ...), custom_call_target="tpu_custom_call" | custom-call | flops 1650000000 | bytes 65536 | tf_op jit(solution)/shard_map/backward_own/pallas_call | solution.py:299
  48.2 3.6 %collective-permute-start.16 = (bf16[48,512]{1,0:T(8,128)(2,1)S(1)}, bf16[48,512]{1,0:T(8,128)(2,1)S(1)}, u32[]{:S(2)}, u32[]{:S(2)}) collective-permute-start(bf16[48,512]{1,0:T(8,128)(2,1)S(1)} %get-tuple-element.70), channel_id=1, source_target_pairs={{0,24},{4,28},{8,16},{12,20},{16,8},{20,12},{24,0},{28,4},{1,25},{... | collective-permute-start | bytes 147464 | tf_op jit(solution)/shard_map/ppermute | solution.py:338
  51.8 1.0 %collective-permute-start.19 = (bf16[144,512]{1,0:T(8,128)(2,1)S(1)}, bf16[144,512]{1,0:T(8,128)(2,1)S(1)}, u32[]{:S(2)}, u32[]{:S(2)}) collective-permute-start(bf16[144,512]{1,0:T(8,128)(2,1)S(1)} %relay.1), channel_id=1, source_target_pairs={{0,8},{4,12},{8,0},{12,4},{16,24},{20,28},{24,16},{28,20},{1,9},{5... | collective-permute-start | bytes 442376 | tf_op jit(solution)/shard_map/ppermute | solution.py:338
  52.8 1.5 %collective-permute-done.16.refs_0_.refs_5_ = bf16[48,512]{1,0:T(8,128)(2,1)S(1)} collective-permute-done((bf16[48,512]{1,0:T(8,128)(2,1)S(1)}, bf16[48,512]{1,0:T(8,128)(2,1)S(1)}, u32[]{:S(2)}, u32[]{:S(2)}) %collective-permute-start.16) | collective-permute-done | bytes 49184 | tf_op jit(solution)/shard_map/ppermute | solution.py:338
  54.3 2.5 %collective-permute-done.17.refs_1_.refs_6_ = bf16[48,512]{1,0:T(8,128)(2,1)S(1)} collective-permute-done((bf16[48,512]{1,0:T(8,128)(2,1)S(1)}, bf16[48,512]{1,0:T(8,128)(2,1)S(1)}, u32[]{:S(2)}, u32[]{:S(2)}) %collective-permute-start.17) | collective-permute-done | bytes 49184 | tf_op jit(solution)/shard_map/ppermute | solution.py:338
  56.9 0.7 %collective-permute-done.19.refs_9_ = bf16[144,512]{1,0:T(8,128)(2,1)S(1)} collective-permute-done((bf16[144,512]{1,0:T(8,128)(2,1)S(1)}, bf16[144,512]{1,0:T(8,128)(2,1)S(1)}, u32[]{:S(2)}, u32[]{:S(2)}) %collective-permute-start.19) | collective-permute-done | bytes 147488 | tf_op jit(solution)/shard_map/ppermute | solution.py:338
  57.5 1.5 %combine.1 = (bf16[192,2048]{1,0:T(8,128)(2,1)}, bf16[192,2048]{1,0:T(8,128)(2,1)}) custom-call(bf16[192,2048]{1,0:T(8,128)(2,1)S(1)} %collective-permute-done.refs_2_.refs_0_, bf16[4,192,192]{2,1,0:T(8,128)(2,1)S(1)} %get-tuple-element.43.refs_1_, bf16[192,2048]{1,0:T(8,128)(2,1)S(1)} %collective-permute-done.1.refs_1_.refs_2_, ...), custom_call_target="tpu_custom_call" | custom-call | flops 2200000000 | bytes 65536 | tf_op jit(solution)/shard_map/combine/pallas_call | solution.py:299
  (41 shorter events, 2.4 us)
Async XLA Ops:
  0.6 14.6 %collective-permute-start.1 = (bf16[192,2048]{1,0:T(8,128)(2,1)}, bf16[192,2048]{1,0:T(8,128)(2,1)S(1)}, u32[]{:S(2)}, u32[]{:S(2)}) collective-permute-start(bf16[192,2048]{1,0:T(8,128)(2,1)} %bitcast.39), channel_id=1, source_target_pairs={{0,1},{1,2},{2,3},{3,0},{4,5},{5,6},{6,7},{7,4},{8,9},{9,10},{10,1... | collective-permute-start | bytes 2359304 | tf_op jit(solution)/shard_map/ppermute | solution.py:335
  3.4 6.8 %collective-permute-start.2 = (bf16[48,512]{1,0:T(8,128)(2,1)S(1)}, bf16[48,512]{1,0:T(8,128)(2,1)S(1)}, u32[]{:S(2)}, u32[]{:S(2)}) collective-permute-start(bf16[48,512]{1,0:T(8,128)(2,1)S(1)} %get-tuple-element.48), channel_id=1, source_target_pairs={{0,24},{4,28},{8,16},{12,20},{16,8},{20,12},{24,0},{28,4},{1,25},{... | collective-permute-start | bytes 147464 | tf_op jit(solution)/shard_map/ppermute | solution.py:338
  8.1 5.4 %collective-permute-start.3 = (bf16[48,512]{1,0:T(8,128)(2,1)S(1)}, bf16[48,512]{1,0:T(8,128)(2,1)S(1)}, u32[]{:S(2)}, u32[]{:S(2)}) collective-permute-start(bf16[48,512]{1,0:T(8,128)(2,1)S(1)} %get-tuple-element.49), channel_id=1, source_target_pairs={{0,16},{4,20},{8,24},{12,28},{16,0},{20,4},{24,8},{28,12},{1,17},{... | collective-permute-start | bytes 147464 | tf_op jit(solution)/shard_map/ppermute | solution.py:338
  8.1 5.4 %collective-permute-start.4 = (bf16[48,512]{1,0:T(8,128)(2,1)S(1)}, bf16[48,512]{1,0:T(8,128)(2,1)S(1)}, u32[]{:S(2)}, u32[]{:S(2)}) collective-permute-start(bf16[48,512]{1,0:T(8,128)(2,1)S(1)} %get-tuple-element.50), channel_id=1, source_target_pairs={{0,8},{4,12},{8,0},{12,4},{16,24},{20,28},{24,16},{28,20},{1,9},{5... | collective-permute-start | bytes 147464 | tf_op jit(solution)/shard_map/ppermute | solution.py:338
  8.7 12.6 %collective-permute-start = (bf16[192,2048]{1,0:T(8,128)(2,1)}, bf16[192,2048]{1,0:T(8,128)(2,1)S(1)}, u32[]{:S(2)}, u32[]{:S(2)}) collective-permute-start(bf16[192,2048]{1,0:T(8,128)(2,1)} %bitcast.40), channel_id=1, source_target_pairs={{0,3},{1,0},{2,1},{3,2},{4,7},{5,4},{6,5},{7,6},{8,11},{9,8},{10,9... | collective-permute-start | bytes 2359304 | tf_op jit(solution)/shard_map/ppermute | solution.py:335
  9.9 18.1 %slice-start.4 = ((s8[8388608]{0:T(1024)(128)(4,1)}), s8[4194304]{0:T(1024)(128)(4,1)S(1)}, s32[]{:S(2)}) async-start(s8[8388608]{0:T(1024)(128)(4,1)} %bitcast.32), calls=%async_computation.4 | async-start | bytes 8388608
  13.4 14.5 %slice-start.2 = ((s8[8388608]{0:T(1024)(128)(4,1)}), s8[4194304]{0:T(1024)(128)(4,1)S(1)}, s32[]{:S(2)}) async-start(s8[8388608]{0:T(1024)(128)(4,1)} %bitcast.26), calls=%async_computation.2 | async-start | bytes 8388608
  13.7 20.4 %collective-permute-start.12 = (bf16[48,2048]{1,0:T(8,128)(2,1)S(1)}, bf16[48,2048]{1,0:T(8,128)(2,1)S(1)}, u32[]{:S(2)}, u32[]{:S(2)}) collective-permute-start(bf16[48,2048]{1,0:T(8,128)(2,1)S(1)} %unpick_saved.1.refs_2_.refs_0_), channel_id=1, source_target_pairs={{0,4},{4,0},{8,12},{12,8},{16,20},{20,16},{24,28},{28,24},{1,5},{5... | collective-permute-start | bytes 589832 | tf_op jit(solution)/shard_map/ppermute | solution.py:345
  15.3 12.7 %slice-start.3 = ((s8[8388608]{0:T(1024)(128)(4,1)}), s8[4194304]{0:T(1024)(128)(4,1)S(1)}, s32[]{:S(2)}) async-start(s8[8388608]{0:T(1024)(128)(4,1)} %bitcast.26), calls=%async_computation.3 | async-start | bytes 8388608
  15.3 12.7 %slice-start.5 = ((s8[8388608]{0:T(1024)(128)(4,1)}), s8[4194304]{0:T(1024)(128)(4,1)S(1)}, s32[]{:S(2)}) async-start(s8[8388608]{0:T(1024)(128)(4,1)} %bitcast.32), calls=%async_computation.5 | async-start | bytes 8388608
  15.6 9.7 %collective-permute-start.8 = (bf16[48,512]{1,0:T(8,128)(2,1)S(1)}, bf16[48,512]{1,0:T(8,128)(2,1)S(1)}, u32[]{:S(2)}, u32[]{:S(2)}) collective-permute-start(bf16[48,512]{1,0:T(8,128)(2,1)S(1)} %get-tuple-element.56), channel_id=1, source_target_pairs={{0,24},{4,28},{8,16},{12,20},{16,8},{20,12},{24,0},{28,4},{1,25},{... | collective-permute-start | bytes 147464 | tf_op jit(solution)/shard_map/ppermute | solution.py:338
  18.5 6.8 %collective-permute-start.9 = (bf16[48,512]{1,0:T(8,128)(2,1)S(1)}, bf16[48,512]{1,0:T(8,128)(2,1)S(1)}, u32[]{:S(2)}, u32[]{:S(2)}) collective-permute-start(bf16[48,512]{1,0:T(8,128)(2,1)S(1)} %get-tuple-element.57), channel_id=1, source_target_pairs={{0,16},{4,20},{8,24},{12,28},{16,0},{20,4},{24,8},{28,12},{1,17},{... | collective-permute-start | bytes 147464 | tf_op jit(solution)/shard_map/ppermute | solution.py:338
  18.5 7.6 %collective-permute-start.10 = (bf16[48,512]{1,0:T(8,128)(2,1)S(1)}, bf16[48,512]{1,0:T(8,128)(2,1)S(1)}, u32[]{:S(2)}, u32[]{:S(2)}) collective-permute-start(bf16[48,512]{1,0:T(8,128)(2,1)S(1)} %get-tuple-element.58), channel_id=1, source_target_pairs={{0,8},{4,12},{8,0},{12,4},{16,24},{20,28},{24,16},{28,20},{1,9},{5... | collective-permute-start | bytes 147464 | tf_op jit(solution)/shard_map/ppermute | solution.py:338
  21.7 8.8 %collective-permute-start.5 = (bf16[48,512]{1,0:T(8,128)(2,1)S(1)}, bf16[48,512]{1,0:T(8,128)(2,1)S(1)}, u32[]{:S(2)}, u32[]{:S(2)}) collective-permute-start(bf16[48,512]{1,0:T(8,128)(2,1)S(1)} %get-tuple-element.53), channel_id=1, source_target_pairs={{0,24},{4,28},{8,16},{12,20},{16,8},{20,12},{24,0},{28,4},{1,25},{... | collective-permute-start | bytes 147464 | tf_op jit(solution)/shard_map/ppermute | solution.py:338
  25.3 5.4 %collective-permute-start.6 = (bf16[48,512]{1,0:T(8,128)(2,1)S(1)}, bf16[48,512]{1,0:T(8,128)(2,1)S(1)}, u32[]{:S(2)}, u32[]{:S(2)}) collective-permute-start(bf16[48,512]{1,0:T(8,128)(2,1)S(1)} %get-tuple-element.54), channel_id=1, source_target_pairs={{0,16},{4,20},{8,24},{12,28},{16,0},{20,4},{24,8},{28,12},{1,17},{... | collective-permute-start | bytes 147464 | tf_op jit(solution)/shard_map/ppermute | solution.py:338
  25.3 5.5 %collective-permute-start.7 = (bf16[48,512]{1,0:T(8,128)(2,1)S(1)}, bf16[48,512]{1,0:T(8,128)(2,1)S(1)}, u32[]{:S(2)}, u32[]{:S(2)}) collective-permute-start(bf16[48,512]{1,0:T(8,128)(2,1)S(1)} %get-tuple-element.55), channel_id=1, source_target_pairs={{0,8},{4,12},{8,0},{12,4},{16,24},{20,28},{24,16},{28,20},{1,9},{5... | collective-permute-start | bytes 147464 | tf_op jit(solution)/shard_map/ppermute | solution.py:338
  26.1 6.5 %slice-start = ((s8[8388608]{0:T(1024)(128)(4,1)}), s8[4194304]{0:T(1024)(128)(4,1)S(1)}, s32[]{:S(2)}) async-start(s8[8388608]{0:T(1024)(128)(4,1)} %bitcast.20), calls=%async_computation | async-start | bytes 8388608
  26.4 7.7 %collective-permute-start.13 = (bf16[48,2048]{1,0:T(8,128)(2,1)S(1)}, bf16[48,2048]{1,0:T(8,128)(2,1)S(1)}, u32[]{:S(2)}, u32[]{:S(2)}) collective-permute-start(bf16[48,2048]{1,0:T(8,128)(2,1)S(1)} %unpick_acts.1.refs_1_), channel_id=1, source_target_pairs={{0,4},{4,0},{8,12},{12,8},{16,20},{20,16},{24,28},{28,24},{1,5},{5... | collective-permute-start | bytes 589832 | tf_op jit(solution)/shard_map/ppermute | solution.py:345
  28.0 4.7 %slice-start.1 = ((s8[8388608]{0:T(1024)(128)(4,1)}), s8[4194304]{0:T(1024)(128)(4,1)S(1)}, s32[]{:S(2)}) async-start(s8[8388608]{0:T(1024)(128)(4,1)} %bitcast.20), calls=%async_computation.1 | async-start | bytes 8388608
  31.1 7.4 %collective-permute-start.11 = (bf16[48,2048]{1,0:T(8,128)(2,1)S(1)}, bf16[48,2048]{1,0:T(8,128)(2,1)S(1)}, u32[]{:S(2)}, u32[]{:S(2)}) collective-permute-start(bf16[48,2048]{1,0:T(8,128)(2,1)S(1)} %unpick_gradients.1.refs_0_), channel_id=1, source_target_pairs={{0,4},{4,0},{8,12},{12,8},{16,20},{20,16},{24,28},{28,24},{1,5},{5... | collective-permute-start | bytes 589832 | tf_op jit(solution)/shard_map/ppermute | solution.py:345
  37.3 6.6 %collective-permute-start.14 = (bf16[48,2048]{1,0:T(8,128)(2,1)S(1)}, bf16[48,2048]{1,0:T(8,128)(2,1)S(1)}, u32[]{:S(2)}, u32[]{:S(2)}) collective-permute-start(bf16[48,2048]{1,0:T(8,128)(2,1)S(1)} %get-tuple-element.66), channel_id=1, source_target_pairs={{0,4},{4,0},{8,12},{12,8},{16,20},{20,16},{24,28},{28,24},{1,5},{5... | collective-permute-start | bytes 589832 | tf_op jit(solution)/shard_map/ppermute | solution.py:345
  41.4 6.4 %collective-permute-start.15 = (bf16[48,2048]{1,0:T(8,128)(2,1)S(1)}, bf16[48,2048]{1,0:T(8,128)(2,1)S(1)}, u32[]{:S(2)}, u32[]{:S(2)}) collective-permute-start(bf16[48,2048]{1,0:T(8,128)(2,1)S(1)} %get-tuple-element.68), channel_id=1, source_target_pairs={{0,4},{4,0},{8,12},{12,8},{16,20},{20,16},{24,28},{28,24},{1,5},{5... | collective-permute-start | bytes 589832 | tf_op jit(solution)/shard_map/ppermute | solution.py:345
  44.2 7.5 %collective-permute-start.18 = (bf16[96,512]{1,0:T(8,128)(2,1)S(1)}, bf16[96,512]{1,0:T(8,128)(2,1)S(1)}, u32[]{:S(2)}, u32[]{:S(2)}) collective-permute-start(bf16[96,512]{1,0:T(8,128)(2,1)S(1)} %get-tuple-element.72), channel_id=1, source_target_pairs={{0,16},{4,20},{8,24},{12,28},{16,0},{20,4},{24,8},{28,12},{1,17},{... | collective-permute-start | bytes 294920 | tf_op jit(solution)/shard_map/ppermute | solution.py:338
  48.2 6.1 %collective-permute-start.16 = (bf16[48,512]{1,0:T(8,128)(2,1)S(1)}, bf16[48,512]{1,0:T(8,128)(2,1)S(1)}, u32[]{:S(2)}, u32[]{:S(2)}) collective-permute-start(bf16[48,512]{1,0:T(8,128)(2,1)S(1)} %get-tuple-element.70), channel_id=1, source_target_pairs={{0,24},{4,28},{8,16},{12,20},{16,8},{20,12},{24,0},{28,4},{1,25},{... | collective-permute-start | bytes 147464 | tf_op jit(solution)/shard_map/ppermute | solution.py:338
  51.8 5.1 %collective-permute-start.17 = (bf16[48,512]{1,0:T(8,128)(2,1)S(1)}, bf16[48,512]{1,0:T(8,128)(2,1)S(1)}, u32[]{:S(2)}, u32[]{:S(2)}) collective-permute-start(bf16[48,512]{1,0:T(8,128)(2,1)S(1)} %get-tuple-element.71), channel_id=1, source_target_pairs={{0,16},{4,20},{8,24},{12,28},{16,0},{20,4},{24,8},{28,12},{1,17},{... | collective-permute-start | bytes 147464 | tf_op jit(solution)/shard_map/ppermute | solution.py:338
  51.8 5.7 %collective-permute-start.19 = (bf16[144,512]{1,0:T(8,128)(2,1)S(1)}, bf16[144,512]{1,0:T(8,128)(2,1)S(1)}, u32[]{:S(2)}, u32[]{:S(2)}) collective-permute-start(bf16[144,512]{1,0:T(8,128)(2,1)S(1)} %relay.1), channel_id=1, source_target_pairs={{0,8},{4,12},{8,0},{12,4},{16,24},{20,28},{24,16},{28,20},{1,9},{5... | collective-permute-start | bytes 442376 | tf_op jit(solution)/shard_map/ppermute | solution.py:338
